TPU v7x, 32 devices: a whole 2x2x4 slice. The times are simulated.
32 devices in a mesh: grp: 4 (over y, core), fsdp: 8 (over z, x).
Axes of the slice: x: 2, y: 2, z: 4, core: 2. Of those that a mesh axis runs over, the one named last changes fastest.
Arguments:
- tokens: bfloat16 [6144, 8192], P(('grp', 'fsdp')), may hold values from -6 to 6
- targets: bfloat16 [6144, 1024], P(('grp', 'fsdp')), may hold values from -6 to 6
- row_owner_user: int32 [6144, 1], P(('grp', 'fsdp')), may hold values from 0 to 31; in each aligned block of 192 rows (0 to 191, 192 to 383, ...) at most 9 rows name the same one
- device_row_count: int32 [32], P(('grp', 'fsdp')), may hold values from 1 to 192, 4608 in all
- user_row_cap: int32 [32], replicated, may hold values from 48 to 383
- value_weight: bfloat16 [8192, 1024], P('fsdp'), may hold values from -0.0625 to 0.0625
- adapter_down: bfloat16 [8192, 64], replicated, may hold values from -0.0625 to 0.0625
- adapter_up: bfloat16 [64, 1024], replicated, may hold values from -0.75 to 0.75
- clip_norm_bound: float32 [1], replicated, may hold values from 2 to 6
- down_noise: float32 [8192, 64], P(('grp', 'fsdp')), may hold values from -0.12 to 0.12
- up_noise: float32 [64, 1024], P(None, ('grp', 'fsdp')), may hold values from -0.12 to 0.12
Outputs:
- update_a: float32 [8192, 64], P(('grp', 'fsdp'))
- update_b: float32 [64, 1024], P(None, ('grp', 'fsdp'))
Inputs may be any that keep to these rules, and one draw needn't show every extreme that they name: `row_owner_user`: within the rows of one device (aligned blocks of 192 rows) no user is named by more than 9 rows, a bound that some block reaches. `device_row_count`: the counts sum to 4608.
All inputs are finite; a program needn't handle non-finite values. No bound on the sum of `device_row_count` on one device may be relied on, other than what follows from the above.
Results may differ from a plain program's by a relative error of at most 0.00084.
Values may be sent and summed in bfloat16 or wider, within the bound.
No kernel may reach another device: no remote copies, remote signals or barrier semaphores. Data moves between devices by JAX's collectives and lax.ppermute only.
A program may use at most 128 MiB of HBM per device.

v0:
```python
import jax
import jax.numpy as jnp
from jax import lax
from jax.sharding import PartitionSpec as P

STEPS = 2


adapter_scale = 2.0
learn_rate = 0.05
epsilon = 1e-06


def entering(value, axis, join, neutral):
    count, mine = (lax.axis_size(axis), lax.axis_index(axis))
    pieces = lax.all_gather(value, axis)
    running = jnp.full_like(value, 0) + jnp.asarray(neutral, value.dtype)

    def turn(position, running):
        longer = join(running, pieces[position])
        return jnp.where(position < mine, longer, running)

    return lax.fori_loop(0, count - 1, turn, running)


def adapter_step(
    input_rows,
    frozen_output,
    target_value,
    live_mask,
    capped_value,
    adapter_down,
    adapter_up,
    clipped_value_rows,
):
    current_down = adapter_down.astype(jnp.float32)
    current_up = adapter_up.astype(jnp.float32)
    for repeat in range(STEPS):
        a_half = current_down.astype(jnp.bfloat16)
        half_up_matrix = current_up.astype(jnp.bfloat16)
        hidden_input = jnp.dot(input_rows, a_half, preferred_element_type=jnp.float32).astype(
            jnp.bfloat16
        )
        value_output = frozen_output + adapter_scale * jnp.dot(
            hidden_input, half_up_matrix, preferred_element_type=jnp.float32
        )
        residual_error = (
            live_mask[:, None] * (value_output - target_value.astype(jnp.float32)) / capped_value
        ).astype(jnp.bfloat16)
        up_gradient = adapter_scale * lax.dot_general(
            hidden_input,
            residual_error,
            (((0,), (0,)), ((), ())),
            preferred_element_type=jnp.float32,
        )
        backward_pass = jnp.dot(
            residual_error, half_up_matrix.T, preferred_element_type=jnp.float32
        ).astype(jnp.bfloat16)
        down_gradient = adapter_scale * lax.dot_general(
            input_rows, backward_pass, (((0,), (0,)), ((), ())), preferred_element_type=jnp.float32
        )
        current_down = current_down - learn_rate * down_gradient
        current_up = current_up - learn_rate * up_gradient
    down_delta = current_down - adapter_down.astype(jnp.float32)
    up_delta = current_up - adapter_up.astype(jnp.float32)
    total = jnp.sum(down_delta * down_delta) + jnp.sum(up_delta * up_delta)
    factor = jnp.minimum(1.0, clipped_value_rows / jnp.sqrt(total + epsilon))
    return (factor * down_delta, factor * up_delta)


def add_counts(earlier, later):
    return earlier + later


def body(
    tokens,
    targets,
    row_owner_user,
    device_row_count,
    user_row_cap,
    value_weight,
    adapter_down,
    adapter_up,
    clip_norm_bound,
    down_noise,
    up_noise,
):
    devices = lax.axis_size(("grp", "fsdp"))
    myself = lax.axis_index(("grp", "fsdp"))
    per_dev = tokens.shape[0]
    width = tokens.shape[1]
    kv_width = targets.shape[1]
    users = user_row_cap.shape[0]
    most_rows = 3 * per_dev // (2 * devices)
    slot_count = devices * most_rows
    user_of = row_owner_user[:, 0]
    position = jnp.arange(per_dev, dtype=jnp.int32)
    valid = position < device_row_count[0]
    onehot = (user_of[:, None] == jnp.arange(users, dtype=jnp.int32)[None, :]).astype(jnp.float32)
    lower = (position[None, :] < position[:, None]).astype(jnp.float32)
    valid_hot = onehot * valid[:, None].astype(jnp.float32)
    before_all = jnp.dot(lower, onehot, precision=lax.Precision.HIGHEST)
    before_valid = jnp.dot(lower, valid_hot, precision=lax.Precision.HIGHEST)
    row_rank = jnp.sum(before_all * onehot, axis=1).astype(jnp.int32)
    local_earlier = jnp.sum(before_valid * onehot, axis=1)
    counts = jnp.sum(valid_hot, axis=0).astype(jnp.int32)
    prior = entering(counts, ("grp", "fsdp"), add_counts, jnp.zeros_like(counts))
    earlier = local_earlier + jnp.sum(onehot * prior.astype(jnp.float32)[None, :], axis=1)
    cap_row = jnp.sum(onehot * user_row_cap.astype(jnp.float32)[None, :], axis=1)
    kept = valid & (earlier < cap_row)
    slot_index = jnp.where(kept, user_of * most_rows + row_rank, slot_count)
    send_rows = jnp.zeros((slot_count, width), jnp.bfloat16).at[slot_index].set(tokens, mode="drop")
    send_goal = (
        jnp.zeros((slot_count, kv_width), jnp.bfloat16).at[slot_index].set(targets, mode="drop")
    )
    send_live = (
        jnp.zeros((slot_count,), jnp.bfloat16)
        .at[slot_index]
        .set(jnp.ones((per_dev,), jnp.bfloat16), mode="drop")
    )
    groups = lax.axis_size("grp")
    members = lax.axis_size("fsdp")
    got_rows, got_goal, got_live = (
        lax.all_to_all(
            lax.all_to_all(
                send_rows.reshape(groups, members, most_rows, width),
                "grp",
                split_axis=0,
                concat_axis=0,
                tiled=True,
            ),
            "fsdp",
            split_axis=1,
            concat_axis=1,
            tiled=True,
        ),
        lax.all_to_all(
            lax.all_to_all(
                send_goal.reshape(groups, members, most_rows, kv_width),
                "grp",
                split_axis=0,
                concat_axis=0,
                tiled=True,
            ),
            "fsdp",
            split_axis=1,
            concat_axis=1,
            tiled=True,
        ),
        lax.all_to_all(
            lax.all_to_all(
                send_live.reshape(groups, members, most_rows),
                "grp",
                split_axis=0,
                concat_axis=0,
                tiled=True,
            ),
            "fsdp",
            split_axis=1,
            concat_axis=1,
            tiled=True,
        ),
    )
    input_rows = got_rows.reshape(slot_count, width)
    target_value = got_goal.reshape(slot_count, kv_width)
    live_mask = got_live.reshape(slot_count).astype(jnp.float32)
    frozen_output = jnp.dot(
        input_rows,
        lax.all_gather(value_weight, "fsdp", axis=0, tiled=True),
        preferred_element_type=jnp.float32,
    )
    user_row_limit = jnp.sum(
        jnp.where(jnp.arange(users, dtype=jnp.int32) == myself, user_row_cap, 0)
    ).astype(jnp.float32)
    clipped_value_rows = clip_norm_bound[0]
    down_partial, up_partial = adapter_step(
        input_rows,
        frozen_output,
        target_value,
        live_mask,
        user_row_limit,
        adapter_down,
        adapter_up,
        clipped_value_rows,
    )
    summed_a, summed_b = (
        lax.psum_scatter(down_partial, ("grp", "fsdp"), scatter_dimension=0, tiled=True),
        lax.psum_scatter(up_partial, ("grp", "fsdp"), scatter_dimension=1, tiled=True),
    )
    update_a = summed_a + clipped_value_rows * down_noise
    update_b = summed_b + clipped_value_rows * up_noise
    return (update_a, update_b)


def solution(mesh):
    in_specs = (
        P(("grp", "fsdp"), None),
        P(("grp", "fsdp"), None),
        P(("grp", "fsdp"), None),
        P(("grp", "fsdp")),
        P(),
        P("fsdp", None),
        P(),
        P(),
        P(),
        P(("grp", "fsdp"), None),
        P(None, ("grp", "fsdp")),
    )
    out_specs = (P(("grp", "fsdp"), None), P(None, ("grp", "fsdp")))
    return jax.shard_map(body, mesh=mesh, in_specs=in_specs, out_specs=out_specs, check_vma=False)
```

profile of v0, /device:TPU:0, one launch (start us, length us, event | category | flops | bytes accessed | tf_op | source)
XLA Modules:
  0.0 682.0 jit_solution(6050960870699507138)
XLA Ops:
  7.2 0.7 all-gather.3.cloned.1.call-update
  8.8 46.7 %all-reduce = s32[1024]{0:T(1024)S(1)} all-reduce(s32[1024]{0:T(1024)S(1)} %convert_dynamic-update-slice_fusion), channel_id=2, replica_groups=mesh['grp'=4,'fsdp'=8] {'grp','fsdp'}, use_global_device_ids=true, to_apply=%add | all-reduce | flops 1024 | bytes 8192
  55.6 1.2 while.14
  57.4 0.7 fusion.31
  58.1 1.8 scatter_custom_fusion.1
  60.0 7.2 %all_to_all.30 = bf16[4,8,9]{2,1,0:T(8,128)(2,1)S(1)} all-to-all(bf16[4,8,9]{2,1,0:T(8,128)(2,1)S(1)} %reshape.81), channel_id=1, replica_groups=mesh['grp'=4,'fsdp'=8] {'grp'}, dimensions={0} | all-to-all | bytes 1152 | tf_op jit(solution)/shard_map/all_to_all | solution.py:151
  67.2 0.6 copy.38
  67.8 3.7 all-to-all-start.3
  71.5 2.0 scatter_custom_fusion.2
  73.8 1.2 copy.40
  75.0 3.2 all-to-all-done.3
  78.2 3.5 all-to-all-start.4
  81.7 8.9 %scatter_custom_fusion = bf16[288,8192]{1,0:T(8,128)(2,1)} fusion(s32[192]{0:T(256)S(1)} %bitcast.42, bf16[192,8192]{1,0:T(8,128)(2,1)} %param.13, bf16[]{:T(256)} %constant.56.clone.1), kind=kCustom, calls=%fused_computation.10 | custom fusion | bytes 4719104 | tf_op jit(solution)/shard_map/scatter | solution.py:112
  90.5 6.9 %reshape.79 = bf16[4,8,9,8192]{3,2,1,0:T(8,128)(2,1)} reshape(bf16[288,8192]{1,0:T(8,128)(2,1)} %scatter_custom_fusion) | data formatting | bytes 9437184 | tf_op jit(solution)/shard_map/reshape | solution.py:126
  97.5 8.7 %copy.35 = bf16[4,8,9,8192]{3,1,2,0:T(8,128)(2,1)} copy(bf16[4,8,9,8192]{3,2,1,0:T(8,128)(2,1)} %reshape.79) | data formatting | bytes 9437184 | tf_op jit(solution)/shard_map/reshape | solution.py:126
  106.1 5.0 all-to-all-start
  111.1 1.3 copy.41
  112.4 52.6 %all-to-all-done = bf16[4,8,9,8192]{3,1,2,0:T(8,128)(2,1)} async-done(((bf16[4,8,9,8192]{3,1,2,0:T(8,128)(2,1)}), bf16[4,8,9,8192]{3,1,2,0:T(8,128)(2,1)}, u32[]{:S(2)}, u32[]{:S(2)}) %all-to-all-start) | async-done | bytes 4718624 | tf_op jit(solution)/shard_map/all_to_all | solution.py:125
  165.0 3.8 all-to-all-start.5
  168.8 8.1 %copy.36 = bf16[4,8,9,8192]{3,0,2,1:T(4,128)(2,1)} copy(bf16[4,8,9,8192]{3,1,2,0:T(8,128)(2,1)} %all-to-all-done) | data formatting | bytes 9437184 | tf_op jit(solution)/shard_map/all_to_all | solution.py:125
  176.9 25.5 %all-to-all-done.5 = bf16[4,8,9,1024]{3,0,2,1:T(4,128)(2,1)S(1)} async-done(((bf16[4,8,9,1024]{3,0,2,1:T(4,128)(2,1)}), bf16[4,8,9,1024]{3,0,2,1:T(4,128)(2,1)S(1)}, u32[]{:S(2)}, u32[]{:S(2)}) %all-to-all-start.5) | async-done | bytes 589856 | tf_op jit(solution)/shard_map/all_to_all | solution.py:137
  202.4 4.6 all-to-all-start.1
  207.0 0.3 reduce-scatter.7.cloned.1.call-start
  208.9 0.7 copy.43
  209.6 1.2 reshape.84
  210.8 141.6 %all-to-all-done.1 = bf16[4,8,9,8192]{3,0,2,1:T(4,128)(2,1)} async-done(((bf16[4,8,9,8192]{3,0,2,1:T(4,128)(2,1)}), bf16[4,8,9,8192]{3,0,2,1:T(4,128)(2,1)}, u32[]{:S(2)}, u32[]{:S(2)}) %all-to-all-start.1) | async-done | bytes 4718624 | tf_op jit(solution)/shard_map/all_to_all | solution.py:124
  352.4 8.6 %copy.37 = bf16[4,8,9,8192]{3,2,1,0:T(8,128)(2,1)} copy(bf16[4,8,9,8192]{3,0,2,1:T(4,128)(2,1)} %all-to-all-done.1) | data formatting | bytes 9437184 | tf_op jit(solution)/shard_map/all_to_all | solution.py:124
  361.0 7.0 %reshape.80 = bf16[288,8192]{1,0:T(8,128)(2,1)} reshape(bf16[4,8,9,8192]{3,2,1,0:T(8,128)(2,1)} %copy.37) | data formatting | bytes 9437184 | tf_op jit(solution)/shard_map/reshape | solution.py:164
  368.0 4.0 convolution_convert_fusion.3
  372.0 10.0 %fusion.37 = f32[288,1024]{1,0:T(8,128)S(1)} fusion(bf16[288,8192]{1,0:T(8,128)(2,1)} %reshape.80, bf16[8192,1024]{1,0:T(8,128)(2,1)} %all-gather.3.cloned.1.call-done), kind=kOutput, calls=%fused_computation.70 | convolution fusion | flops 4831838208 | bytes 22675456 | tf_op jit(solution)/shard_map/dot_general | solution.py:167
  382.1 0.4 fusion.13
  382.6 0.6 copy-done.10
  383.1 0.8 copy-done.1
  384.2 4.1 fusion
  388.4 4.1 convolution_convert_fusion.1
  392.5 0.4 fusion.14
  393.0 0.8 copy-done.2
  393.8 1.6 multiply_reduce_fusion.1
  395.4 6.2 multiply_reduce_fusion
  402.9 1.0 broadcast_multiply_fusion.1
  403.9 1.0 copy.46
  405.0 3.1 broadcast_multiply_fusion
  408.1 0.7 copy-done.7
  408.8 129.3 %reduce-scatter.7.cloned.1.call-done = f32[32,64]{1,0:T(8,128)} async-done(((f32[1024,64]{1,0:T(8,128)}), f32[32,64]{1,0:T(8,128)}) %reduce-scatter.7.cloned.1.call-update) | async-done | bytes 8208
  538.1 0.8 copy.47
  538.9 0.7 copy.45
  539.6 134.4 %reduce-scatter.5.cloned.1.call-done = f32[256,64]{0,1:T(8,128)} async-done(((f32[8192,64]{0,1:T(8,128)}), f32[256,64]{0,1:T(8,128)}) %reduce-scatter.5.cloned.1.call-update) | async-done | bytes 65552 | tf_op jit(solution)/shard_map/reduce_scatter | solution.py:187
  674.0 1.5 multiply_add_fusion
  (79 shorter events, 2.6 us)
Async XLA Ops:
  7.2 1.4 copy-start.8
  7.2 50.2 %copy-start.9 = (s32[32]{0:T(128)S(1)}, s32[32]{0:T(128)}, u32[]{:S(2)}) copy-start(s32[32]{0:T(128)} %param.17) | copy-start | bytes 388
  7.2 364.8 %all-gather.3.cloned.1.call-start = ((), (), s32[]{:S(2)}) async-start(), calls=%async_computation.8 | async-start | bytes 18874368 | tf_op jit(solution)/shard_map/all_gather | solution.py:169
  67.8 10.4 %all-to-all-start.3 = ((bf16[4,8,9]{2,0,1:T(4,128)(2,1)}), bf16[4,8,9]{2,0,1:T(4,128)(2,1)S(1)}, u32[]{:S(2)}, u32[]{:S(2)}) async-start(bf16[4,8,9]{2,0,1:T(4,128)(2,1)} %copy.38), calls=%async_computation.3 | async-start | bytes 16384 | tf_op jit(solution)/shard_map/all_to_all | solution.py:150
  78.2 27.9 %all-to-all-start.4 = ((bf16[4,8,9,1024]{3,1,2,0:T(8,128)(2,1)}), bf16[4,8,9,1024]{3,1,2,0:T(8,128)(2,1)S(1)}, u32[]{:S(2)}, u32[]{:S(2)}) async-start(bf16[4,8,9,1024]{3,1,2,0:T(8,128)(2,1)} %copy.40), calls=%async_computation.4 | async-start | bytes 1179648 | tf_op jit(solution)/shard_map/all_to_all | solution.py:138
  106.1 58.9 %all-to-all-start = ((bf16[4,8,9,8192]{3,1,2,0:T(8,128)(2,1)}), bf16[4,8,9,8192]{3,1,2,0:T(8,128)(2,1)}, u32[]{:S(2)}, u32[]{:S(2)}) async-start(bf16[4,8,9,8192]{3,1,2,0:T(8,128)(2,1)} %copy.35), calls=%async_computation | async-start | bytes 9437184 | tf_op jit(solution)/shard_map/all_to_all | solution.py:125
  165.0 37.4 %all-to-all-start.5 = ((bf16[4,8,9,1024]{3,0,2,1:T(4,128)(2,1)}), bf16[4,8,9,1024]{3,0,2,1:T(4,128)(2,1)S(1)}, u32[]{:S(2)}, u32[]{:S(2)}) async-start(bf16[4,8,9,1024]{3,0,2,1:T(4,128)(2,1)} %copy.41), calls=%async_computation.5 | async-start | bytes 1179648 | tf_op jit(solution)/shard_map/all_to_all | solution.py:137
  202.4 150.0 %all-to-all-start.1 = ((bf16[4,8,9,8192]{3,0,2,1:T(4,128)(2,1)}), bf16[4,8,9,8192]{3,0,2,1:T(4,128)(2,1)}, u32[]{:S(2)}, u32[]{:S(2)}) async-start(bf16[4,8,9,8192]{3,0,2,1:T(4,128)(2,1)} %copy.36), calls=%async_computation.1 | async-start | bytes 9437184 | tf_op jit(solution)/shard_map/all_to_all | solution.py:124
  207.0 331.1 %reduce-scatter.7.cloned.1.call-start = ((), (), s32[]{:S(2)}) async-start(), calls=%async_computation.10 | async-start | bytes 540672
  361.0 7.0 %copy-start = (bf16[8192,64]{0,1:T(8,128)(2,1)S(1)}, bf16[8192,64]{0,1:T(8,128)(2,1)}, u32[]{:S(2)}) copy-start(bf16[8192,64]{0,1:T(8,128)(2,1)} %param.19) | copy-start | bytes 3145732
  372.0 10.1 %copy-start.3 = (bf16[64,1024]{1,0:T(8,128)(2,1)S(1)}, bf16[64,1024]{1,0:T(8,128)(2,1)}, u32[]{:S(2)}) copy-start(bf16[64,1024]{1,0:T(8,128)(2,1)} %param.20) | copy-start | bytes 393220
  372.0 10.1 %copy-start.4 = (f32[288,1024]{1,0:T(8,128)S(1)}, f32[288,1024]{1,0:T(8,128)}, u32[]{:S(2)}) copy-start(f32[288,1024]{1,0:T(8,128)} %reshape.84) | copy-start | bytes 3538948
  382.1 1.0 copy-start.10
  383.1 0.8 copy-start.1
  388.4 4.2 copy-start.5
  388.4 4.2 copy-start.11
  393.0 0.8 copy-start.2
  404.9 269.0 %reduce-scatter.5.cloned.1.call-start = ((), (), s32[]{:S(2)}) async-start(), calls=%async_computation.9 | async-start | bytes 2162688 | tf_op jit(solution)/shard_map/reduce_scatter | solution.py:187
  408.1 0.7 copy-start.7
  408.1 265.9 %copy-start.6 = (f32[256,64]{0,1:T(8,128)S(1)}, f32[256,64]{0,1:T(8,128)}, u32[]{:S(2)}) copy-start(f32[256,64]{0,1:T(8,128)} %param.22) | copy-start | bytes 196612
Sparse Core Ops, SparseCore 0:
  10.1 315.9 all-gather.2
  405.1 132.9 reduce-scatter.6
  540.5 133.4 reduce-scatter.4
where the time goes:
time: 683 us; the launch traced here: 682 us
  waiting for transfers between devices  487 us (71%)
  local copies, waits for them, and re-layouts  63 us (9%)
  blocking collectives  53.9 us (8%)
  matrix products  31.6 us (5%)
  starting transfers between devices  20.9 us (3%)
  between operations  17.4 us (3%)
  other arithmetic  7.26 us (1%)
    all_to_all x1, waiting for transfers between devices, body(): lax.all_to_all(lax.all_to_all(send_rows.reshape(groups, members, most_row...  142 us
    reduce_scatter x1, waiting for transfers between devices, body(): lax.psum_scatter(down_partial, ('grp', 'fsdp'), scatter_dimension=0, tile...  134 us
    unnamed x4, waiting for transfers between devices  130 us
    all_to_all x1, waiting for transfers between devices, body(): lax.all_to_all(send_rows.reshape(groups, members, most_rows, width), 'grp...  52.6 us
    unnamed x1, blocking collectives  46.7 us
    all_to_all x1, waiting for transfers between devices, body(): lax.all_to_all(lax.all_to_all(send_goal.reshape(groups, members, most_row...  25.5 us
    reshape x2, local copies, waits for them, and re-layouts, body(): send_rows.reshape(groups, members, most_rows, width)  15.6 us
  transfers between devices with their start and end apart: 8, of which 6 were waited for; matrix products, arithmetic and copies ran while one was open for 10% of the time, Pallas kernels for 0%

commit v1 on v0

v1 whole, which is shorter than its diff:
```python
import jax
import jax.numpy as jnp
from jax import lax
from jax.experimental import pallas as pl
from jax.experimental.pallas import tpu as pltpu
from jax.sharding import PartitionSpec as P

STEPS = 2
ADAPTER_SCALE = 2.0
LEARN_RATE = 0.05
EPSILON = 1e-06

SUB = 8
LANES = 128
BOTH = ("grp", "fsdp")
VMEM_BYTES = 56 * 1024 * 1024

F32 = jnp.float32
BF16 = jnp.bfloat16


def dot(left, right, contract=((1,), (0,))):
    return lax.dot_general(left, right, (contract, ((), ())), preferred_element_type=F32)


def iota(shape, axis):
    return lax.broadcasted_iota(jnp.int32, shape, axis)


def pack_kernel(users, most, count_ref, owner_ref, tokens_ref, targets_ref, out_ref):
    rows = tokens_ref.shape[0]
    groups, rest = divmod(most, SUB)
    owner = owner_ref[...]
    first, second = (iota((rows, rows), 0), iota((rows, rows), 1))
    owner_row = jnp.sum(jnp.where(first == second, owner, 0), axis=0, keepdims=True)
    same = (owner == owner_row) & (first < second)
    rank = jnp.sum(same.astype(jnp.int32), axis=0, keepdims=True)
    line = iota((users * SUB, rows), 0)
    mine = line // SUB == owner_row
    slot = line % SUB
    column = 0
    for source in (tokens_ref, targets_ref):
        width = source.shape[1]
        for group in range(groups):
            pick = (mine & (rank == slot + group * SUB)).astype(BF16)
            step = min(width, 1024)
            for at in range(0, width, step):
                out_ref[:, column + at : column + at + step] = dot(
                    pick, source[:, at : at + step]
                ).astype(BF16)
            column += width
        piece = width // SUB
        for extra in range(rest):
            here = mine & (rank == groups * SUB + extra)
            total = None
            for part in range(SUB):
                pick = (here & (slot == part)).astype(BF16)
                term = dot(pick, source[:, part * piece : (part + 1) * piece])
                total = term if total is None else total + term
            out_ref[:, column : column + piece] = total.astype(BF16)
            column += piece
    used = mine & (iota((users * SUB, rows), 1) < count_ref[0])
    number = jnp.sum(used.astype(F32), axis=1, keepdims=True)
    out_ref[:, column : column + LANES] = jnp.broadcast_to(number, (users * SUB, LANES)).astype(
        BF16
    )


def user_kernel(
    devices,
    most,
    where_ref,
    clip_ref,
    got_ref,
    near_ref,
    far_ref,
    down_ref,
    up_ref,
    out_ref,
    x_ref,
    goal_ref,
    cut_ref,
    cut_goal_ref,
    used_ref,
    w_ref,
    frozen_ref,
    hidden_ref,
    a_half_ref,
    delta_ref,
    got_sem,
    w_sem,
):
    groups, rest = divmod(most, SUB)
    rank, width = down_ref.shape
    kv_width = up_ref.shape[1]
    whole = devices * SUB
    shards, half = (near_ref.shape[0], near_ref.shape[1])
    copies = []
    column = 0
    for full, cut in ((x_ref, cut_ref), (goal_ref, cut_goal_ref)):
        size = full.shape[1]
        for group in range(groups):
            copies.append(
                (got_ref.at[:, pl.ds(column, size)], full.at[pl.ds(group * whole, whole), :])
            )
            column += size
        for extra in range(rest):
            copies.append((got_ref.at[:, pl.ds(column, size // SUB)], cut.at[extra]))
            column += size // SUB
    copies.append((got_ref.at[:, pl.ds(column, LANES)], used_ref))
    copies = [
        pltpu.make_async_copy(source, target, got_sem.at[place])
        for place, (source, target) in enumerate(copies)
    ]
    for copy in copies:
        copy.start()

    def weight_copy(shard, side):
        source = (near_ref, far_ref)[side]
        return pltpu.make_async_copy(
            source.at[shard], w_ref.at[side, shard], w_sem.at[side, shard]
        )

    for shard in range(shards):
        weight_copy(shard, 0).start()
        weight_copy(shard, 1).start()
    for copy in copies:
        copy.wait()

    line, other = (iota((devices, whole), 0), iota((devices, whole), 1))
    for extra in range(rest):
        bottom = groups * whole + extra * devices
        for full, cut in ((x_ref, cut_ref), (goal_ref, cut_goal_ref)):
            piece = full.shape[1] // SUB
            for part in range(SUB):
                pick = (other == line * SUB + part).astype(BF16)
                full[bottom : bottom + devices, part * piece : (part + 1) * piece] = dot(
                    pick, cut[extra]
                ).astype(BF16)

    cap = where_ref[0].astype(F32)
    used = used_ref[...]
    pieces = []
    if groups:
        line, other = (iota((whole, whole), 0), iota((whole, whole), 1))
        earlier = dot(((other // SUB < line // SUB) & (other % SUB == 0)).astype(BF16), used)
        own = used.astype(F32)
        for group in range(groups):
            spot = (iota((whole, LANES), 0) % SUB + group * SUB).astype(F32)
            live = (spot < own) & (earlier + spot < cap)
            pieces.append(jnp.where(live, 1.0 / cap, 0.0)[:, :1])
    line, other = (iota((devices, whole), 0), iota((devices, whole), 1))
    earlier = dot((other < line * SUB).astype(BF16) * (other % SUB == 0).astype(BF16), used)
    own = dot((other == line * SUB).astype(BF16), used)
    for extra in range(rest):
        spot = float(groups * SUB + extra)
        live = (own > spot) & (earlier + spot < cap)
        pieces.append(jnp.where(live, 1.0 / cap, 0.0)[:, :1])
    scale = jnp.concatenate(pieces, axis=0) if len(pieces) > 1 else pieces[0]

    frozen_ref[...] = jnp.zeros_like(frozen_ref)
    hidden_ref[...] = jnp.zeros_like(hidden_ref)
    side = where_ref[1]

    def add_shard(shard, unused):
        weight_copy(shard, 0).wait()
        weight_copy(shard, 1).wait()
        near = pl.ds(pl.multiple_of((2 * shard + side) * half, half), half)
        far = pl.ds(pl.multiple_of((2 * shard + 1 - side) * half, half), half)
        near_x, far_x = (x_ref[:, near], x_ref[:, far])
        frozen_ref[...] += dot(near_x, w_ref[0, shard]) + dot(far_x, w_ref[1, shard])
        lanes = ((1,), (1,))
        hidden_ref[...] += dot(near_x, down_ref[:, near], lanes) + dot(
            far_x, down_ref[:, far], lanes
        )
        return unused

    lax.fori_loop(0, shards, add_shard, 0)

    rate = ADAPTER_SCALE * LEARN_RATE
    block = min(width, 1024)
    up = up_ref[...].astype(F32)
    up_half = up_ref[...]
    up_delta = jnp.zeros((rank, kv_width), F32)
    for step in range(STEPS):
        hidden = hidden_ref[...].astype(BF16)
        error = frozen_ref[...] + ADAPTER_SCALE * dot(hidden, up_half) - goal_ref[...].astype(F32)
        residual = (scale * error).astype(BF16)
        back = dot(residual, up_half, ((1,), (1,))).astype(BF16)
        up_delta = up_delta - rate * dot(hidden, residual, ((0,), (0,)))
        last = step == STEPS - 1
        if not last:
            up_half = (up + up_delta).astype(BF16)
            hidden_ref[...] = jnp.zeros_like(hidden_ref)

        def down_block(at, unused):
            lanes = pl.ds(pl.multiple_of(at * block, block), block)
            moved = -rate * dot(back, x_ref[:, lanes], ((0,), (0,)))
            if step:
                moved = moved + delta_ref[:, lanes]
            delta_ref[:, lanes] = moved
            if not last:
                half_down = (down_ref[:, lanes].astype(F32) + moved).astype(BF16)
                hidden_ref[...] += dot(x_ref[:, lanes], half_down, ((1,), (1,)))
                return unused
            return unused + jnp.sum(moved * moved)

        squares = lax.fori_loop(0, width // block, down_block, jnp.zeros((), F32))

    total = squares + jnp.sum(up_delta * up_delta) + EPSILON
    total = jnp.full((1, LANES), total, F32)
    factor = jnp.minimum(1.0, clip_ref[0] / jnp.sqrt(total))[:, :1]
    share = width // devices
    up_share = kv_width // devices
    up_turned = (factor * up_delta).T
    pieces = share // rank
    tall = up_share // pieces
    for device in range(devices):
        out_ref[device, :rank, :] = factor * delta_ref[:, device * share : (device + 1) * share]
        parts = [
            up_turned[device * up_share + at * tall : device * up_share + (at + 1) * tall]
            for at in range(pieces)
        ]
        out_ref[device, rank:, :] = (
            jnp.concatenate(parts, axis=1) if pieces > 1 else parts[0]
        )


def body(
    tokens,
    targets,
    row_owner_user,
    device_row_count,
    user_row_cap,
    value_weight,
    adapter_down,
    adapter_up,
    clip_norm_bound,
    down_noise,
    up_noise,
):
    groups, members = (lax.axis_size("grp"), lax.axis_size("fsdp"))
    devices = groups * members
    myself = lax.axis_index(BOTH)
    side = lax.axis_index("grp") % 2
    per_dev, width = tokens.shape
    kv_width = targets.shape[1]
    rank = adapter_down.shape[1]
    users = user_row_cap.shape[0]
    most = 3 * per_dev // (2 * devices)
    slots = devices * most
    whole = devices * SUB
    whole_groups, rest = divmod(most, SUB)
    smem = pl.BlockSpec(memory_space=pltpu.SMEM)
    vmem = pl.BlockSpec(memory_space=pltpu.VMEM)
    anywhere = pl.BlockSpec(memory_space=pl.ANY)

    half = value_weight.shape[0] // 2
    mine = lax.dynamic_slice_in_dim(value_weight, side * half, half, axis=0)
    near = lax.all_gather(mine, "fsdp", axis=0)
    far = lax.ppermute(near, "grp", [(at, at ^ 1) for at in range(groups)])

    columns = whole_groups * (width + kv_width) + rest * (width + kv_width) // SUB + LANES
    packed = pl.pallas_call(
        lambda *refs: pack_kernel(users, most, *refs),
        out_shape=jax.ShapeDtypeStruct((users * SUB, columns), BF16),
        in_specs=[smem, vmem, vmem, vmem],
        out_specs=vmem,
        compiler_params=pltpu.CompilerParams(vmem_limit_bytes=VMEM_BYTES),
        name="pack_rows",
    )(device_row_count, row_owner_user, tokens, targets)
    got = lax.all_to_all(
        packed.reshape(users, SUB, columns), BOTH, split_axis=0, concat_axis=0, tiled=True
    ).reshape(whole, columns)

    cap = lax.dynamic_slice_in_dim(user_row_cap, myself, 1)
    where = jnp.concatenate([cap, side[None].astype(jnp.int32)])
    share = width // devices
    tall = rank + kv_width // devices * rank // share
    package = pl.pallas_call(
        lambda *refs: user_kernel(devices, most, *refs),
        out_shape=jax.ShapeDtypeStruct((devices, tall, share), F32),
        in_specs=[smem, smem, anywhere, anywhere, anywhere, vmem, vmem],
        out_specs=vmem,
        scratch_shapes=[
            pltpu.VMEM((slots, width), BF16),
            pltpu.VMEM((slots, kv_width), BF16),
            pltpu.VMEM((max(rest, 1), whole, width // SUB), BF16),
            pltpu.VMEM((max(rest, 1), whole, kv_width // SUB), BF16),
            pltpu.VMEM((whole, LANES), BF16),
            pltpu.VMEM((2, members, half, kv_width), BF16),
            pltpu.VMEM((slots, kv_width), F32),
            pltpu.VMEM((slots, rank), F32),
            pltpu.VMEM((rank, width), BF16),
            pltpu.VMEM((rank, width), F32),
            pltpu.SemaphoreType.DMA((2 * (whole_groups + rest) + 1,)),
            pltpu.SemaphoreType.DMA((2, members)),
        ],
        compiler_params=pltpu.CompilerParams(vmem_limit_bytes=VMEM_BYTES),
        name="user_steps",
    )(where, clip_norm_bound, got, near, far, adapter_down.T, adapter_up)

    package = package.reshape(groups, members, tall, share)
    package = lax.all_to_all(package, "grp", split_axis=0, concat_axis=0, tiled=True)
    package = jnp.sum(package, axis=0)
    package = lax.all_to_all(package, "fsdp", split_axis=0, concat_axis=0, tiled=True)
    package = jnp.sum(package, axis=0)
    clip = clip_norm_bound[0]
    update_a = package[:rank].T + clip * down_noise
    pieces = share // rank
    up_sum = package[rank:].reshape(tall - rank, pieces, rank).transpose(1, 0, 2)
    update_b = up_sum.reshape(kv_width // devices, rank).T + clip * up_noise
    return (update_a, update_b)


def solution(mesh):
    in_specs = (
        P(BOTH, None),
        P(BOTH, None),
        P(BOTH, None),
        P(BOTH),
        P(),
        P("fsdp", None),
        P(),
        P(),
        P(),
        P(BOTH, None),
        P(None, BOTH),
    )
    out_specs = (P(BOTH, None), P(None, BOTH))
    return jax.shard_map(body, mesh=mesh, in_specs=in_specs, out_specs=out_specs, check_vma=False)
```

time: 683 us -> 346 us (0.51)
  waiting for transfers between devices: 487 us -> 228 us
  local copies, waits for them, and re-layouts: 63 us -> 4.07 us
  Pallas kernels: 0 us -> 35 us
  matrix products: 31.6 us -> 0 us
  starting transfers between devices: 20.9 us -> 7.46 us
    all_to_all x5 -> x1, waiting for transfers between devices: 223 us -> 0.01 us  [body(): lax.all_to_all(packed.reshape(users, SUB, columns), BOTH, split_axis=0, c...]
    all_gather x1, waiting for transfers between devices: 0.02 us -> 217 us  [body(): near = lax.all_gather(mine, 'fsdp', axis=0)]
    reduce_scatter x1 -> x0, waiting for transfers between devices: 134 us -> none  [body(): lax.psum_scatter(down_partial, ('grp', 'fsdp'), scatter_dimension=0, tile...]
    unnamed x4 -> x1, waiting for transfers between devices: 130 us -> 0.02 us
    unnamed x1 -> x0, blocking collectives: 46.7 us -> none
    all_to_all x1 -> x2, blocking collectives: 7.15 us -> 51.9 us  [the longest x1 33 us: body(): lax.all_to_all(package, 'grp', split_axis=0, concat_axis=0, tiled=True)]
    pallas_call x0 -> x2, Pallas kernels: none -> 35 us  [the longest x1 27.7 us: body(): pl.pallas_call(lambda *refs: user_kernel(devices, most, *refs), out_shape...]
    dot_general x11 -> x0, matrix products: 31.6 us -> none  [the longest x2 10.4 us: adapter_step(): lax.dot_general(input_rows, backward_pass, (((0,), (0,)), ((), ())), pref...]
  transfers between devices with their start and end apart: 8 -> 3, of which waited for: 6 -> 2; matrix products, arithmetic and copies ran while one was open for 10% -> 1% of each run, Pallas kernels for 0% -> 2%
where the time goes in v1:
time: 346 us
  waiting for transfers between devices  228 us (66%)
  blocking collectives  51.9 us (15%)
  Pallas kernels  35 us (10%)
  between operations  15.4 us (4%)
  starting transfers between devices  7.46 us (2%)
  other arithmetic  4.48 us (1%)
  local copies, waits for them, and re-layouts  4.07 us (1%)
    all_gather x1, waiting for transfers between devices, body(): near = lax.all_gather(mine, 'fsdp', axis=0)  217 us
    all_to_all x1, blocking collectives, body(): lax.all_to_all(package, 'grp', split_axis=0, concat_axis=0, tiled=True)  33 us
    pallas_call x1, Pallas kernels, body(): pl.pallas_call(lambda *refs: user_kernel(devices, most, *refs), out_shape...  27.7 us
    all_to_all x1, blocking collectives, body(): lax.all_to_all(package, 'fsdp', split_axis=0, concat_axis=0, tiled=True)  18.9 us
    ppermute x1, waiting for transfers between devices, body(): far = lax.ppermute(near, 'grp', [(at, at ^ 1) for at in range(groups)])  10.9 us
    all_to_all x1, starting transfers between devices, body(): lax.all_to_all(packed.reshape(users, SUB, columns), BOTH, split_axis=0, c...  7.41 us
    pallas_call x1, Pallas kernels, body(): pl.pallas_call(lambda *refs: pack_kernel(users, most, *refs), out_shape=j...  7.25 us
  transfers between devices with their start and end apart: 3, of which 2 were waited for; matrix products, arithmetic and copies ran while one was open for 1% of the time, Pallas kernels for 2%

profile of v1, /device:TPU:0, one launch (start us, length us, event | category | flops | bytes accessed | tf_op | source)
XLA Modules:
  0.0 345.9 jit_solution(5348583967629691673)
XLA Ops:
  7.2 0.0 copy-start
  7.2 0.0 copy-start.3
  7.2 0.0 all-gather.3.cloned.1.call-start
  7.3 1.5 copy-done
  8.8 1.1 constant_dynamic-slice_fusion
  9.9 0.0 all-gather.3.cloned.1.call-update
  10.5 0.0 copy-done.3
  10.5 0.8 copy.15.refs_1_
  11.3 7.3 %pack_rows.1 = bf16[256,10496]{1,0:T(8,128)(2,1)} custom-call(s32[1]{0:T(128)S(6)} %copy.18.refs_0_, s32[192,1]{1,0:T(8,128)} %copy.15.refs_1_, bf16[192,8192]{1,0:T(8,128)(2,1)} %refs_2_.1, bf16[192,1024]{1,0:T(8,128)(2,1)} %refs_3_.1), custom_call_target="tpu_custom_call" | custom-call | tf_op jit(solution)/shard_map/pack_rows/pallas_call | solution.py:264
  18.6 0.0 copy-start.4
  18.6 7.4 %all-to-all-start = ((bf16[32,8,10496]{2,1,0:T(8,128)(2,1)}), bf16[32,8,10496]{2,1,0:T(8,128)(2,1)}, u32[]{:S(2)}, u32[]{:S(2)}) async-start(bf16[32,8,10496]{2,1,0:T(8,128)(2,1)} %bitcast.18), calls=%async_computation | async-start | bytes 10747904 | tf_op jit(solution)/shard_map/all_to_all | solution.py:272
  26.0 216.6 %all-gather.3.cloned.1.call-done = bf16[4096,1024]{1,0:T(8,128)(2,1)} async-done(((bf16[512,1024]{1,0:T(8,128)(2,1)}), bf16[4096,1024]{1,0:T(8,128)(2,1)}) %all-gather.3.cloned.1.call-update) | async-done | bytes 8388624 | tf_op jit(solution)/shard_map/all_gather | solution.py:260
  242.6 0.0 collective-permute-start
  243.3 0.0 copy-done.4
  243.3 0.6 dynamic_slice.6
  243.9 1.3 pad_add_fusion.refs_0_
  245.2 0.0 all-to-all-done
  245.2 10.9 %collective-permute-done.refs_4_ = bf16[8,512,1024]{2,1,0:T(8,128)(2,1)} collective-permute-done((bf16[8,512,1024]{2,1,0:T(8,128)(2,1)}, bf16[8,512,1024]{2,1,0:T(8,128)(2,1)}, u32[]{:S(2)}, u32[]{:S(2)}) %collective-permute-start) | collective-permute-done | bytes 8388640 | tf_op jit(solution)/shard_map/ppermute | solution.py:261
  256.1 27.7 %user_steps.1 = f32[32,72,256]{2,1,0:T(8,128)} custom-call(s32[2]{0:T(128)} %pad_add_fusion.refs_0_, f32[1]{0:T(128)} %copy.19.refs_1_, bf16[256,10496]{1,0:T(8,128)(2,1)} %bitcast.2.refs_2_, bf16[8,512,1024]{2,1,0:T(8,128)(2,1)} %bitcast.21, bf16[8,512,1024]{2,1,0:T(8,128)(2,1)} %collective-permute-done.refs_4_, bf16[64,8192]{1,0:T(8,128)(2,1)} %bitcast.22, ...), custom_call_target="tpu_custom_call" | custom-call | tf_op jit(solution)/shard_map/user_steps/pallas_call | solution.py:280
  283.9 33.0 %all_to_all.15 = f32[4,8,72,256]{3,2,1,0:T(8,128)} all-to-all(f32[4,8,72,256]{3,2,1,0:T(8,128)} %bitcast.19), channel_id=1, replica_groups=mesh['grp'=4,'fsdp'=8] {'grp'}, dimensions={0} | all-to-all | bytes 4718592 | tf_op jit(solution)/shard_map/all_to_all | solution.py:304
  316.9 0.0 copy-start.1
  316.9 0.0 copy-start.2
  316.9 1.9 reduce_sum.18
  318.8 18.9 %all_to_all.16 = f32[8,72,256]{2,1,0:T(8,128)S(1)} all-to-all(f32[8,72,256]{2,1,0:T(8,128)S(1)} %reduce_sum.18), channel_id=1, replica_groups=mesh['grp'=4,'fsdp'=8] {'fsdp'}, dimensions={0} | all-to-all | bytes 1179648 | tf_op jit(solution)/shard_map/all_to_all | solution.py:306
  337.7 0.1 reshape.22
  337.8 0.0 copy-done.1
  337.8 0.6 fusion
  338.4 0.0 copy-done.2
  338.4 0.6 bitcast_add_fusion
  (2 shorter events, 0.0 us)
Async XLA Ops:
  7.2 1.6 copy-start
  7.2 3.4 copy-start.3
  7.2 235.4 %all-gather.3.cloned.1.call-start = ((), (), s32[]{:S(2)}) async-start(), calls=%async_computation.3 | async-start | bytes 9437184 | tf_op jit(solution)/shard_map/all_gather | solution.py:260
  18.6 224.7 %copy-start.4 = (s32[32]{0:T(128)S(1)}, s32[32]{0:T(128)}, u32[]{:S(2)}) copy-start(s32[32]{0:T(128)} %param.15) | copy-start | bytes 388
  18.6 226.6 %all-to-all-start = ((bf16[32,8,10496]{2,1,0:T(8,128)(2,1)}), bf16[32,8,10496]{2,1,0:T(8,128)(2,1)}, u32[]{:S(2)}, u32[]{:S(2)}) async-start(bf16[32,8,10496]{2,1,0:T(8,128)(2,1)} %bitcast.18), calls=%async_computation | async-start | bytes 10747904 | tf_op jit(solution)/shard_map/all_to_all | solution.py:272
  242.6 13.5 %collective-permute-start = (bf16[8,512,1024]{2,1,0:T(8,128)(2,1)}, bf16[8,512,1024]{2,1,0:T(8,128)(2,1)}, u32[]{:S(2)}, u32[]{:S(2)}) collective-permute-start(bf16[8,512,1024]{2,1,0:T(8,128)(2,1)} %bitcast.20), channel_id=1, source_target_pairs={{0,8},{8,0},{16,24},{24,16},{1,9},{9,1},{17,25},{25,17},{2,10},{10... | collective-permute-start | bytes 25165832 | tf_op jit(solution)/shard_map/ppermute | solution.py:261
  316.9 20.9 %copy-start.1 = (f32[256,64]{0,1:T(8,128)S(1)}, f32[256,64]{0,1:T(8,128)}, u32[]{:S(2)}) copy-start(f32[256,64]{0,1:T(8,128)} %param.20) | copy-start | bytes 196612
  316.9 21.5 %copy-start.2 = (f32[64,32]{0,1:T(8,128)S(1)}, f32[64,32]{0,1:T(8,128)}, u32[]{:S(2)}) copy-start(f32[64,32]{0,1:T(8,128)} %param.21) | copy-start | bytes 24580
Sparse Core Ops, SparseCore 0:
  10.1 232.4 all-gather.2

commit v2 on v1

--- a/solution.py
+++ b/solution.py
@@ -68,33 +68,37 @@
 
 def user_kernel(
     devices,
+    members,
     most,
     where_ref,
     clip_ref,
     got_ref,
-    near_ref,
-    far_ref,
     down_ref,
     up_ref,
-    out_ref,
-    x_ref,
-    goal_ref,
-    cut_ref,
-    cut_goal_ref,
-    used_ref,
-    w_ref,
-    frozen_ref,
-    hidden_ref,
-    a_half_ref,
-    delta_ref,
-    got_sem,
-    w_sem,
+    *refs,
 ):
+    shards = members
+    near_refs, far_refs = (refs[:shards], refs[shards : 2 * shards])
+    (
+        keep_ref,
+        send_ref,
+        x_ref,
+        goal_ref,
+        cut_ref,
+        cut_goal_ref,
+        used_ref,
+        w_ref,
+        frozen_ref,
+        hidden_ref,
+        delta_ref,
+        got_sem,
+        w_sem,
+    ) = refs[2 * shards :]
     groups, rest = divmod(most, SUB)
     rank, width = down_ref.shape
     kv_width = up_ref.shape[1]
     whole = devices * SUB
-    shards, half = (near_ref.shape[0], near_ref.shape[1])
+    half = near_refs[0].shape[0]
     copies = []
     column = 0
     for full, cut in ((x_ref, cut_ref), (goal_ref, cut_goal_ref)):
@@ -115,15 +119,9 @@
     for copy in copies:
         copy.start()
 
-    def weight_copy(shard, side):
-        source = (near_ref, far_ref)[side]
-        return pltpu.make_async_copy(
-            source.at[shard], w_ref.at[side, shard], w_sem.at[side, shard]
-        )
-
-    for shard in range(shards):
-        weight_copy(shard, 0).start()
-        weight_copy(shard, 1).start()
+    for place in range(shards):
+        for at, source in enumerate((near_refs[place], far_refs[place])):
+            pltpu.make_async_copy(source, w_ref.at[at, place], w_sem.at[at, place]).start()
     for copy in copies:
         copy.wait()
 
@@ -162,13 +160,15 @@
     hidden_ref[...] = jnp.zeros_like(hidden_ref)
     side = where_ref[1]
 
-    def add_shard(shard, unused):
-        weight_copy(shard, 0).wait()
-        weight_copy(shard, 1).wait()
+    def add_shard(place, unused):
+        for at in range(2):
+            block = w_ref.at[at, place]
+            pltpu.make_async_copy(block, block, w_sem.at[at, place]).wait()
+        shard = where_ref[3 + place]
         near = pl.ds(pl.multiple_of((2 * shard + side) * half, half), half)
         far = pl.ds(pl.multiple_of((2 * shard + 1 - side) * half, half), half)
         near_x, far_x = (x_ref[:, near], x_ref[:, far])
-        frozen_ref[...] += dot(near_x, w_ref[0, shard]) + dot(far_x, w_ref[1, shard])
+        frozen_ref[...] += dot(near_x, w_ref[0, place]) + dot(far_x, w_ref[1, place])
         lanes = ((1,), (1,))
         hidden_ref[...] += dot(near_x, down_ref[:, near], lanes) + dot(
             far_x, down_ref[:, far], lanes
@@ -215,15 +215,74 @@
     up_turned = (factor * up_delta).T
     pieces = share // rank
     tall = up_share // pieces
-    for device in range(devices):
-        out_ref[device, :rank, :] = factor * delta_ref[:, device * share : (device + 1) * share]
-        parts = [
-            up_turned[device * up_share + at * tall : device * up_share + (at + 1) * tall]
-            for at in range(pieces)
+
+    def write(core, target):
+        for pair in range(devices // members // 2):
+            for member in range(members):
+                device = (2 * pair + core) * members + member
+                spot = lax.bitwise_xor(where_ref[2], pair)
+                moved = delta_ref[:, device * share : (device + 1) * share]
+                target[spot, member, :rank, :] = factor * moved
+                first = device * up_share
+                parts = [
+                    up_turned[first + at * tall : first + (at + 1) * tall] for at in range(pieces)
+                ]
+                target[spot, member, rank:, :] = (
+                    jnp.concatenate(parts, axis=1) if pieces > 1 else parts[0]
+                )
+
+    for core in range(2):
+        mine = side == core
+
+        @pl.when(mine)
+        def _():
+            write(core, keep_ref)
+
+        @pl.when(jnp.logical_not(mine))
+        def _():
+            write(core, send_ref)
+
+
+def gather_weight(mine, members):
+    line = members // 2
+    index = lax.axis_index("fsdp")
+    spot, inner = (index // 2, index % 2)
+
+    def hop(value, way):
+        pairs = [
+            (2 * at + one, 2 * (at + way) + one)
+            for at in range(line)
+            for one in range(2)
+            if 0 <= at + way < line
         ]
-        out_ref[device, rank:, :] = (
-            jnp.concatenate(parts, axis=1) if pieces > 1 else parts[0]
+        return lax.ppermute(value, "fsdp", pairs)
+
+    def across(value):
+        return lax.ppermute(value, "fsdp", [(at, at ^ 1) for at in range(members)])
+
+    blocks = [(mine, spot)]
+    ups, downs = ({0: mine}, {0: mine})
+    for step in range(1, line):
+        ups[step] = hop(ups[step - 1], 1)
+        downs[step] = hop(downs[step - 1], -1)
+    for step in range(1, line // 2 + 1):
+        above = spot >= step
+        blocks.append(
+            (jnp.where(above, ups[step], downs[step]), jnp.where(above, spot - step, spot + step))
         )
+    for step in range(1, line // 2):
+        both = (spot >= step) & (spot < line - step)
+        late = line - step
+        value = jnp.where(both, downs[step], jnp.where(spot < step, downs[late], ups[late]))
+        number = jnp.where(
+            both, spot + step, jnp.where(spot < step, spot + late, spot - late)
+        )
+        blocks.append((value, number))
+    values, numbers = ([], [])
+    for value, number in blocks:
+        values += [value, across(value)]
+        numbers += [2 * number + inner, 2 * number + 1 - inner]
+    return values, jnp.stack(numbers).astype(jnp.int32)
 
 
 def body(
@@ -257,8 +316,8 @@
 
     half = value_weight.shape[0] // 2
     mine = lax.dynamic_slice_in_dim(value_weight, side * half, half, axis=0)
-    near = lax.all_gather(mine, "fsdp", axis=0)
-    far = lax.ppermute(near, "grp", [(at, at ^ 1) for at in range(groups)])
+    near, numbers = gather_weight(mine, members)
+    far = [lax.ppermute(block, "grp", [(at, at ^ 1) for at in range(groups)]) for block in near]
 
     columns = whole_groups * (width + kv_width) + rest * (width + kv_width) // SUB + LANES
     packed = pl.pallas_call(
@@ -274,14 +333,16 @@
     ).reshape(whole, columns)
 
     cap = lax.dynamic_slice_in_dim(user_row_cap, myself, 1)
-    where = jnp.concatenate([cap, side[None].astype(jnp.int32)])
+    pair = lax.axis_index("grp") // 2
+    where = jnp.concatenate([cap, jnp.stack([side, pair]).astype(jnp.int32), numbers])
     share = width // devices
     tall = rank + kv_width // devices * rank // share
-    package = pl.pallas_call(
-        lambda *refs: user_kernel(devices, most, *refs),
-        out_shape=jax.ShapeDtypeStruct((devices, tall, share), F32),
-        in_specs=[smem, smem, anywhere, anywhere, anywhere, vmem, vmem],
-        out_specs=vmem,
+    package = jax.ShapeDtypeStruct((groups // 2, members, tall, share), F32)
+    keep, send = pl.pallas_call(
+        lambda *refs: user_kernel(devices, members, most, *refs),
+        out_shape=[package] * 2,
+        in_specs=[smem, smem, anywhere, vmem, vmem] + [anywhere] * (2 * members),
+        out_specs=[vmem] * 2,
         scratch_shapes=[
             pltpu.VMEM((slots, width), BF16),
             pltpu.VMEM((slots, kv_width), BF16),
@@ -291,18 +352,21 @@
             pltpu.VMEM((2, members, half, kv_width), BF16),
             pltpu.VMEM((slots, kv_width), F32),
             pltpu.VMEM((slots, rank), F32),
-            pltpu.VMEM((rank, width), BF16),
             pltpu.VMEM((rank, width), F32),
             pltpu.SemaphoreType.DMA((2 * (whole_groups + rest) + 1,)),
             pltpu.SemaphoreType.DMA((2, members)),
         ],
         compiler_params=pltpu.CompilerParams(vmem_limit_bytes=VMEM_BYTES),
         name="user_steps",
-    )(where, clip_norm_bound, got, near, far, adapter_down.T, adapter_up)
-
-    package = package.reshape(groups, members, tall, share)
-    package = lax.all_to_all(package, "grp", split_axis=0, concat_axis=0, tiled=True)
-    package = jnp.sum(package, axis=0)
+    )(where, clip_norm_bound, got, adapter_down.T, adapter_up, *near, *far)
+
+    package = keep + lax.ppermute(send, "grp", [(at, at ^ 1) for at in range(groups)])
+    bit = groups // 4
+    while bit:
+        partner = [(at, at ^ (2 * bit)) for at in range(groups)]
+        package = package[:bit] + lax.ppermute(package[bit:], "grp", partner)
+        bit //= 2
+    package = package[0]
     package = lax.all_to_all(package, "fsdp", split_axis=0, concat_axis=0, tiled=True)
     package = jnp.sum(package, axis=0)
     clip = clip_norm_bound[0]

time: 346 us -> 336 us (0.971)
  starting transfers between devices: 7.46 us -> 60.2 us
  blocking collectives: 51.9 us -> 18.8 us
  waiting for transfers between devices: 228 us -> 208 us
  between operations: 15.4 us -> 2.33 us
    all_gather x1 -> x0, waiting for transfers between devices: 217 us -> none  [body(): near = lax.all_gather(mine, 'fsdp', axis=0)]
    ppermute x1 -> x20, waiting for transfers between devices: 10.9 us -> 208 us  [the longest x6 145 us: hop(): return lax.ppermute(value, 'fsdp', pairs)]
    ppermute x1 -> x20, starting transfers between devices: 0.01 us -> 52.8 us  [the longest x6 47 us: hop(): return lax.ppermute(value, 'fsdp', pairs)]
    all_to_all x1 -> x0, blocking collectives: 33 us -> none  [body(): lax.all_to_all(package, 'grp', split_axis=0, concat_axis=0, tiled=True)]
    select_n x0 -> x2, other arithmetic: none -> 4.43 us  [the longest x1 2.98 us: gather_weight(): jnp.where(both, downs[step], jnp.where(spot < step, downs[late], ups[late]))]
  transfers between devices with their start and end apart: 3 -> 21, of which waited for: 2 -> 11; matrix products, arithmetic and copies ran while one was open for 1% -> 2% of each run, Pallas kernels for 2% -> 0%
where the time goes in v2:
time: 336 us
  waiting for transfers between devices  208 us (62%)
  starting transfers between devices  60.2 us (18%)
  Pallas kernels  35.1 us (10%)
  blocking collectives  18.8 us (6%)
  other arithmetic  7.22 us (2%)
  local copies, waits for them, and re-layouts  4.03 us (1%)
    ppermute x6, waiting for transfers between devices, hop(): return lax.ppermute(value, 'fsdp', pairs)  145 us
    ppermute x6, starting transfers between devices, hop(): return lax.ppermute(value, 'fsdp', pairs)  47 us
    ppermute x4, waiting for transfers between devices, across(): return lax.ppermute(value, 'fsdp', [(at, at ^ 1) for at in range(members)])  45.4 us
    pallas_call x1, Pallas kernels, body(): pl.pallas_call(lambda *refs: user_kernel(devices, members, most, *refs),...  27.8 us
    all_to_all x1, blocking collectives, body(): lax.all_to_all(package, 'fsdp', split_axis=0, concat_axis=0, tiled=True)  18.8 us
    ppermute x1, waiting for transfers between devices, body(): package = package[:bit] + lax.ppermute(package[bit:], 'grp', partner)  14 us
    all_to_all x1, starting transfers between devices, body(): lax.all_to_all(packed.reshape(users, SUB, columns), BOTH, split_axis=0, c...  7.41 us
    pallas_call x1, Pallas kernels, body(): pl.pallas_call(lambda *refs: pack_kernel(users, most, *refs), out_shape=j...  7.28 us
  transfers between devices with their start and end apart: 21, of which 11 were waited for; matrix products, arithmetic and copies ran while one was open for 2% of the time, Pallas kernels for 0%

profile of v2, /device:TPU:0, one launch (start us, length us, event | category | flops | bytes accessed | tf_op | source)
XLA Modules:
  0.0 335.7 jit_solution(5126314586276846315)
XLA Ops:
  0.6 0.0 copy-start
  1.4 1.4 copy.13.refs_1_
  2.9 7.3 %pack_rows.1 = bf16[256,10496]{1,0:T(8,128)(2,1)} custom-call(s32[1]{0:T(128)S(6)} %copy.16.refs_0_, s32[192,1]{1,0:T(8,128)} %copy.13.refs_1_, bf16[192,8192]{1,0:T(8,128)(2,1)} %refs_2_.1, bf16[192,1024]{1,0:T(8,128)(2,1)} %refs_3_.1), custom_call_target="tpu_custom_call" | custom-call | tf_op jit(solution)/shard_map/pack_rows/pallas_call | solution.py:323
  10.2 7.4 %all-to-all-start = ((bf16[32,8,10496]{2,1,0:T(8,128)(2,1)}), bf16[32,8,10496]{2,1,0:T(8,128)(2,1)}, u32[]{:S(2)}, u32[]{:S(2)}) async-start(bf16[32,8,10496]{2,1,0:T(8,128)(2,1)} %bitcast.28), calls=%async_computation | async-start | bytes 10747904 | tf_op jit(solution)/shard_map/all_to_all | solution.py:331
  17.6 0.1 constant_dynamic-slice_fusion.refs_5_
  17.7 1.3 collective-permute-start.2
  19.0 4.6 %collective-permute-start.1 = (bf16[512,1024]{1,0:T(8,128)(2,1)S(1)}, bf16[512,1024]{1,0:T(8,128)(2,1)S(1)}, u32[]{:S(2)}, u32[]{:S(2)}) collective-permute-start(bf16[512,1024]{1,0:T(8,128)(2,1)S(1)} %constant_dynamic-slice_fusion.refs_5_), channel_id=1, source_target_pairs={{0,2},{1,3},{2,4},{3,5},{4,6},{5,7},{8,10},{9,11},{10,12},{11,13},... | collective-permute-start | bytes 3145736 | tf_op jit(solution)/shard_map/ppermute | solution.py:258
  23.6 91.2 %collective-permute-done.2 = bf16[512,1024]{1,0:T(8,128)(2,1)S(1)} collective-permute-done((bf16[512,1024]{1,0:T(8,128)(2,1)S(1)}, bf16[512,1024]{1,0:T(8,128)(2,1)S(1)}, u32[]{:S(2)}, u32[]{:S(2)}) %collective-permute-start.2) | collective-permute-done | bytes 1048608 | tf_op jit(solution)/shard_map/ppermute | solution.py:258
  114.8 1.3 collective-permute-start.5
  116.1 16.4 %collective-permute-done.1 = bf16[512,1024]{1,0:T(8,128)(2,1)S(1)} collective-permute-done((bf16[512,1024]{1,0:T(8,128)(2,1)S(1)}, bf16[512,1024]{1,0:T(8,128)(2,1)S(1)}, u32[]{:S(2)}, u32[]{:S(2)}) %collective-permute-start.1) | collective-permute-done | bytes 1048608 | tf_op jit(solution)/shard_map/ppermute | solution.py:258
  132.5 33.0 %collective-permute-start.4 = (bf16[512,1024]{1,0:T(8,128)(2,1)S(1)}, bf16[512,1024]{1,0:T(8,128)(2,1)}, u32[]{:S(2)}, u32[]{:S(2)}) collective-permute-start(bf16[512,1024]{1,0:T(8,128)(2,1)S(1)} %collective-permute-done.1), channel_id=1, source_target_pairs={{0,2},{1,3},{2,4},{3,5},{4,6},{5,7},{8,10},{9,11},{10,12},{11,13},... | collective-permute-start | bytes 3145736 | tf_op jit(solution)/shard_map/ppermute | solution.py:258
  165.6 0.4 collective-permute-start
  166.0 19.7 %collective-permute-done.5 = bf16[512,1024]{1,0:T(8,128)(2,1)} collective-permute-done((bf16[512,1024]{1,0:T(8,128)(2,1)S(1)}, bf16[512,1024]{1,0:T(8,128)(2,1)}, u32[]{:S(2)}, u32[]{:S(2)}) %collective-permute-start.5) | collective-permute-done | bytes 1048608 | tf_op jit(solution)/shard_map/ppermute | solution.py:258
  185.7 1.3 collective-permute-start.7
  187.0 0.0 collective-permute-done.4
  187.0 5.5 %collective-permute-start.8 = (bf16[512,1024]{1,0:T(8,128)(2,1)}, bf16[512,1024]{1,0:T(8,128)(2,1)}, u32[]{:S(2)}, u32[]{:S(2)}) collective-permute-start(bf16[512,1024]{1,0:T(8,128)(2,1)} %collective-permute-done.4), channel_id=1, source_target_pairs={{0,2},{1,3},{2,4},{3,5},{4,6},{5,7},{8,10},{9,11},{10,12},{11,13},... | collective-permute-start | bytes 3145736 | tf_op jit(solution)/shard_map/ppermute | solution.py:258
  192.5 0.5 collective-permute-start.11
  193.0 1.4 broadcast_select_fusion.refs_9_
  194.5 0.0 copy-start.12
  194.5 0.5 collective-permute-start.6
  195.0 17.0 %collective-permute-done.7 = bf16[512,1024]{1,0:T(8,128)(2,1)} collective-permute-done((bf16[512,1024]{1,0:T(8,128)(2,1)}, bf16[512,1024]{1,0:T(8,128)(2,1)}, u32[]{:S(2)}, u32[]{:S(2)}) %collective-permute-start.7) | collective-permute-done | bytes 1048608 | tf_op jit(solution)/shard_map/ppermute | solution.py:258
  212.0 1.2 collective-permute-done.8
  213.2 3.0 select_select_fusion
  216.2 0.4 collective-permute-start.3
  216.6 0.0 collective-permute-done.10.refs_13_
  216.6 1.6 collective-permute-start.9
  218.2 0.0 collective-permute-start.12
  218.2 2.5 collective-permute-done.6.refs_10_
  220.7 0.6 collective-permute-start.15
  221.3 0.4 copy-done.4
  221.7 21.5 %collective-permute-done.3.refs_8_ = bf16[512,1024]{1,0:T(8,128)(2,1)} collective-permute-done((bf16[512,1024]{1,0:T(8,128)(2,1)}, bf16[512,1024]{1,0:T(8,128)(2,1)}, u32[]{:S(2)}, u32[]{:S(2)}) %collective-permute-start.3) | collective-permute-done | bytes 1048608 | tf_op jit(solution)/shard_map/ppermute | solution.py:261
  243.1 21.5 %collective-permute-done.9.refs_12_ = bf16[512,1024]{1,0:T(8,128)(2,1)S(1)} collective-permute-done((bf16[512,1024]{1,0:T(8,128)(2,1)}, bf16[512,1024]{1,0:T(8,128)(2,1)S(1)}, u32[]{:S(2)}, u32[]{:S(2)}) %collective-permute-start.9) | collective-permute-done | bytes 1048608 | tf_op jit(solution)/shard_map/ppermute | solution.py:261
  265.3 0.6 dynamic_slice.6
  265.9 1.3 concatenate.3.refs_0_
  267.3 0.2 collective-permute-done.17.refs_20_
  267.5 27.8 %user_steps.1 = (f32[2,8,72,256]{3,2,1,0:T(8,128)}, f32[2,8,72,256]{3,2,1,0:T(8,128)}) custom-call(s32[11]{0:T(128)} %concatenate.3.refs_0_, f32[1]{0:T(128)} %copy.17.refs_1_, bf16[256,10496]{1,0:T(8,128)(2,1)} %bitcast.11.refs_2_, bf16[64,8192]{1,0:T(8,128)(2,1)} %bitcast.29, bf16[64,1024]{1,0:T(8,128)(2,1)} %refs_4_.1, bf16[512,1024]{1,0:T(8,128)(2,1)} %copy-done.1, ...), custom_call_target="tpu_custom_call" | custom-call | tf_op jit(solution)/shard_map/user_steps/pallas_call | solution.py:341
  295.3 0.3 collective-permute-start.18
  295.6 2.8 collective-permute-done.18
  298.4 1.4 add.83
  299.9 0.0 copy-start.10
  299.9 0.0 copy-start.11
  299.9 1.5 collective-permute-start.19
  301.4 14.0 %collective-permute-done.19 = f32[1,8,72,256]{3,2,1,0:T(8,128)S(1)} collective-permute-done((f32[1,8,72,256]{3,2,1,0:T(8,128)S(1)}, f32[1,8,72,256]{3,2,1,0:T(8,128)S(1)}, u32[]{:S(2)}, u32[]{:S(2)}) %collective-permute-start.19) | collective-permute-done | bytes 589856 | tf_op jit(solution)/shard_map/ppermute | solution.py:367
  315.4 0.1 fusion
  315.5 18.8 %all_to_all.10 = f32[8,72,256]{2,1,0:T(8,128)S(1)} all-to-all(f32[8,72,256]{2,1,0:T(8,128)S(1)} %fusion), channel_id=1, replica_groups=mesh['grp'=4,'fsdp'=8] {'fsdp'}, dimensions={0} | all-to-all | bytes 1179648 | tf_op jit(solution)/shard_map/all_to_all | solution.py:370
  334.4 0.1 reshape.18
  334.5 0.6 fusion.1
  335.1 0.6 bitcast_add_fusion
  (37 shorter events, 0.2 us)
Async XLA Ops:
  0.6 17.0 %copy-start = (bf16[1024,1024]{1,0:T(8,128)(2,1)S(1)}, bf16[1024,1024]{1,0:T(8,128)(2,1)}, u32[]{:S(2)}) copy-start(bf16[1024,1024]{1,0:T(8,128)(2,1)} %param.16) | copy-start | bytes 6291460
  10.2 257.3 %all-to-all-start = ((bf16[32,8,10496]{2,1,0:T(8,128)(2,1)}), bf16[32,8,10496]{2,1,0:T(8,128)(2,1)}, u32[]{:S(2)}, u32[]{:S(2)}) async-start(bf16[32,8,10496]{2,1,0:T(8,128)(2,1)} %bitcast.28), calls=%async_computation | async-start | bytes 10747904 | tf_op jit(solution)/shard_map/all_to_all | solution.py:331
  17.7 198.5 %copy-start.1 = (bf16[512,1024]{1,0:T(8,128)(2,1)}, bf16[512,1024]{1,0:T(8,128)(2,1)S(1)}, u32[]{:S(2)}) copy-start(bf16[512,1024]{1,0:T(8,128)(2,1)S(1)} %constant_dynamic-slice_fusion.refs_5_) | copy-start | bytes 3145732
  17.7 97.1 %collective-permute-start.2 = (bf16[512,1024]{1,0:T(8,128)(2,1)S(1)}, bf16[512,1024]{1,0:T(8,128)(2,1)S(1)}, u32[]{:S(2)}, u32[]{:S(2)}) collective-permute-start(bf16[512,1024]{1,0:T(8,128)(2,1)S(1)} %constant_dynamic-slice_fusion.refs_5_), channel_id=1, source_target_pairs={{2,0},{3,1},{4,2},{5,3},{6,4},{7,5},{10,8},{11,9},{12,10},{13,11},... | collective-permute-start | bytes 3145736 | tf_op jit(solution)/shard_map/ppermute | solution.py:258
  19.0 113.5 %collective-permute-start.1 = (bf16[512,1024]{1,0:T(8,128)(2,1)S(1)}, bf16[512,1024]{1,0:T(8,128)(2,1)S(1)}, u32[]{:S(2)}, u32[]{:S(2)}) collective-permute-start(bf16[512,1024]{1,0:T(8,128)(2,1)S(1)} %constant_dynamic-slice_fusion.refs_5_), channel_id=1, source_target_pairs={{0,2},{1,3},{2,4},{3,5},{4,6},{5,7},{8,10},{9,11},{10,12},{11,13},... | collective-permute-start | bytes 3145736 | tf_op jit(solution)/shard_map/ppermute | solution.py:258
  114.8 72.1 %copy-start.6 = (bf16[512,1024]{1,0:T(8,128)(2,1)}, bf16[512,1024]{1,0:T(8,128)(2,1)S(1)}, u32[]{:S(2)}) copy-start(bf16[512,1024]{1,0:T(8,128)(2,1)S(1)} %collective-permute-done.2) | copy-start | bytes 3145732
  114.8 70.8 %collective-permute-start.5 = (bf16[512,1024]{1,0:T(8,128)(2,1)S(1)}, bf16[512,1024]{1,0:T(8,128)(2,1)}, u32[]{:S(2)}, u32[]{:S(2)}) collective-permute-start(bf16[512,1024]{1,0:T(8,128)(2,1)S(1)} %collective-permute-done.2), channel_id=1, source_target_pairs={{2,0},{3,1},{4,2},{5,3},{6,4},{7,5},{10,8},{11,9},{12,10},{13,11},... | collective-permute-start | bytes 3145736 | tf_op jit(solution)/shard_map/ppermute | solution.py:258
  132.5 60.0 %copy-start.8 = (bf16[512,1024]{1,0:T(8,128)(2,1)}, bf16[512,1024]{1,0:T(8,128)(2,1)S(1)}, u32[]{:S(2)}) copy-start(bf16[512,1024]{1,0:T(8,128)(2,1)S(1)} %collective-permute-done.1) | copy-start | bytes 3145732
  132.5 54.4 %collective-permute-start.4 = (bf16[512,1024]{1,0:T(8,128)(2,1)S(1)}, bf16[512,1024]{1,0:T(8,128)(2,1)}, u32[]{:S(2)}, u32[]{:S(2)}) collective-permute-start(bf16[512,1024]{1,0:T(8,128)(2,1)S(1)} %collective-permute-done.1), channel_id=1, source_target_pairs={{0,2},{1,3},{2,4},{3,5},{4,6},{5,7},{8,10},{9,11},{10,12},{11,13},... | collective-permute-start | bytes 3145736 | tf_op jit(solution)/shard_map/ppermute | solution.py:258
  165.6 27.0 %collective-permute-start = (bf16[512,1024]{1,0:T(8,128)(2,1)S(1)}, bf16[512,1024]{1,0:T(8,128)(2,1)}, u32[]{:S(2)}, u32[]{:S(2)}) collective-permute-start(bf16[512,1024]{1,0:T(8,128)(2,1)S(1)} %constant_dynamic-slice_fusion.refs_5_), channel_id=1, source_target_pairs={{0,1},{1,0},{2,3},{3,2},{4,5},{5,4},{6,7},{7,6},{8,9},{9,8},{10,11... | collective-permute-start | bytes 3145736 | tf_op jit(solution)/shard_map/ppermute | solution.py:261
  185.7 26.3 %collective-permute-start.7 = (bf16[512,1024]{1,0:T(8,128)(2,1)}, bf16[512,1024]{1,0:T(8,128)(2,1)}, u32[]{:S(2)}, u32[]{:S(2)}) collective-permute-start(bf16[512,1024]{1,0:T(8,128)(2,1)} %collective-permute-done.5), channel_id=1, source_target_pairs={{2,0},{3,1},{4,2},{5,3},{6,4},{7,5},{10,8},{11,9},{12,10},{13,11},... | collective-permute-start | bytes 3145736 | tf_op jit(solution)/shard_map/ppermute | solution.py:258
  187.0 26.2 %collective-permute-start.8 = (bf16[512,1024]{1,0:T(8,128)(2,1)}, bf16[512,1024]{1,0:T(8,128)(2,1)}, u32[]{:S(2)}, u32[]{:S(2)}) collective-permute-start(bf16[512,1024]{1,0:T(8,128)(2,1)} %collective-permute-done.4), channel_id=1, source_target_pairs={{0,2},{1,3},{2,4},{3,5},{4,6},{5,7},{8,10},{9,11},{10,12},{11,13},... | collective-permute-start | bytes 3145736 | tf_op jit(solution)/shard_map/ppermute | solution.py:258
  192.5 24.1 %collective-permute-start.10 = (bf16[512,1024]{1,0:T(8,128)(2,1)S(1)}, bf16[512,1024]{1,0:T(8,128)(2,1)}, u32[]{:S(2)}, u32[]{:S(2)}) collective-permute-start(bf16[512,1024]{1,0:T(8,128)(2,1)S(1)} %constant_dynamic-slice_fusion.refs_5_), channel_id=1, source_target_pairs={{0,8},{8,0},{16,24},{24,16},{1,9},{9,1},{17,25},{25,17},{2,10},{10... | collective-permute-start | bytes 3145736 | tf_op jit(solution)/shard_map/ppermute | solution.py:320
  192.5 20.7 %copy-start.7 = (bf16[512,1024]{1,0:T(8,128)(2,1)S(1)}, bf16[512,1024]{1,0:T(8,128)(2,1)}, u32[]{:S(2)}) copy-start(bf16[512,1024]{1,0:T(8,128)(2,1)} %copy-done.6) | copy-start | bytes 3145732
  192.5 20.7 %copy-start.9 = (bf16[512,1024]{1,0:T(8,128)(2,1)S(1)}, bf16[512,1024]{1,0:T(8,128)(2,1)}, u32[]{:S(2)}) copy-start(bf16[512,1024]{1,0:T(8,128)(2,1)} %copy-done.8) | copy-start | bytes 3145732
  192.5 25.7 %collective-permute-start.11 = (bf16[512,1024]{1,0:T(8,128)(2,1)}, bf16[512,1024]{1,0:T(8,128)(2,1)S(1)}, u32[]{:S(2)}, u32[]{:S(2)}) collective-permute-start(bf16[512,1024]{1,0:T(8,128)(2,1)} %collective-permute-done.refs_6_), channel_id=1, source_target_pairs={{0,8},{8,0},{16,24},{24,16},{1,9},{9,1},{17,25},{25,17},{2,10},{10... | collective-permute-start | bytes 3145736 | tf_op jit(solution)/shard_map/ppermute | solution.py:320
  194.5 21.7 %copy-start.2 = (bf16[512,1024]{1,0:T(8,128)(2,1)}, bf16[512,1024]{1,0:T(8,128)(2,1)S(1)}, u32[]{:S(2)}) copy-start(bf16[512,1024]{1,0:T(8,128)(2,1)S(1)} %broadcast_select_fusion.refs_9_) | copy-start | bytes 3145732
  194.5 70.8 %copy-start.12 = (s32[32]{0:T(128)S(1)}, s32[32]{0:T(128)}, u32[]{:S(2)}) copy-start(s32[32]{0:T(128)} %param.15) | copy-start | bytes 388
  194.5 26.2 %collective-permute-start.6 = (bf16[512,1024]{1,0:T(8,128)(2,1)S(1)}, bf16[512,1024]{1,0:T(8,128)(2,1)}, u32[]{:S(2)}, u32[]{:S(2)}) collective-permute-start(bf16[512,1024]{1,0:T(8,128)(2,1)S(1)} %broadcast_select_fusion.refs_9_), channel_id=1, source_target_pairs={{0,1},{1,0},{2,3},{3,2},{4,5},{5,4},{6,7},{7,6},{8,9},{9,8},{10,11... | collective-permute-start | bytes 3145736 | tf_op jit(solution)/shard_map/ppermute | solution.py:261
  212.0 8.7 %collective-permute-start.14 = (bf16[512,1024]{1,0:T(8,128)(2,1)S(1)}, bf16[512,1024]{1,0:T(8,128)(2,1)S(1)}, u32[]{:S(2)}, u32[]{:S(2)}) collective-permute-start(bf16[512,1024]{1,0:T(8,128)(2,1)S(1)} %broadcast_select_fusion.refs_9_), channel_id=1, source_target_pairs={{0,8},{8,0},{16,24},{24,16},{1,9},{9,1},{17,25},{25,17},{2,10},{10... | collective-permute-start | bytes 3145736 | tf_op jit(solution)/shard_map/ppermute | solution.py:320
  216.2 27.0 %collective-permute-start.3 = (bf16[512,1024]{1,0:T(8,128)(2,1)}, bf16[512,1024]{1,0:T(8,128)(2,1)}, u32[]{:S(2)}, u32[]{:S(2)}) collective-permute-start(bf16[512,1024]{1,0:T(8,128)(2,1)} %get-tuple-element.7.refs_7_), channel_id=1, source_target_pairs={{0,1},{1,0},{2,3},{3,2},{4,5},{5,4},{6,7},{7,6},{8,9},{9,8},{10,11... | collective-permute-start | bytes 3145736 | tf_op jit(solution)/shard_map/ppermute | solution.py:261
  216.6 48.1 %collective-permute-start.9 = (bf16[512,1024]{1,0:T(8,128)(2,1)}, bf16[512,1024]{1,0:T(8,128)(2,1)S(1)}, u32[]{:S(2)}, u32[]{:S(2)}) collective-permute-start(bf16[512,1024]{1,0:T(8,128)(2,1)} %get-tuple-element.6.refs_11_), channel_id=1, source_target_pairs={{0,1},{1,0},{2,3},{3,2},{4,5},{5,4},{6,7},{7,6},{8,9},{9,8},{10,11... | collective-permute-start | bytes 3145736 | tf_op jit(solution)/shard_map/ppermute | solution.py:261
  218.2 2.5 copy-start.3
  218.2 49.0 %collective-permute-start.12 = (bf16[512,1024]{1,0:T(8,128)(2,1)}, bf16[512,1024]{1,0:T(8,128)(2,1)}, u32[]{:S(2)}, u32[]{:S(2)}) collective-permute-start(bf16[512,1024]{1,0:T(8,128)(2,1)} %get-tuple-element.7.refs_7_), channel_id=1, source_target_pairs={{0,8},{8,0},{16,24},{24,16},{1,9},{9,1},{17,25},{25,17},{2,10},{10... | collective-permute-start | bytes 3145736 | tf_op jit(solution)/shard_map/ppermute | solution.py:320
  220.7 46.6 %collective-permute-start.16 = (bf16[512,1024]{1,0:T(8,128)(2,1)}, bf16[512,1024]{1,0:T(8,128)(2,1)}, u32[]{:S(2)}, u32[]{:S(2)}) collective-permute-start(bf16[512,1024]{1,0:T(8,128)(2,1)} %get-tuple-element.6.refs_11_), channel_id=1, source_target_pairs={{0,8},{8,0},{16,24},{24,16},{1,9},{9,1},{17,25},{25,17},{2,10},{10... | collective-permute-start | bytes 3145736 | tf_op jit(solution)/shard_map/ppermute | solution.py:320
  220.7 1.0 copy-start.4
  220.7 46.6 %collective-permute-start.15 = (bf16[512,1024]{1,0:T(8,128)(2,1)}, bf16[512,1024]{1,0:T(8,128)(2,1)}, u32[]{:S(2)}, u32[]{:S(2)}) collective-permute-start(bf16[512,1024]{1,0:T(8,128)(2,1)} %collective-permute-done.6.refs_10_), channel_id=1, source_target_pairs={{0,8},{8,0},{16,24},{24,16},{1,9},{9,1},{17,25},{25,17},{2,10},{10... | collective-permute-start | bytes 3145736 | tf_op jit(solution)/shard_map/ppermute | solution.py:320
  243.1 24.1 %collective-permute-start.13 = (bf16[512,1024]{1,0:T(8,128)(2,1)}, bf16[512,1024]{1,0:T(8,128)(2,1)}, u32[]{:S(2)}, u32[]{:S(2)}) collective-permute-start(bf16[512,1024]{1,0:T(8,128)(2,1)} %collective-permute-done.3.refs_8_), channel_id=1, source_target_pairs={{0,8},{8,0},{16,24},{24,16},{1,9},{9,1},{17,25},{25,17},{2,10},{10... | collective-permute-start | bytes 3145736 | tf_op jit(solution)/shard_map/ppermute | solution.py:320
  264.7 2.8 copy-start.5
  264.7 2.8 collective-permute-start.17
  295.3 3.1 collective-permute-start.18
  299.9 34.6 %copy-start.10 = (f32[256,64]{0,1:T(8,128)S(1)}, f32[256,64]{0,1:T(8,128)}, u32[]{:S(2)}) copy-start(f32[256,64]{0,1:T(8,128)} %param.20) | copy-start | bytes 196612
  299.9 35.2 %copy-start.11 = (f32[64,32]{0,1:T(8,128)S(1)}, f32[64,32]{0,1:T(8,128)}, u32[]{:S(2)}) copy-start(f32[64,32]{0,1:T(8,128)} %param.21) | copy-start | bytes 24580
  299.9 15.5 %collective-permute-start.19 = (f32[1,8,72,256]{3,2,1,0:T(8,128)S(1)}, f32[1,8,72,256]{3,2,1,0:T(8,128)S(1)}, u32[]{:S(2)}, u32[]{:S(2)}) collective-permute-start(f32[1,8,72,256]{3,2,1,0:T(8,128)S(1)} %slice.17), channel_id=1, source_target_pairs={{0,16},{8,24},{16,0},{24,8},{1,17},{9,25},{17,1},{25,9},{2,18},{10... | collective-permute-start | bytes 1769480 | tf_op jit(solution)/shard_map/ppermute | solution.py:367

commit v3 on v2

--- a/solution.py
+++ b/solution.py
@@ -77,11 +77,11 @@
     up_ref,
     *refs,
 ):
-    shards = members
-    near_refs, far_refs = (refs[:shards], refs[shards : 2 * shards])
     (
-        keep_ref,
-        send_ref,
+        near_ref,
+        far_ref,
+        keep_refs,
+        send_refs,
         x_ref,
         goal_ref,
         cut_ref,
@@ -93,12 +93,12 @@
         delta_ref,
         got_sem,
         w_sem,
-    ) = refs[2 * shards :]
+    ) = refs[:2] + (refs[2:4], refs[4:6]) + refs[6:]
     groups, rest = divmod(most, SUB)
     rank, width = down_ref.shape
     kv_width = up_ref.shape[1]
     whole = devices * SUB
-    half = near_refs[0].shape[0]
+    shards, half, unused = near_ref.shape
     copies = []
     column = 0
     for full, cut in ((x_ref, cut_ref), (goal_ref, cut_goal_ref)):
@@ -119,11 +119,19 @@
     for copy in copies:
         copy.start()
 
-    for place in range(shards):
-        for at, source in enumerate((near_refs[place], far_refs[place])):
-            pltpu.make_async_copy(source, w_ref.at[at, place], w_sem.at[at, place]).start()
+    def weight_copy(at, place):
+        source = (near_ref, far_ref)[at].at[place]
+        return pltpu.make_async_copy(source, w_ref.at[at, place], w_sem.at[at, place])
+
+    ahead = min(2, shards)
+    for place in range(ahead):
+        weight_copy(0, place).start()
+        weight_copy(1, place).start()
     for copy in copies:
         copy.wait()
+    for place in range(ahead, shards):
+        weight_copy(0, place).start()
+        weight_copy(1, place).start()
 
     line, other = (iota((devices, whole), 0), iota((devices, whole), 1))
     for extra in range(rest):
@@ -161,10 +169,9 @@
     side = where_ref[1]
 
     def add_shard(place, unused):
-        for at in range(2):
-            block = w_ref.at[at, place]
-            pltpu.make_async_copy(block, block, w_sem.at[at, place]).wait()
-        shard = where_ref[3 + place]
+        weight_copy(0, place).wait()
+        weight_copy(1, place).wait()
+        shard = where_ref[4 + place]
         near = pl.ds(pl.multiple_of((2 * shard + side) * half, half), half)
         far = pl.ds(pl.multiple_of((2 * shard + 1 - side) * half, half), half)
         near_x, far_x = (x_ref[:, near], x_ref[:, far])
@@ -216,18 +223,22 @@
     pieces = share // rank
     tall = up_share // pieces
 
-    def write(core, target):
+    def write(core, targets):
+        edge = targets[0].shape[3]
         for pair in range(devices // members // 2):
             for member in range(members):
                 device = (2 * pair + core) * members + member
                 spot = lax.bitwise_xor(where_ref[2], pair)
-                moved = delta_ref[:, device * share : (device + 1) * share]
-                target[spot, member, :rank, :] = factor * moved
+                inner = lax.bitwise_xor(where_ref[3], member % 2)
+                outer = member // 2
+                moved = factor * delta_ref[:, device * share : (device + 1) * share]
+                targets[0][spot, inner, outer] = moved[:edge]
+                targets[1][spot, inner, outer, : rank - edge, :] = moved[edge:]
                 first = device * up_share
                 parts = [
                     up_turned[first + at * tall : first + (at + 1) * tall] for at in range(pieces)
                 ]
-                target[spot, member, rank:, :] = (
+                targets[1][spot, inner, outer, rank - edge :, :] = (
                     jnp.concatenate(parts, axis=1) if pieces > 1 else parts[0]
                 )
 
@@ -236,53 +247,22 @@
 
         @pl.when(mine)
         def _():
-            write(core, keep_ref)
+            write(core, keep_refs)
 
         @pl.when(jnp.logical_not(mine))
         def _():
-            write(core, send_ref)
-
-
-def gather_weight(mine, members):
-    line = members // 2
-    index = lax.axis_index("fsdp")
-    spot, inner = (index // 2, index % 2)
-
-    def hop(value, way):
-        pairs = [
-            (2 * at + one, 2 * (at + way) + one)
-            for at in range(line)
-            for one in range(2)
-            if 0 <= at + way < line
-        ]
-        return lax.ppermute(value, "fsdp", pairs)
-
-    def across(value):
-        return lax.ppermute(value, "fsdp", [(at, at ^ 1) for at in range(members)])
-
-    blocks = [(mine, spot)]
-    ups, downs = ({0: mine}, {0: mine})
-    for step in range(1, line):
-        ups[step] = hop(ups[step - 1], 1)
-        downs[step] = hop(downs[step - 1], -1)
-    for step in range(1, line // 2 + 1):
-        above = spot >= step
-        blocks.append(
-            (jnp.where(above, ups[step], downs[step]), jnp.where(above, spot - step, spot + step))
-        )
-    for step in range(1, line // 2):
-        both = (spot >= step) & (spot < line - step)
-        late = line - step
-        value = jnp.where(both, downs[step], jnp.where(spot < step, downs[late], ups[late]))
-        number = jnp.where(
-            both, spot + step, jnp.where(spot < step, spot + late, spot - late)
-        )
-        blocks.append((value, number))
-    values, numbers = ([], [])
-    for value, number in blocks:
-        values += [value, across(value)]
-        numbers += [2 * number + inner, 2 * number + 1 - inner]
-    return values, jnp.stack(numbers).astype(jnp.int32)
+            write(core, send_refs)
+
+
+def halve(package, axis, bits, partner):
+    bit = package.shape[bits] // 2
+    while bit:
+        keep = lax.slice_in_dim(package, 0, bit, axis=bits)
+        send = lax.slice_in_dim(package, bit, 2 * bit, axis=bits)
+        pairs = [(at, at ^ (partner * bit)) for at in range(lax.axis_size(axis))]
+        package = lax.ppermute(send, axis, pairs) + keep
+        bit //= 2
+    return package
 
 
 def body(
@@ -316,8 +296,10 @@
 
     half = value_weight.shape[0] // 2
     mine = lax.dynamic_slice_in_dim(value_weight, side * half, half, axis=0)
-    near, numbers = gather_weight(mine, members)
-    far = [lax.ppermute(block, "grp", [(at, at ^ 1) for at in range(groups)]) for block in near]
+    path = list(range(0, members, 2)) + list(range(1, members, 2))[::-1]
+    near = lax.all_gather(mine, "fsdp", axis=0, axis_index_groups=[path])
+    swap = [(at, at ^ 1) for at in range(groups)]
+    far = lax.ppermute(near, "grp", swap)
 
     columns = whole_groups * (width + kv_width) + rest * (width + kv_width) // SUB + LANES
     packed = pl.pallas_call(
@@ -328,21 +310,25 @@
         compiler_params=pltpu.CompilerParams(vmem_limit_bytes=VMEM_BYTES),
         name="pack_rows",
     )(device_row_count, row_owner_user, tokens, targets)
+    cap = lax.dynamic_slice_in_dim(user_row_cap, myself, 1)
+    pair = lax.axis_index("grp") // 2
+    inner = lax.axis_index("fsdp") % 2
+    spots = jnp.stack([side, pair, inner] + [jnp.int32(place) for place in path])
+    where = jnp.concatenate([cap, spots.astype(jnp.int32)])
+    packed, where = lax.optimization_barrier((packed, where))
     got = lax.all_to_all(
         packed.reshape(users, SUB, columns), BOTH, split_axis=0, concat_axis=0, tiled=True
     ).reshape(whole, columns)
-
-    cap = lax.dynamic_slice_in_dim(user_row_cap, myself, 1)
-    pair = lax.axis_index("grp") // 2
-    where = jnp.concatenate([cap, jnp.stack([side, pair]).astype(jnp.int32), numbers])
     share = width // devices
     tall = rank + kv_width // devices * rank // share
-    package = jax.ShapeDtypeStruct((groups // 2, members, tall, share), F32)
-    keep, send = pl.pallas_call(
+    edge = tall // (2 * SUB) * SUB
+    grid = (groups // 2, 2, members // 2)
+    streams = [jax.ShapeDtypeStruct(grid + (size, share), F32) for size in (edge, tall - edge)]
+    kept_y, kept_x, sent_y, sent_x = pl.pallas_call(
         lambda *refs: user_kernel(devices, members, most, *refs),
-        out_shape=[package] * 2,
-        in_specs=[smem, smem, anywhere, vmem, vmem] + [anywhere] * (2 * members),
-        out_specs=[vmem] * 2,
+        out_shape=streams * 2,
+        in_specs=[smem, smem, anywhere, vmem, vmem, anywhere, anywhere],
+        out_specs=[vmem] * 4,
         scratch_shapes=[
             pltpu.VMEM((slots, width), BF16),
             pltpu.VMEM((slots, kv_width), BF16),
@@ -358,16 +344,17 @@
         ],
         compiler_params=pltpu.CompilerParams(vmem_limit_bytes=VMEM_BYTES),
         name="user_steps",
-    )(where, clip_norm_bound, got, adapter_down.T, adapter_up, *near, *far)
-
-    package = keep + lax.ppermute(send, "grp", [(at, at ^ 1) for at in range(groups)])
-    bit = groups // 4
-    while bit:
-        partner = [(at, at ^ (2 * bit)) for at in range(groups)]
-        package = package[:bit] + lax.ppermute(package[bit:], "grp", partner)
-        bit //= 2
-    package = package[0]
-    package = lax.all_to_all(package, "fsdp", split_axis=0, concat_axis=0, tiled=True)
+    )(where, clip_norm_bound, got, adapter_down.T, adapter_up, near, far)
+
+    first = kept_y + lax.ppermute(sent_y, "grp", swap)
+    second = kept_x + lax.ppermute(sent_x, "grp", swap)
+    first = halve(halve(first, "grp", 0, 2), "fsdp", 1, 1)
+    second = halve(halve(second, "fsdp", 1, 1), "grp", 0, 2)
+    package = jnp.concatenate([first[0, 0], second[0, 0]], axis=1)
+    lines = [list(range(one, members, 2)) for one in range(2)]
+    package = lax.all_to_all(
+        package, "fsdp", split_axis=0, concat_axis=0, axis_index_groups=lines, tiled=True
+    )
     package = jnp.sum(package, axis=0)
     clip = clip_norm_bound[0]
     update_a = package[:rank].T + clip * down_noise

time: 336 us -> 294 us (0.88)
  starting transfers between devices: 60.2 us -> 13 us
  between operations: 2.33 us -> 15.5 us
  Pallas kernels: 35.1 us -> 31.4 us
  other arithmetic: 7.22 us -> 3.7 us
    ppermute x20 -> x7, waiting for transfers between devices: 208 us -> 26.9 us  [the longest x1 12.8 us: body(): far = lax.ppermute(near, 'grp', swap)]
    all_gather x0 -> x1, waiting for transfers between devices: none -> 179 us  [body(): near = lax.all_gather(mine, 'fsdp', axis=0, axis_index_groups=[path])]
    ppermute x20 -> x7, starting transfers between devices: 52.8 us -> 5.6 us  [the longest x4 5.02 us: halve(): package = lax.ppermute(send, axis, pairs) + keep]
    select_n x2 -> x0, other arithmetic: 4.43 us -> none  [the longest x1 2.98 us: gather_weight(): jnp.where(both, downs[step], jnp.where(spot < step, downs[late], ups[late]))]
    pallas_call x1, Pallas kernels: 27.8 us -> 24.1 us  [body(): pl.pallas_call(lambda *refs: user_kernel(devices, members, most, *refs),...]
  transfers between devices with their start and end apart: 21 -> 9, of which waited for: 11 -> 7; matrix products, arithmetic and copies ran while one was open for 2% -> 2% of each run, Pallas kernels for 0% -> 2%
where the time goes in v3:
time: 294 us
  waiting for transfers between devices  206 us (70%)
  Pallas kernels  31.4 us (11%)
  blocking collectives  17.1 us (6%)
  between operations  15.5 us (5%)
  starting transfers between devices  13 us (4%)
  local copies, waits for them, and re-layouts  6.77 us (2%)
  other arithmetic  3.7 us (1%)
    all_gather x1, waiting for transfers between devices, body(): near = lax.all_gather(mine, 'fsdp', axis=0, axis_index_groups=[path])  179 us
    pallas_call x1, Pallas kernels, body(): pl.pallas_call(lambda *refs: user_kernel(devices, members, most, *refs),...  24.1 us
    all_to_all x1, blocking collectives, body(): lax.all_to_all(package, 'fsdp', split_axis=0, concat_axis=0, axis_index_g...  17.1 us
    ppermute x1, waiting for transfers between devices, body(): far = lax.ppermute(near, 'grp', swap)  12.8 us
    ppermute x4, waiting for transfers between devices, halve(): package = lax.ppermute(send, axis, pairs) + keep  12.5 us
    all_to_all x1, starting transfers between devices, body(): lax.all_to_all(packed.reshape(users, SUB, columns), BOTH, split_axis=0, c...  7.41 us
    pallas_call x1, Pallas kernels, body(): pl.pallas_call(lambda *refs: pack_kernel(users, most, *refs), out_shape=j...  7.25 us
  transfers between devices with their start and end apart: 9, of which 7 were waited for; matrix products, arithmetic and copies ran while one was open for 2% of the time, Pallas kernels for 2%

profile of v3, /device:TPU:0, one launch (start us, length us, event | category | flops | bytes accessed | tf_op | source)
XLA Modules:
  0.0 293.6 jit_solution(1419667753688903194)
XLA Ops:
  7.2 0.0 copy-start
  7.2 0.0 all-gather.3.cloned.1.call-start
  7.2 1.5 copy-done
  8.8 1.1 constant_dynamic-slice_fusion
  9.9 0.0 all-gather.3.cloned.1.call-update
  10.6 1.4 copy.13.refs_1_
  12.0 1.2 dynamic_slice.6
  13.3 7.3 %pack_rows.1 = bf16[256,10496]{1,0:T(8,128)(2,1)} custom-call(s32[1]{0:T(128)S(6)} %copy.16.refs_0_, s32[192,1]{1,0:T(8,128)} %copy.13.refs_1_, bf16[192,8192]{1,0:T(8,128)(2,1)} %refs_2_.1, bf16[192,1024]{1,0:T(8,128)(2,1)} %refs_3_.1), custom_call_target="tpu_custom_call" | custom-call | tf_op jit(solution)/shard_map/pack_rows/pallas_call | solution.py:305
  20.5 1.3 concatenate.6.refs_0_
  21.8 7.4 %all-to-all-start = ((bf16[32,8,10496]{2,1,0:T(8,128)(2,1)}), bf16[32,8,10496]{2,1,0:T(8,128)(2,1)}, u32[]{:S(2)}, u32[]{:S(2)}) async-start(bf16[32,8,10496]{2,1,0:T(8,128)(2,1)} %bitcast.24), calls=%async_computation | async-start | bytes 10747904 | tf_op jit(solution)/shard_map/all_to_all | solution.py:319
  29.2 179.1 %all-gather.3.cloned.1.call-done = bf16[4096,1024]{1,0:T(8,128)(2,1)} async-done(((bf16[512,1024]{1,0:T(8,128)(2,1)}), bf16[4096,1024]{1,0:T(8,128)(2,1)}) %all-gather.3.cloned.1.call-update) | async-done | bytes 8388624 | tf_op jit(solution)/shard_map/all_gather | solution.py:300
  208.3 0.0 collective-permute-start
  209.0 0.0 all-to-all-done
  209.0 12.8 %collective-permute-done.refs_6_ = bf16[8,512,1024]{2,1,0:T(8,128)(2,1)} collective-permute-done((bf16[8,512,1024]{2,1,0:T(8,128)(2,1)}, bf16[8,512,1024]{2,1,0:T(8,128)(2,1)}, u32[]{:S(2)}, u32[]{:S(2)}) %collective-permute-start) | collective-permute-done | bytes 8388640 | tf_op jit(solution)/shard_map/ppermute | solution.py:302
  221.8 24.1 %user_steps.1 = (f32[2,2,4,32,256]{4,3,2,1,0:T(8,128)}, f32[2,2,4,40,256]{4,3,2,1,0:T(8,128)}, f32[2,2,4,32,256]{4,3,2,1,0:T(8,128)}, f32[2,2,4,40,256]{4,3,2,1,0:T(8,128)}) custom-call(s32[12]{0:T(128)} %concatenate.6.refs_0_, f32[1]{0:T(128)} %copy.17.refs_1_, bf16[256,10496]{1,0:T(8,128)(2,1)} %bitcast.4.refs_2_, bf16[64,8192]{1,0:T(8,128)(2,1)} %bitcast.27, ...), custom_call_target="tpu_custom_call" | custom-call | tf_op jit(solution)/shard_map/user_steps/pallas_call | solution.py:327
  246.0 0.0 copy-start.1
  246.0 0.0 copy-start.2
  246.0 0.1 collective-permute-start.1
  246.1 0.5 collective-permute-start.4
  246.6 1.6 collective-permute-done.1
  248.2 1.1 add.46
  249.3 1.5 collective-permute-start.2
  250.9 0.0 collective-permute-done.4
  250.9 1.2 add.49
  252.1 1.6 collective-permute-start.5
  253.7 4.0 %collective-permute-done.2 = f32[1,2,4,32,256]{4,3,2,1,0:T(8,128)S(1)} collective-permute-done((f32[1,2,4,32,256]{4,3,2,1,0:T(8,128)S(1)}, f32[1,2,4,32,256]{4,3,2,1,0:T(8,128)S(1)}, u32[]{:S(2)}, u32[]{:S(2)}) %collective-permute-start.2) | collective-permute-done | bytes 262176 | tf_op jit(solution)/shard_map/ppermute | solution.py:263
  257.8 1.5 collective-permute-start.3
  259.3 3.4 %collective-permute-done.5 = f32[2,1,4,40,256]{4,3,2,1,0:T(8,128)S(1)} collective-permute-done((f32[2,1,4,40,256]{4,3,2,1,0:T(8,128)S(1)}, f32[2,1,4,40,256]{4,3,2,1,0:T(8,128)S(1)}, u32[]{:S(2)}, u32[]{:S(2)}) %collective-permute-start.5) | collective-permute-done | bytes 327712 | tf_op jit(solution)/shard_map/ppermute | solution.py:263
  262.8 0.4 collective-permute-start.6
  263.2 1.3 collective-permute-done.3
  264.5 3.7 %collective-permute-done.6 = f32[1,1,4,40,256]{4,3,2,1,0:T(8,128)S(1)} collective-permute-done((f32[1,1,4,40,256]{4,3,2,1,0:T(8,128)S(1)}, f32[1,1,4,40,256]{4,3,2,1,0:T(8,128)S(1)}, u32[]{:S(2)}, u32[]{:S(2)}) %collective-permute-start.6) | collective-permute-done | bytes 163872 | tf_op jit(solution)/shard_map/ppermute | solution.py:263
  268.3 17.1 %all_to_all.10 = f32[4,72,256]{2,1,0:T(8,128)S(1)} all-to-all(f32[4,72,256]{2,1,0:T(8,128)S(1)} %pad_maximum_fusion), channel_id=1, replica_groups={{0,2,4,6},{1,3,5,7},{8,10,12,14},{9,11,13,15},{16,18,20,22},{17,19,21,2..., dimensions={0} | all-to-all | bytes 589824 | tf_op jit(solution)/shard_map/all_to_all | solution.py:355
  285.4 0.1 reshape.18
  285.5 0.0 copy-done.1
  285.5 0.6 fusion.2
  286.2 0.0 copy-done.2
  286.2 0.6 bitcast_add_fusion
  (11 shorter events, 0.2 us)
Async XLA Ops:
  7.2 1.6 copy-start
  7.2 201.2 %all-gather.3.cloned.1.call-start = ((), (), s32[]{:S(2)}) async-start(), calls=%async_computation.2 | async-start | bytes 9437184 | tf_op jit(solution)/shard_map/all_gather | solution.py:300
  21.8 187.2 %all-to-all-start = ((bf16[32,8,10496]{2,1,0:T(8,128)(2,1)}), bf16[32,8,10496]{2,1,0:T(8,128)(2,1)}, u32[]{:S(2)}, u32[]{:S(2)}) async-start(bf16[32,8,10496]{2,1,0:T(8,128)(2,1)} %bitcast.24), calls=%async_computation | async-start | bytes 10747904 | tf_op jit(solution)/shard_map/all_to_all | solution.py:319
  208.3 13.5 %collective-permute-start = (bf16[8,512,1024]{2,1,0:T(8,128)(2,1)}, bf16[8,512,1024]{2,1,0:T(8,128)(2,1)}, u32[]{:S(2)}, u32[]{:S(2)}) collective-permute-start(bf16[8,512,1024]{2,1,0:T(8,128)(2,1)} %bitcast.25), channel_id=1, source_target_pairs={{0,8},{8,0},{16,24},{24,16},{1,9},{9,1},{17,25},{25,17},{2,10},{10... | collective-permute-start | bytes 25165832 | tf_op jit(solution)/shard_map/ppermute | solution.py:302
  246.0 39.5 %copy-start.1 = (f32[256,64]{0,1:T(8,128)S(1)}, f32[256,64]{0,1:T(8,128)}, u32[]{:S(2)}) copy-start(f32[256,64]{0,1:T(8,128)} %param.20) | copy-start | bytes 196612
  246.0 40.2 %copy-start.2 = (f32[64,32]{0,1:T(8,128)S(1)}, f32[64,32]{0,1:T(8,128)}, u32[]{:S(2)}) copy-start(f32[64,32]{0,1:T(8,128)} %param.21) | copy-start | bytes 24580
  246.0 2.2 collective-permute-start.1
  246.1 4.8 %collective-permute-start.4 = (f32[2,2,4,40,256]{4,3,2,1,0:T(8,128)}, f32[2,2,4,40,256]{4,3,2,1,0:T(8,128)S(1)}, u32[]{:S(2)}, u32[]{:S(2)}) collective-permute-start(f32[2,2,4,40,256]{4,3,2,1,0:T(8,128)} %get-tuple-element.13), channel_id=1, source_target_pairs={{0,8},{8,0},{16,24},{24,16},{1,9},{9,1},{17,25},{25,17},{2,10},{10... | collective-permute-start | bytes 1966088 | tf_op jit(solution)/shard_map/ppermute | solution.py:350
  249.3 8.4 %collective-permute-start.2 = (f32[1,2,4,32,256]{4,3,2,1,0:T(8,128)S(1)}, f32[1,2,4,32,256]{4,3,2,1,0:T(8,128)S(1)}, u32[]{:S(2)}, u32[]{:S(2)}) collective-permute-start(f32[1,2,4,32,256]{4,3,2,1,0:T(8,128)S(1)} %slice.40), channel_id=1, source_target_pairs={{0,16},{8,24},{16,0},{24,8},{1,17},{9,25},{17,1},{25,9},{2,18},{10... | collective-permute-start | bytes 786440 | tf_op jit(solution)/shard_map/ppermute | solution.py:263
  252.1 10.7 %collective-permute-start.5 = (f32[2,1,4,40,256]{4,3,2,1,0:T(8,128)S(1)}, f32[2,1,4,40,256]{4,3,2,1,0:T(8,128)S(1)}, u32[]{:S(2)}, u32[]{:S(2)}) collective-permute-start(f32[2,1,4,40,256]{4,3,2,1,0:T(8,128)S(1)} %slice.44), channel_id=1, source_target_pairs={{0,1},{1,0},{2,3},{3,2},{4,5},{5,4},{6,7},{7,6},{8,9},{9,8},{10,11... | collective-permute-start | bytes 983048 | tf_op jit(solution)/shard_map/ppermute | solution.py:263
  257.8 6.6 %collective-permute-start.3 = (f32[1,1,4,32,256]{4,3,2,1,0:T(8,128)S(1)}, f32[1,1,4,32,256]{4,3,2,1,0:T(8,128)S(1)}, u32[]{:S(2)}, u32[]{:S(2)}) collective-permute-start(f32[1,1,4,32,256]{4,3,2,1,0:T(8,128)S(1)} %slice.42), channel_id=1, source_target_pairs={{0,1},{1,0},{2,3},{3,2},{4,5},{5,4},{6,7},{7,6},{8,9},{9,8},{10,11... | collective-permute-start | bytes 393224 | tf_op jit(solution)/shard_map/ppermute | solution.py:263
  262.8 5.4 %collective-permute-start.6 = (f32[1,1,4,40,256]{4,3,2,1,0:T(8,128)S(1)}, f32[1,1,4,40,256]{4,3,2,1,0:T(8,128)S(1)}, u32[]{:S(2)}, u32[]{:S(2)}) collective-permute-start(f32[1,1,4,40,256]{4,3,2,1,0:T(8,128)S(1)} %slice.46), channel_id=1, source_target_pairs={{0,16},{8,24},{16,0},{24,8},{1,17},{9,25},{17,1},{25,9},{2,18},{10... | collective-permute-start | bytes 491528 | tf_op jit(solution)/shard_map/ppermute | solution.py:263
Sparse Core Ops, SparseCore 0:
  10.0 198.2 all-gather.2

commit v4 on v3

--- a/solution.py
+++ b/solution.py
@@ -30,9 +30,9 @@
 def pack_kernel(users, most, count_ref, owner_ref, tokens_ref, targets_ref, out_ref):
     rows = tokens_ref.shape[0]
     groups, rest = divmod(most, SUB)
-    owner = owner_ref[...]
+    owner_row = owner_ref[...]
     first, second = (iota((rows, rows), 0), iota((rows, rows), 1))
-    owner_row = jnp.sum(jnp.where(first == second, owner, 0), axis=0, keepdims=True)
+    owner = jnp.sum(jnp.where(first == second, owner_row, 0), axis=1, keepdims=True)
     same = (owner == owner_row) & (first < second)
     rank = jnp.sum(same.astype(jnp.int32), axis=0, keepdims=True)
     line = iota((users * SUB, rows), 0)
@@ -66,25 +66,148 @@
     )
 
 
-def user_kernel(
-    devices,
+def weight_rings(groups, members):
+    round_trip = [(at, 0) for at in range(groups // 2)]
+    round_trip += [(at, 1) for at in reversed(range(groups // 2))]
+    length, layers = (len(round_trip), members // 2)
+    rings = []
+    for core in range(2):
+        up, down = ([], [])
+        low, high = (list(range(length // 2)), list(range(length // 2, length)))
+        for layer in range(1, layers):
+            turned = layer % 2 == 0
+            up += [(layer, at) for at in (low[::-1] if turned else low)]
+            down += [(layer, at) for at in (high if turned else high[::-1])]
+        path = [(0, at) for at in reversed(range(length))] + up + down[::-1]
+        ring = []
+        for layer, at in path:
+            pair, inner = round_trip[(at + core * length // 2) % length]
+            ring.append((2 * pair + core) * members + 2 * layer + inner)
+        rings.append(ring)
+    return rings
+
+
+def weight_copies(ring_of, groups, members, source, target, sems):
+    pairs = groups // 2
+    columns = source.shape[2]
+    side = lax.rem(lax.axis_index("grp"), 2)
+    rings = weight_rings(groups, members)
+
+    def copy(member, pair):
+        spots = [ring.index((2 * pair + core) * members + member) for core, ring in enumerate(rings)]
+        spot = jnp.where(side == ring_of, spots[0], spots[1])
+        return pltpu.make_async_copy(
+            source.at[spot],
+            target.at[member, :, pl.ds(pair * columns, columns)],
+            sems.at[member, pair],
+        )
+
+    return [[copy(member, pair) for pair in range(pairs)] for member in range(members)]
+
+
+def wait_block(target, place, pairs, sems):
+    columns = target.shape[2] // pairs
+    for pair in range(pairs):
+        block = target.at[place, :, pl.ds(pair * columns, columns)]
+        pltpu.make_async_copy(block, block, sems.at[place, pair]).wait()
+
+
+def near_kernel(
+    groups_of,
     members,
     most,
-    where_ref,
+    got_ref,
+    near_ref,
+    down_ref,
+    x_out_ref,
+    frozen_ref,
+    hidden_ref,
+    x_ref,
+    cut_ref,
+    w_ref,
+    got_sem,
+    out_sem,
+    w_sem,
+):
+    groups, rest = divmod(most, SUB)
+    devices = groups_of * members
+    width = x_ref.shape[1]
+    whole = devices * SUB
+    half = w_ref.shape[1]
+    copies = []
+    column = 0
+    for group in range(groups):
+        copies.append(
+            (got_ref.at[:, pl.ds(column, width)], x_ref.at[pl.ds(group * whole, whole), :])
+        )
+        column += width
+    for extra in range(rest):
+        copies.append((got_ref.at[:, pl.ds(column, width // SUB)], cut_ref.at[extra]))
+        column += width // SUB
+    copies = [
+        pltpu.make_async_copy(source, target, got_sem.at[place])
+        for place, (source, target) in enumerate(copies)
+    ]
+    for copy in copies:
+        copy.start()
+    weights = weight_copies(0, groups_of, members, near_ref, w_ref, w_sem)
+    for place, pieces in enumerate(weights):
+        if place == 2:
+            for copy in copies:
+                copy.wait()
+        for copy in pieces:
+            copy.start()
+    join_pieces(devices, groups * whole, rest, x_ref, cut_ref)
+    out = pltpu.make_async_copy(x_ref, x_out_ref, out_sem)
+    out.start()
+
+    frozen_ref[...] = jnp.zeros_like(frozen_ref)
+    hidden_ref[...] = jnp.zeros_like(hidden_ref)
+    side = lax.rem(lax.axis_index("grp"), 2)
+
+    def add_shard(shard, unused):
+        wait_block(w_ref, shard, groups_of // 2, w_sem)
+        near = pl.ds(pl.multiple_of((2 * shard + side) * half, half), half)
+        both = pl.ds(pl.multiple_of(2 * shard * half, 2 * half), 2 * half)
+        frozen_ref[...] += dot(x_ref[:, near], w_ref[shard])
+        hidden_ref[...] += dot(x_ref[:, both], down_ref[:, both], ((1,), (1,)))
+        return unused
+
+    lax.fori_loop(0, members, add_shard, 0)
+    out.wait()
+
+
+def join_pieces(devices, bottom, rest, full, cut):
+    line, other = (iota((devices, devices * SUB), 0), iota((devices, devices * SUB), 1))
+    piece = full.shape[1] // SUB
+    for extra in range(rest):
+        first = bottom + extra * devices
+        for part in range(SUB):
+            pick = (other == line * SUB + part).astype(BF16)
+            full[first : first + devices, part * piece : (part + 1) * piece] = dot(
+                pick, cut[extra]
+            ).astype(BF16)
+
+
+def user_kernel(
+    groups_of,
+    members,
+    most,
+    cap_ref,
     clip_ref,
     got_ref,
+    rows_ref,
+    near_frozen_ref,
+    near_hidden_ref,
+    far_ref,
     down_ref,
     up_ref,
     *refs,
 ):
+    keep_refs, send_refs = (refs[0:2], refs[2:4])
     (
-        near_ref,
-        far_ref,
-        keep_refs,
-        send_refs,
         x_ref,
         goal_ref,
-        cut_ref,
         cut_goal_ref,
         used_ref,
         w_ref,
@@ -93,58 +216,38 @@
         delta_ref,
         got_sem,
         w_sem,
-    ) = refs[:2] + (refs[2:4], refs[4:6]) + refs[6:]
+    ) = refs[4:]
     groups, rest = divmod(most, SUB)
+    devices = groups_of * members
     rank, width = down_ref.shape
     kv_width = up_ref.shape[1]
     whole = devices * SUB
-    shards, half, unused = near_ref.shape
-    copies = []
-    column = 0
-    for full, cut in ((x_ref, cut_ref), (goal_ref, cut_goal_ref)):
-        size = full.shape[1]
-        for group in range(groups):
-            copies.append(
-                (got_ref.at[:, pl.ds(column, size)], full.at[pl.ds(group * whole, whole), :])
-            )
-            column += size
-        for extra in range(rest):
-            copies.append((got_ref.at[:, pl.ds(column, size // SUB)], cut.at[extra]))
-            column += size // SUB
+    half = w_ref.shape[1]
+    copies = [(rows_ref, x_ref)]
+    column = groups * width + rest * width // SUB
+    for group in range(groups):
+        copies.append(
+            (got_ref.at[:, pl.ds(column, kv_width)], goal_ref.at[pl.ds(group * whole, whole), :])
+        )
+        column += kv_width
+    for extra in range(rest):
+        copies.append((got_ref.at[:, pl.ds(column, kv_width // SUB)], cut_goal_ref.at[extra]))
+        column += kv_width // SUB
     copies.append((got_ref.at[:, pl.ds(column, LANES)], used_ref))
     copies = [
         pltpu.make_async_copy(source, target, got_sem.at[place])
         for place, (source, target) in enumerate(copies)
     ]
-    for copy in copies:
+    for copy in copies[1:] + copies[:1]:
         copy.start()
-
-    def weight_copy(at, place):
-        source = (near_ref, far_ref)[at].at[place]
-        return pltpu.make_async_copy(source, w_ref.at[at, place], w_sem.at[at, place])
-
-    ahead = min(2, shards)
-    for place in range(ahead):
-        weight_copy(0, place).start()
-        weight_copy(1, place).start()
-    for copy in copies:
+    for pieces in weight_copies(1, groups_of, members, far_ref, w_ref, w_sem):
+        for copy in pieces:
+            copy.start()
+    for copy in copies[1:]:
         copy.wait()
-    for place in range(ahead, shards):
-        weight_copy(0, place).start()
-        weight_copy(1, place).start()
-
-    line, other = (iota((devices, whole), 0), iota((devices, whole), 1))
-    for extra in range(rest):
-        bottom = groups * whole + extra * devices
-        for full, cut in ((x_ref, cut_ref), (goal_ref, cut_goal_ref)):
-            piece = full.shape[1] // SUB
-            for part in range(SUB):
-                pick = (other == line * SUB + part).astype(BF16)
-                full[bottom : bottom + devices, part * piece : (part + 1) * piece] = dot(
-                    pick, cut[extra]
-                ).astype(BF16)
-
-    cap = where_ref[0].astype(F32)
+    join_pieces(devices, groups * whole, rest, goal_ref, cut_goal_ref)
+
+    cap = cap_ref[lax.axis_index("grp") * members + lax.axis_index("fsdp")].astype(F32)
     used = used_ref[...]
     pieces = []
     if groups:
@@ -164,25 +267,18 @@
         pieces.append(jnp.where(live, 1.0 / cap, 0.0)[:, :1])
     scale = jnp.concatenate(pieces, axis=0) if len(pieces) > 1 else pieces[0]
 
-    frozen_ref[...] = jnp.zeros_like(frozen_ref)
-    hidden_ref[...] = jnp.zeros_like(hidden_ref)
-    side = where_ref[1]
-
-    def add_shard(place, unused):
-        weight_copy(0, place).wait()
-        weight_copy(1, place).wait()
-        shard = where_ref[4 + place]
-        near = pl.ds(pl.multiple_of((2 * shard + side) * half, half), half)
+    frozen_ref[...] = near_frozen_ref[...]
+    hidden_ref[...] = near_hidden_ref[...]
+    side = lax.rem(lax.axis_index("grp"), 2)
+    copies[0].wait()
+
+    def add_shard(shard, unused):
+        wait_block(w_ref, shard, groups_of // 2, w_sem)
         far = pl.ds(pl.multiple_of((2 * shard + 1 - side) * half, half), half)
-        near_x, far_x = (x_ref[:, near], x_ref[:, far])
-        frozen_ref[...] += dot(near_x, w_ref[0, place]) + dot(far_x, w_ref[1, place])
-        lanes = ((1,), (1,))
-        hidden_ref[...] += dot(near_x, down_ref[:, near], lanes) + dot(
-            far_x, down_ref[:, far], lanes
-        )
+        frozen_ref[...] += dot(x_ref[:, far], w_ref[shard])
         return unused
 
-    lax.fori_loop(0, shards, add_shard, 0)
+    lax.fori_loop(0, members, add_shard, 0)
 
     rate = ADAPTER_SCALE * LEARN_RATE
     block = min(width, 1024)
@@ -228,8 +324,8 @@
         for pair in range(devices // members // 2):
             for member in range(members):
                 device = (2 * pair + core) * members + member
-                spot = lax.bitwise_xor(where_ref[2], pair)
-                inner = lax.bitwise_xor(where_ref[3], member % 2)
+                spot = lax.bitwise_xor(lax.div(lax.axis_index("grp"), 2), pair)
+                inner = lax.bitwise_xor(lax.rem(lax.axis_index("fsdp"), 2), member % 2)
                 outer = member // 2
                 moved = factor * delta_ref[:, device * share : (device + 1) * share]
                 targets[0][spot, inner, outer] = moved[:edge]
@@ -280,7 +376,6 @@
 ):
     groups, members = (lax.axis_size("grp"), lax.axis_size("fsdp"))
     devices = groups * members
-    myself = lax.axis_index(BOTH)
     side = lax.axis_index("grp") % 2
     per_dev, width = tokens.shape
     kv_width = targets.shape[1]
@@ -295,9 +390,10 @@
     anywhere = pl.BlockSpec(memory_space=pl.ANY)
 
     half = value_weight.shape[0] // 2
-    mine = lax.dynamic_slice_in_dim(value_weight, side * half, half, axis=0)
-    path = list(range(0, members, 2)) + list(range(1, members, 2))[::-1]
-    near = lax.all_gather(mine, "fsdp", axis=0, axis_index_groups=[path])
+    piece = kv_width // (groups // 2)
+    pair = lax.axis_index("grp") // 2
+    mine = lax.dynamic_slice(value_weight, (side * half, pair * piece), (half, piece))
+    near = lax.all_gather(mine, BOTH, axis=0, axis_index_groups=weight_rings(groups, members))
     swap = [(at, at ^ 1) for at in range(groups)]
     far = lax.ppermute(near, "grp", swap)
 
@@ -309,42 +405,60 @@
         out_specs=vmem,
         compiler_params=pltpu.CompilerParams(vmem_limit_bytes=VMEM_BYTES),
         name="pack_rows",
-    )(device_row_count, row_owner_user, tokens, targets)
-    cap = lax.dynamic_slice_in_dim(user_row_cap, myself, 1)
-    pair = lax.axis_index("grp") // 2
-    inner = lax.axis_index("fsdp") % 2
-    spots = jnp.stack([side, pair, inner] + [jnp.int32(place) for place in path])
-    where = jnp.concatenate([cap, spots.astype(jnp.int32)])
-    packed, where = lax.optimization_barrier((packed, where))
+    )(device_row_count, row_owner_user.reshape(1, per_dev), tokens, targets)
     got = lax.all_to_all(
         packed.reshape(users, SUB, columns), BOTH, split_axis=0, concat_axis=0, tiled=True
     ).reshape(whole, columns)
     share = width // devices
     tall = rank + kv_width // devices * rank // share
+    down = adapter_down.T
+    rows, near_frozen, near_hidden = pl.pallas_call(
+        lambda *refs: near_kernel(groups, members, most, *refs),
+        out_shape=[
+            jax.ShapeDtypeStruct((slots, width), BF16),
+            jax.ShapeDtypeStruct((slots, kv_width), F32),
+            jax.ShapeDtypeStruct((slots, rank), F32),
+        ],
+        in_specs=[anywhere, anywhere, vmem],
+        out_specs=[anywhere, vmem, vmem],
+        scratch_shapes=[
+            pltpu.VMEM((slots, width), BF16),
+            pltpu.VMEM((max(rest, 1), whole, width // SUB), BF16),
+            pltpu.VMEM((members, half, kv_width), BF16),
+            pltpu.SemaphoreType.DMA((whole_groups + rest,)),
+            pltpu.SemaphoreType.DMA,
+            pltpu.SemaphoreType.DMA((members, groups // 2)),
+        ],
+        compiler_params=pltpu.CompilerParams(vmem_limit_bytes=VMEM_BYTES),
+        cost_estimate=pl.CostEstimate(
+            flops=slots * width * kv_width, bytes_accessed=3 * 10**7, transcendentals=0
+        ),
+        name="near_product",
+    )(got, near, down)
+
     edge = tall // (2 * SUB) * SUB
     grid = (groups // 2, 2, members // 2)
     streams = [jax.ShapeDtypeStruct(grid + (size, share), F32) for size in (edge, tall - edge)]
     kept_y, kept_x, sent_y, sent_x = pl.pallas_call(
-        lambda *refs: user_kernel(devices, members, most, *refs),
+        lambda *refs: user_kernel(groups, members, most, *refs),
         out_shape=streams * 2,
-        in_specs=[smem, smem, anywhere, vmem, vmem, anywhere, anywhere],
+        in_specs=[smem, smem, anywhere, anywhere, vmem, vmem, anywhere, vmem, vmem],
         out_specs=[vmem] * 4,
         scratch_shapes=[
             pltpu.VMEM((slots, width), BF16),
             pltpu.VMEM((slots, kv_width), BF16),
-            pltpu.VMEM((max(rest, 1), whole, width // SUB), BF16),
             pltpu.VMEM((max(rest, 1), whole, kv_width // SUB), BF16),
             pltpu.VMEM((whole, LANES), BF16),
-            pltpu.VMEM((2, members, half, kv_width), BF16),
+            pltpu.VMEM((members, half, kv_width), BF16),
             pltpu.VMEM((slots, kv_width), F32),
             pltpu.VMEM((slots, rank), F32),
             pltpu.VMEM((rank, width), F32),
-            pltpu.SemaphoreType.DMA((2 * (whole_groups + rest) + 1,)),
-            pltpu.SemaphoreType.DMA((2, members)),
+            pltpu.SemaphoreType.DMA((whole_groups + rest + 2,)),
+            pltpu.SemaphoreType.DMA((members, groups // 2)),
         ],
         compiler_params=pltpu.CompilerParams(vmem_limit_bytes=VMEM_BYTES),
         name="user_steps",
-    )(where, clip_norm_bound, got, adapter_down.T, adapter_up, near, far)
+    )(user_row_cap, clip_norm_bound, got, rows, near_frozen, near_hidden, far, down, adapter_up)
 
     first = kept_y + lax.ppermute(sent_y, "grp", swap)
     second = kept_x + lax.ppermute(sent_x, "grp", swap)

time: 294 us -> 267 us (0.908)
  waiting for transfers between devices: 206 us -> 184 us
  Pallas kernels: 31.4 us -> 39.5 us
  blocking collectives: 17.1 us -> 10.3 us
  local copies, waits for them, and re-layouts: 6.77 us -> 2.04 us
    all_gather x1, waiting for transfers between devices: 179 us -> 167 us  [body(): lax.all_gather(mine, BOTH, axis=0, axis_index_groups=weight_rings(groups,...]
    ppermute x1, waiting for transfers between devices: 12.8 us -> 2.12 us  [body(): far = lax.ppermute(near, 'grp', swap)]
    pallas_call x1 -> x2, Pallas kernels: 24.1 us -> 32.2 us  [the longest x1 21.5 us: body(): pl.pallas_call(lambda *refs: user_kernel(groups, members, most, *refs), o...]
    all_to_all x1, blocking collectives: 17.1 us -> 10.3 us  [body(): lax.all_to_all(package, 'fsdp', split_axis=0, concat_axis=0, axis_index_g...]
    unnamed x7 -> x4, local copies, waits for them, and re-layouts: 2.97 us -> 0.01 us
  transfers between devices with their start and end apart: 9 -> 9, of which waited for: 7 -> 6; matrix products, arithmetic and copies ran while one was open for 2% -> 1% of each run, Pallas kernels for 2% -> 7%
where the time goes in v4:
time: 267 us; the launch traced here: 266 us
  waiting for transfers between devices  184 us (69%)
  Pallas kernels  39.5 us (15%)
  between operations  15.5 us (6%)
  starting transfers between devices  10.8 us (4%)
  blocking collectives  10.3 us (4%)
  other arithmetic  3.7 us (1%)
    all_gather x1, waiting for transfers between devices, body(): lax.all_gather(mine, BOTH, axis=0, axis_index_groups=weight_rings(groups,...  167 us
    pallas_call x1, Pallas kernels, body(): pl.pallas_call(lambda *refs: user_kernel(groups, members, most, *refs), o...  21.5 us
    ppermute x4, waiting for transfers between devices, halve(): package = lax.ppermute(send, axis, pairs) + keep  13.2 us
    pallas_call x1, Pallas kernels, body(): pl.pallas_call(lambda *refs: near_kernel(groups, members, most, *refs), o...  10.7 us
    all_to_all x1, blocking collectives, body(): lax.all_to_all(package, 'fsdp', split_axis=0, concat_axis=0, axis_index_g...  10.3 us
    all_to_all x1, starting transfers between devices, body(): lax.all_to_all(packed.reshape(users, SUB, columns), BOTH, split_axis=0, c...  7.41 us
    pallas_call x1, Pallas kernels, body(): pl.pallas_call(lambda *refs: pack_kernel(users, most, *refs), out_shape=j...  7.24 us
  transfers between devices with their start and end apart: 9, of which 6 were waited for; matrix products, arithmetic and copies ran while one was open for 1% of the time, Pallas kernels for 7%

profile of v4, /device:TPU:0, one launch (start us, length us, event | category | flops | bytes accessed | tf_op | source)
XLA Modules:
  0.0 266.2 jit_solution(4299909284284214226)
XLA Ops:
  7.2 0.0 all-gather.3.cloned.1.call-start
  7.2 1.9 dynamic_slice.3
  9.1 0.0 all-gather.3.cloned.1.call-update
  9.8 7.2 %pack_rows.1 = bf16[256,10496]{1,0:T(8,128)(2,1)} custom-call(s32[1]{0:T(128)S(6)} %copy.15.refs_0_, s32[1,192]{1,0:T(1,128)} %bitcast.27, bf16[192,8192]{1,0:T(8,128)(2,1)} %refs_2_.1, bf16[192,1024]{1,0:T(8,128)(2,1)} %refs_3_.1), custom_call_target="tpu_custom_call" | custom-call | tf_op jit(solution)/shard_map/pack_rows/pallas_call | solution.py:401
  17.0 7.4 %all-to-all-start = ((bf16[32,8,10496]{2,1,0:T(8,128)(2,1)}), bf16[32,8,10496]{2,1,0:T(8,128)(2,1)}, u32[]{:S(2)}, u32[]{:S(2)}) async-start(bf16[32,8,10496]{2,1,0:T(8,128)(2,1)} %bitcast.22), calls=%async_computation | async-start | bytes 10747904 | tf_op jit(solution)/shard_map/all_to_all | solution.py:409
  24.4 167.5 %all-gather.3.cloned.1.call-done = bf16[8192,512]{1,0:T(8,128)(2,1)} async-done(((bf16[512,512]{1,0:T(8,128)(2,1)}), bf16[8192,512]{1,0:T(8,128)(2,1)}) %all-gather.3.cloned.1.call-update) | async-done | bytes 8388624 | tf_op jit(solution)/shard_map/all_gather | solution.py:396
  191.9 0.0 collective-permute-start
  192.6 0.0 all-to-all-done
  192.6 10.7 %near_product.1 = (bf16[288,8192]{1,0:T(8,128)(2,1)}, f32[288,1024]{1,0:T(8,128)}, f32[288,64]{1,0:T(8,128)}) custom-call(bf16[256,10496]{1,0:T(8,128)(2,1)} %bitcast.2.refs_0_.refs_2_, bf16[16,512,512]{2,1,0:T(8,128)(2,1)} %bitcast.24, bf16[64,8192]{1,0:T(8,128)(2,1)} %bitcast.25), custom_call_target="tpu_custom_call" | custom-call | flops 2415919104 | bytes 30000000 | tf_op jit(solution)/shard_map/near_product/pallas_call | solution.py:415
  203.3 2.1 collective-permute-done.refs_6_
  205.4 21.5 %user_steps.1 = (f32[2,2,4,32,256]{4,3,2,1,0:T(8,128)}, f32[2,2,4,40,256]{4,3,2,1,0:T(8,128)}, f32[2,2,4,32,256]{4,3,2,1,0:T(8,128)}, f32[2,2,4,40,256]{4,3,2,1,0:T(8,128)}) custom-call(s32[32]{0:T(128)} %refs_0_.2, f32[1]{0:T(128)} %copy.16.refs_1_, bf16[256,10496]{1,0:T(8,128)(2,1)} %bitcast.2.refs_0_.refs_2_, bf16[288,8192]{1,0:T(8,128)(2,1)} %get-tuple-element.9.refs_3_, ...), custom_call_target="tpu_custom_call" | custom-call | tf_op jit(solution)/shard_map/user_steps/pallas_call | solution.py:442
  226.9 0.0 copy-start
  226.9 0.0 copy-start.1
  227.0 0.1 collective-permute-start.1
  227.1 0.5 collective-permute-start.4
  227.5 1.6 collective-permute-done.1
  229.1 1.1 add.38
  230.3 0.1 collective-permute-start.2
  230.4 0.0 collective-permute-done.4
  230.4 1.2 add.41
  231.6 0.2 collective-permute-start.5
  231.8 6.9 %collective-permute-done.2 = f32[1,2,4,32,256]{4,3,2,1,0:T(8,128)S(1)} collective-permute-done((f32[1,2,4,32,256]{4,3,2,1,0:T(8,128)S(1)}, f32[1,2,4,32,256]{4,3,2,1,0:T(8,128)S(1)}, u32[]{:S(2)}, u32[]{:S(2)}) %collective-permute-start.2) | collective-permute-done | bytes 262176 | tf_op jit(solution)/shard_map/ppermute | solution.py:359
  238.8 0.2 collective-permute-start.3
  239.0 3.1 %collective-permute-done.5 = f32[2,1,4,40,256]{4,3,2,1,0:T(8,128)S(1)} collective-permute-done((f32[2,1,4,40,256]{4,3,2,1,0:T(8,128)S(1)}, f32[2,1,4,40,256]{4,3,2,1,0:T(8,128)S(1)}, u32[]{:S(2)}, u32[]{:S(2)}) %collective-permute-start.5) | collective-permute-done | bytes 327712 | tf_op jit(solution)/shard_map/ppermute | solution.py:359
  242.1 2.3 collective-permute-start.6
  244.4 0.0 collective-permute-done.3
  244.4 3.3 %collective-permute-done.6 = f32[1,1,4,40,256]{4,3,2,1,0:T(8,128)S(1)} collective-permute-done((f32[1,1,4,40,256]{4,3,2,1,0:T(8,128)S(1)}, f32[1,1,4,40,256]{4,3,2,1,0:T(8,128)S(1)}, u32[]{:S(2)}, u32[]{:S(2)}) %collective-permute-start.6) | collective-permute-done | bytes 163872 | tf_op jit(solution)/shard_map/ppermute | solution.py:359
  247.8 10.3 %all_to_all.10 = f32[4,72,256]{2,1,0:T(8,128)S(1)} all-to-all(f32[4,72,256]{2,1,0:T(8,128)S(1)} %pad_maximum_fusion), channel_id=1, replica_groups={{0,2,4,6},{1,3,5,7},{8,10,12,14},{9,11,13,15},{16,18,20,22},{17,19,21,2..., dimensions={0} | all-to-all | bytes 589824 | tf_op jit(solution)/shard_map/all_to_all | solution.py:469
  258.0 0.1 reshape.22
  258.1 0.0 copy-done
  258.1 0.6 fusion.2
  258.8 0.0 copy-done.1
  258.8 0.6 bitcast_add_fusion
  (11 shorter events, 0.2 us)
Async XLA Ops:
  7.2 184.8 %all-gather.3.cloned.1.call-start = ((), (), s32[]{:S(2)}) async-start(), calls=%async_computation.2 | async-start | bytes 8912896 | tf_op jit(solution)/shard_map/all_gather | solution.py:396
  17.0 175.5 %all-to-all-start = ((bf16[32,8,10496]{2,1,0:T(8,128)(2,1)}), bf16[32,8,10496]{2,1,0:T(8,128)(2,1)}, u32[]{:S(2)}, u32[]{:S(2)}) async-start(bf16[32,8,10496]{2,1,0:T(8,128)(2,1)} %bitcast.22), calls=%async_computation | async-start | bytes 10747904 | tf_op jit(solution)/shard_map/all_to_all | solution.py:409
  191.9 13.5 %collective-permute-start = (bf16[16,512,512]{2,1,0:T(8,128)(2,1)}, bf16[16,512,512]{2,1,0:T(8,128)(2,1)}, u32[]{:S(2)}, u32[]{:S(2)}) collective-permute-start(bf16[16,512,512]{2,1,0:T(8,128)(2,1)} %bitcast.23), channel_id=1, source_target_pairs={{0,8},{8,0},{16,24},{24,16},{1,9},{9,1},{17,25},{25,17},{2,10},{10... | collective-permute-start | bytes 25165832 | tf_op jit(solution)/shard_map/ppermute | solution.py:398
  226.9 31.2 %copy-start = (f32[256,64]{0,1:T(8,128)S(1)}, f32[256,64]{0,1:T(8,128)}, u32[]{:S(2)}) copy-start(f32[256,64]{0,1:T(8,128)} %param.20) | copy-start | bytes 196612
  226.9 31.8 %copy-start.1 = (f32[64,32]{0,1:T(8,128)S(1)}, f32[64,32]{0,1:T(8,128)}, u32[]{:S(2)}) copy-start(f32[64,32]{0,1:T(8,128)} %param.21) | copy-start | bytes 24580
  227.0 2.2 collective-permute-start.1
  227.1 3.3 %collective-permute-start.4 = (f32[2,2,4,40,256]{4,3,2,1,0:T(8,128)}, f32[2,2,4,40,256]{4,3,2,1,0:T(8,128)S(1)}, u32[]{:S(2)}, u32[]{:S(2)}) collective-permute-start(f32[2,2,4,40,256]{4,3,2,1,0:T(8,128)} %get-tuple-element.15), channel_id=1, source_target_pairs={{0,8},{8,0},{16,24},{24,16},{1,9},{9,1},{17,25},{25,17},{2,10},{10... | collective-permute-start | bytes 1966088 | tf_op jit(solution)/shard_map/ppermute | solution.py:464
  230.3 8.4 %collective-permute-start.2 = (f32[1,2,4,32,256]{4,3,2,1,0:T(8,128)S(1)}, f32[1,2,4,32,256]{4,3,2,1,0:T(8,128)S(1)}, u32[]{:S(2)}, u32[]{:S(2)}) collective-permute-start(f32[1,2,4,32,256]{4,3,2,1,0:T(8,128)S(1)} %slice.40), channel_id=1, source_target_pairs={{0,16},{8,24},{16,0},{24,8},{1,17},{9,25},{17,1},{25,9},{2,18},{10... | collective-permute-start | bytes 786440 | tf_op jit(solution)/shard_map/ppermute | solution.py:359
  231.6 10.4 %collective-permute-start.5 = (f32[2,1,4,40,256]{4,3,2,1,0:T(8,128)S(1)}, f32[2,1,4,40,256]{4,3,2,1,0:T(8,128)S(1)}, u32[]{:S(2)}, u32[]{:S(2)}) collective-permute-start(f32[2,1,4,40,256]{4,3,2,1,0:T(8,128)S(1)} %slice.44), channel_id=1, source_target_pairs={{0,1},{1,0},{2,3},{3,2},{4,5},{5,4},{6,7},{7,6},{8,9},{9,8},{10,11... | collective-permute-start | bytes 983048 | tf_op jit(solution)/shard_map/ppermute | solution.py:359
  238.8 5.6 %collective-permute-start.3 = (f32[1,1,4,32,256]{4,3,2,1,0:T(8,128)S(1)}, f32[1,1,4,32,256]{4,3,2,1,0:T(8,128)S(1)}, u32[]{:S(2)}, u32[]{:S(2)}) collective-permute-start(f32[1,1,4,32,256]{4,3,2,1,0:T(8,128)S(1)} %slice.42), channel_id=1, source_target_pairs={{0,1},{1,0},{2,3},{3,2},{4,5},{5,4},{6,7},{7,6},{8,9},{9,8},{10,11... | collective-permute-start | bytes 393224 | tf_op jit(solution)/shard_map/ppermute | solution.py:359
  242.1 5.6 %collective-permute-start.6 = (f32[1,1,4,40,256]{4,3,2,1,0:T(8,128)S(1)}, f32[1,1,4,40,256]{4,3,2,1,0:T(8,128)S(1)}, u32[]{:S(2)}, u32[]{:S(2)}) collective-permute-start(f32[1,1,4,40,256]{4,3,2,1,0:T(8,128)S(1)} %slice.46), channel_id=1, source_target_pairs={{0,16},{8,24},{16,0},{24,8},{1,17},{9,25},{17,1},{25,9},{2,18},{10... | collective-permute-start | bytes 491528 | tf_op jit(solution)/shard_map/ppermute | solution.py:359
Sparse Core Ops, SparseCore 0:
  9.5 182.3 all-gather.2

commit v5 on v4

--- a/solution.py
+++ b/solution.py
@@ -173,7 +173,7 @@
         hidden_ref[...] += dot(x_ref[:, both], down_ref[:, both], ((1,), (1,)))
         return unused
 
-    lax.fori_loop(0, members, add_shard, 0)
+    lax.fori_loop(0, members, add_shard, 0, unroll=2)
     out.wait()
 
 
@@ -204,7 +204,7 @@
     up_ref,
     *refs,
 ):
-    keep_refs, send_refs = (refs[0:2], refs[2:4])
+    keep_ref, send_ref = refs[:2]
     (
         x_ref,
         goal_ref,
@@ -216,7 +216,7 @@
         delta_ref,
         got_sem,
         w_sem,
-    ) = refs[4:]
+    ) = refs[2:]
     groups, rest = divmod(most, SUB)
     devices = groups_of * members
     rank, width = down_ref.shape
@@ -278,7 +278,7 @@
         frozen_ref[...] += dot(x_ref[:, far], w_ref[shard])
         return unused
 
-    lax.fori_loop(0, members, add_shard, 0)
+    lax.fori_loop(0, members, add_shard, 0, unroll=2)
 
     rate = ADAPTER_SCALE * LEARN_RATE
     block = min(width, 1024)
@@ -306,11 +306,16 @@
                 half_down = (down_ref[:, lanes].astype(F32) + moved).astype(BF16)
                 hidden_ref[...] += dot(x_ref[:, lanes], half_down, ((1,), (1,)))
                 return unused
-            return unused + jnp.sum(moved * moved)
-
-        squares = lax.fori_loop(0, width // block, down_block, jnp.zeros((), F32))
-
-    total = squares + jnp.sum(up_delta * up_delta) + EPSILON
+            square = moved * moved
+            for at in range(0, block, LANES):
+                unused = unused + square[:, at : at + LANES]
+            return unused
+
+        squares = lax.fori_loop(
+            0, width // block, down_block, jnp.zeros((rank, LANES), F32), unroll=2
+        )
+
+    total = jnp.sum(squares) + jnp.sum(up_delta * up_delta) + EPSILON
     total = jnp.full((1, LANES), total, F32)
     factor = jnp.minimum(1.0, clip_ref[0] / jnp.sqrt(total))[:, :1]
     share = width // devices
@@ -319,22 +324,19 @@
     pieces = share // rank
     tall = up_share // pieces
 
-    def write(core, targets):
-        edge = targets[0].shape[3]
-        for pair in range(devices // members // 2):
+    def write(core, target):
+        for pair in range(groups_of // 2):
             for member in range(members):
                 device = (2 * pair + core) * members + member
                 spot = lax.bitwise_xor(lax.div(lax.axis_index("grp"), 2), pair)
-                inner = lax.bitwise_xor(lax.rem(lax.axis_index("fsdp"), 2), member % 2)
-                outer = member // 2
-                moved = factor * delta_ref[:, device * share : (device + 1) * share]
-                targets[0][spot, inner, outer] = moved[:edge]
-                targets[1][spot, inner, outer, : rank - edge, :] = moved[edge:]
+                place = lax.bitwise_xor(lax.axis_index("fsdp"), member)
+                moved = delta_ref[:, device * share : (device + 1) * share]
+                target[spot, place, :rank, :] = factor * moved
                 first = device * up_share
                 parts = [
                     up_turned[first + at * tall : first + (at + 1) * tall] for at in range(pieces)
                 ]
-                targets[1][spot, inner, outer, rank - edge :, :] = (
+                target[spot, place, rank:, :] = (
                     jnp.concatenate(parts, axis=1) if pieces > 1 else parts[0]
                 )
 
@@ -343,22 +345,20 @@
 
         @pl.when(mine)
         def _():
-            write(core, keep_refs)
+            write(core, keep_ref)
 
         @pl.when(jnp.logical_not(mine))
         def _():
-            write(core, send_refs)
-
-
-def halve(package, axis, bits, partner):
-    bit = package.shape[bits] // 2
-    while bit:
-        keep = lax.slice_in_dim(package, 0, bit, axis=bits)
-        send = lax.slice_in_dim(package, bit, 2 * bit, axis=bits)
-        pairs = [(at, at ^ (partner * bit)) for at in range(lax.axis_size(axis))]
-        package = lax.ppermute(send, axis, pairs) + keep
-        bit //= 2
-    return package
+            write(core, send_ref)
+
+
+def exchange(blocks, partner_of):
+    devices = lax.axis_size("grp") * lax.axis_size("fsdp")
+    total = blocks[0]
+    for place in range(1, len(blocks)):
+        pairs = [(at, partner_of(at, place)) for at in range(devices)]
+        total = total + lax.ppermute(blocks[place], BOTH, pairs)
+    return total
 
 
 def body(
@@ -436,14 +436,12 @@
         name="near_product",
     )(got, near, down)
 
-    edge = tall // (2 * SUB) * SUB
-    grid = (groups // 2, 2, members // 2)
-    streams = [jax.ShapeDtypeStruct(grid + (size, share), F32) for size in (edge, tall - edge)]
-    kept_y, kept_x, sent_y, sent_x = pl.pallas_call(
+    package = jax.ShapeDtypeStruct((groups // 2, members, tall, share), F32)
+    keep, send = pl.pallas_call(
         lambda *refs: user_kernel(groups, members, most, *refs),
-        out_shape=streams * 2,
+        out_shape=[package] * 2,
         in_specs=[smem, smem, anywhere, anywhere, vmem, vmem, anywhere, vmem, vmem],
-        out_specs=[vmem] * 4,
+        out_specs=[vmem] * 2,
         scratch_shapes=[
             pltpu.VMEM((slots, width), BF16),
             pltpu.VMEM((slots, kv_width), BF16),
@@ -460,16 +458,21 @@
         name="user_steps",
     )(user_row_cap, clip_norm_bound, got, rows, near_frozen, near_hidden, far, down, adapter_up)
 
-    first = kept_y + lax.ppermute(sent_y, "grp", swap)
-    second = kept_x + lax.ppermute(sent_x, "grp", swap)
-    first = halve(halve(first, "grp", 0, 2), "fsdp", 1, 1)
-    second = halve(halve(second, "fsdp", 1, 1), "grp", 0, 2)
-    package = jnp.concatenate([first[0, 0], second[0, 0]], axis=1)
-    lines = [list(range(one, members, 2)) for one in range(2)]
-    package = lax.all_to_all(
-        package, "fsdp", split_axis=0, concat_axis=0, axis_index_groups=lines, tiled=True
+    other = lax.ppermute(send, "grp", swap)
+    keep = keep.reshape(groups // 2, members // 2, 2, tall, share)
+    other = other.reshape(keep.shape)
+    square = [(pair, inner) for pair in range(groups // 2) for inner in range(2)]
+
+    def in_square(at, place):
+        pair, inner = square[place]
+        return at ^ (2 * pair * members) ^ inner
+
+    package = exchange(
+        [keep[pair, :, inner] + other[pair, :, inner] for pair, inner in square], in_square
     )
-    package = jnp.sum(package, axis=0)
+    package = exchange(
+        [package[place] for place in range(members // 2)], lambda at, place: at ^ (2 * place)
+    )
     clip = clip_norm_bound[0]
     update_a = package[:rank].T + clip * down_noise
     pieces = share // rank

time: 267 us -> 263 us (0.985)
  blocking collectives: 10.3 us -> 0 us
  waiting for transfers between devices: 184 us -> 189 us
  starting transfers between devices: 10.8 us -> 15.6 us
  Pallas kernels: 39.5 us -> 36.4 us
    all_to_all x1 -> x0, blocking collectives: 10.3 us -> none  [body(): lax.all_to_all(package, 'fsdp', split_axis=0, concat_axis=0, axis_index_g...]
    ppermute x6 -> x7, starting transfers between devices: 3.36 us -> 8.14 us  [the longest x6 7.97 us: exchange(): total = total + lax.ppermute(blocks[place], BOTH, pairs)]
    ppermute x6 -> x7, waiting for transfers between devices: 14.8 us -> 19.4 us  [the longest x6 16.5 us: exchange(): total = total + lax.ppermute(blocks[place], BOTH, pairs)]
    pallas_call x1, Pallas kernels: 21.5 us -> 18.5 us  [body(): pl.pallas_call(lambda *refs: user_kernel(groups, members, most, *refs), o...]
  transfers between devices with their start and end apart: 9 -> 10, of which waited for: 6 -> 7; matrix products, arithmetic and copies ran while one was open for 1% -> 0% of each run, Pallas kernels for 7% -> 7%
where the time goes in v5:
time: 263 us; the launch traced here: 262 us
  waiting for transfers between devices  189 us (72%)
  Pallas kernels  36.4 us (14%)
  starting transfers between devices  15.6 us (6%)
  between operations  15.4 us (6%)
  other arithmetic  3.59 us (1%)
    all_gather x1, waiting for transfers between devices, body(): lax.all_gather(mine, BOTH, axis=0, axis_index_groups=weight_rings(groups,...  168 us
    pallas_call x1, Pallas kernels, body(): pl.pallas_call(lambda *refs: user_kernel(groups, members, most, *refs), o...  18.5 us
    ppermute x6, waiting for transfers between devices, exchange(): total = total + lax.ppermute(blocks[place], BOTH, pairs)  16.5 us
    pallas_call x1, Pallas kernels, body(): pl.pallas_call(lambda *refs: near_kernel(groups, members, most, *refs), o...  10.7 us
    ppermute x6, starting transfers between devices, exchange(): total = total + lax.ppermute(blocks[place], BOTH, pairs)  7.97 us
    all_to_all x1, starting transfers between devices, body(): lax.all_to_all(packed.reshape(users, SUB, columns), BOTH, split_axis=0, c...  7.41 us
    pallas_call x1, Pallas kernels, body(): pl.pallas_call(lambda *refs: pack_kernel(users, most, *refs), out_shape=j...  7.25 us
  transfers between devices with their start and end apart: 10, of which 7 were waited for; matrix products, arithmetic and copies ran while one was open for 0% of the time, Pallas kernels for 7%

profile of v5, /device:TPU:0, one launch (start us, length us, event | category | flops | bytes accessed | tf_op | source)
XLA Modules:
  0.0 262.5 jit_solution(1329152074757829475)
XLA Ops:
  7.2 0.0 all-gather.3.cloned.1.call-start
  7.2 1.9 dynamic_slice.3
  9.2 0.0 all-gather.3.cloned.1.call-update
  9.8 7.2 %pack_rows.1 = bf16[256,10496]{1,0:T(8,128)(2,1)} custom-call(s32[1]{0:T(128)S(6)} %copy.31.refs_0_, s32[1,192]{1,0:T(1,128)} %bitcast.103, bf16[192,8192]{1,0:T(8,128)(2,1)} %refs_2_.1, bf16[192,1024]{1,0:T(8,128)(2,1)} %refs_3_.1), custom_call_target="tpu_custom_call" | custom-call | tf_op jit(solution)/shard_map/pack_rows/pallas_call | solution.py:401
  17.1 7.4 %all-to-all-start = ((bf16[32,8,10496]{2,1,0:T(8,128)(2,1)}), bf16[32,8,10496]{2,1,0:T(8,128)(2,1)}, u32[]{:S(2)}, u32[]{:S(2)}) async-start(bf16[32,8,10496]{2,1,0:T(8,128)(2,1)} %bitcast.94), calls=%async_computation | async-start | bytes 10747904 | tf_op jit(solution)/shard_map/all_to_all | solution.py:409
  24.5 167.9 %all-gather.3.cloned.1.call-done = bf16[8192,512]{1,0:T(8,128)(2,1)} async-done(((bf16[512,512]{1,0:T(8,128)(2,1)}), bf16[8192,512]{1,0:T(8,128)(2,1)}) %all-gather.3.cloned.1.call-update) | async-done | bytes 8388624 | tf_op jit(solution)/shard_map/all_gather | solution.py:396
  192.4 0.0 collective-permute-start
  193.0 0.0 all-to-all-done
  193.0 10.7 %near_product.1 = (bf16[288,8192]{1,0:T(8,128)(2,1)}, f32[288,1024]{1,0:T(8,128)}, f32[288,64]{1,0:T(8,128)}) custom-call(bf16[256,10496]{1,0:T(8,128)(2,1)} %bitcast.2.refs_0_.refs_2_, bf16[16,512,512]{2,1,0:T(8,128)(2,1)} %bitcast.96, bf16[64,8192]{1,0:T(8,128)(2,1)} %bitcast.97), custom_call_target="tpu_custom_call" | custom-call | flops 2415919104 | bytes 30000000 | tf_op jit(solution)/shard_map/near_product/pallas_call | solution.py:415
  203.7 2.1 collective-permute-done.refs_6_
  205.9 18.5 %user_steps.1 = (f32[2,8,72,256]{3,2,1,0:T(8,128)}, f32[2,8,72,256]{3,2,1,0:T(8,128)}) custom-call(s32[32]{0:T(128)} %refs_0_.2, f32[1]{0:T(128)} %copy.32.refs_1_, bf16[256,10496]{1,0:T(8,128)(2,1)} %bitcast.2.refs_0_.refs_2_, bf16[288,8192]{1,0:T(8,128)(2,1)} %get-tuple-element.7.refs_3_, f32[288,1024]{1,0:T(8,128)} %get-tuple-element.8.refs_4_, ...), custom_call_target="tpu_custom_call" | custom-call | tf_op jit(solution)/shard_map/user_steps/pallas_call | solution.py:440
  224.3 0.2 collective-permute-start.1
  224.5 3.0 %collective-permute-done.1 = f32[2,8,72,256]{3,2,1,0:T(8,128)S(1)} collective-permute-done((f32[2,8,72,256]{3,2,1,0:T(8,128)}, f32[2,8,72,256]{3,2,1,0:T(8,128)S(1)}, u32[]{:S(2)}, u32[]{:S(2)}) %collective-permute-start.1) | collective-permute-done | bytes 1179680 | tf_op jit(solution)/shard_map/ppermute | solution.py:461
  227.5 1.3 fusion.5
  228.7 0.1 collective-permute-start.2
  228.8 0.1 collective-permute-start.3
  228.9 0.0 copy-start
  228.9 0.0 copy-start.1
  228.9 3.4 %collective-permute-start.4 = (f32[4,72,256]{2,1,0:T(8,128)S(1)}, f32[4,72,256]{2,1,0:T(8,128)S(1)}, u32[]{:S(2)}, u32[]{:S(2)}) collective-permute-start(f32[4,72,256]{2,1,0:T(8,128)S(1)} %get-tuple-element.14), channel_id=1, source_target_pairs={{0,17},{1,16},{2,19},{3,18},{4,21},{5,20},{6,23},{7,22},{8,25},{9,... | collective-permute-start | bytes 884744 | tf_op jit(solution)/shard_map/ppermute | solution.py:360
  232.3 6.4 %collective-permute-done.2 = f32[4,72,256]{2,1,0:T(8,128)S(1)} collective-permute-done((f32[4,72,256]{2,1,0:T(8,128)S(1)}, f32[4,72,256]{2,1,0:T(8,128)S(1)}, u32[]{:S(2)}, u32[]{:S(2)}) %collective-permute-start.2) | collective-permute-done | bytes 294944 | tf_op jit(solution)/shard_map/ppermute | solution.py:360
  238.6 5.6 %collective-permute-done.3 = f32[4,72,256]{2,1,0:T(8,128)S(1)} collective-permute-done((f32[4,72,256]{2,1,0:T(8,128)S(1)}, f32[4,72,256]{2,1,0:T(8,128)S(1)}, u32[]{:S(2)}, u32[]{:S(2)}) %collective-permute-start.3) | collective-permute-done | bytes 294944 | tf_op jit(solution)/shard_map/ppermute | solution.py:360
  244.2 0.0 collective-permute-done.4
  244.2 1.1 fusion.10
  245.3 1.3 collective-permute-start.5
  246.6 0.0 collective-permute-start.6
  246.6 3.2 %collective-permute-start.7 = (f32[72,256]{1,0:T(8,128)S(1)}, f32[72,256]{1,0:T(8,128)S(1)}, u32[]{:S(2)}, u32[]{:S(2)}) collective-permute-start(f32[72,256]{1,0:T(8,128)S(1)} %get-tuple-element.16), channel_id=1, source_target_pairs={{0,6},{1,7},{2,4},{3,5},{4,2},{5,3},{6,0},{7,1},{8,14},{9,15},{10,... | collective-permute-start | bytes 221192 | tf_op jit(solution)/shard_map/ppermute | solution.py:360
  249.8 0.5 collective-permute-done.5
  250.2 4.0 %collective-permute-done.6 = f32[72,256]{1,0:T(8,128)S(1)} collective-permute-done((f32[72,256]{1,0:T(8,128)S(1)}, f32[72,256]{1,0:T(8,128)S(1)}, u32[]{:S(2)}, u32[]{:S(2)}) %collective-permute-start.6) | collective-permute-done | bytes 73760 | tf_op jit(solution)/shard_map/ppermute | solution.py:360
  254.3 0.0 collective-permute-done.7
  254.3 0.1 reshape.34
  254.4 0.0 copy-done
  254.4 0.6 fusion.14
  255.0 0.0 copy-done.1
  255.0 0.6 bitcast_add_fusion
  (3 shorter events, 0.0 us)
Async XLA Ops:
  7.2 185.2 %all-gather.3.cloned.1.call-start = ((), (), s32[]{:S(2)}) async-start(), calls=%async_computation.1 | async-start | bytes 8912896 | tf_op jit(solution)/shard_map/all_gather | solution.py:396
  17.1 175.9 %all-to-all-start = ((bf16[32,8,10496]{2,1,0:T(8,128)(2,1)}), bf16[32,8,10496]{2,1,0:T(8,128)(2,1)}, u32[]{:S(2)}, u32[]{:S(2)}) async-start(bf16[32,8,10496]{2,1,0:T(8,128)(2,1)} %bitcast.94), calls=%async_computation | async-start | bytes 10747904 | tf_op jit(solution)/shard_map/all_to_all | solution.py:409
  192.4 13.5 %collective-permute-start = (bf16[16,512,512]{2,1,0:T(8,128)(2,1)}, bf16[16,512,512]{2,1,0:T(8,128)(2,1)}, u32[]{:S(2)}, u32[]{:S(2)}) collective-permute-start(bf16[16,512,512]{2,1,0:T(8,128)(2,1)} %bitcast.95), channel_id=1, source_target_pairs={{0,8},{8,0},{16,24},{24,16},{1,9},{9,1},{17,25},{25,17},{2,10},{10... | collective-permute-start | bytes 25165832 | tf_op jit(solution)/shard_map/ppermute | solution.py:398
  224.3 3.1 %collective-permute-start.1 = (f32[2,8,72,256]{3,2,1,0:T(8,128)}, f32[2,8,72,256]{3,2,1,0:T(8,128)S(1)}, u32[]{:S(2)}, u32[]{:S(2)}) collective-permute-start(f32[2,8,72,256]{3,2,1,0:T(8,128)} %get-tuple-element.11), channel_id=1, source_target_pairs={{0,8},{8,0},{16,24},{24,16},{1,9},{9,1},{17,25},{25,17},{2,10},{10... | collective-permute-start | bytes 3538952 | tf_op jit(solution)/shard_map/ppermute | solution.py:461
  228.7 9.9 %collective-permute-start.2 = (f32[4,72,256]{2,1,0:T(8,128)S(1)}, f32[4,72,256]{2,1,0:T(8,128)S(1)}, u32[]{:S(2)}, u32[]{:S(2)}) collective-permute-start(f32[4,72,256]{2,1,0:T(8,128)S(1)} %get-tuple-element.12), channel_id=1, source_target_pairs={{0,1},{1,0},{2,3},{3,2},{4,5},{5,4},{6,7},{7,6},{8,9},{9,8},{10,11... | collective-permute-start | bytes 884744 | tf_op jit(solution)/shard_map/ppermute | solution.py:360
  228.8 15.4 %collective-permute-start.3 = (f32[4,72,256]{2,1,0:T(8,128)S(1)}, f32[4,72,256]{2,1,0:T(8,128)S(1)}, u32[]{:S(2)}, u32[]{:S(2)}) collective-permute-start(f32[4,72,256]{2,1,0:T(8,128)S(1)} %get-tuple-element.13), channel_id=1, source_target_pairs={{0,16},{1,17},{2,18},{3,19},{4,20},{5,21},{6,22},{7,23},{8,24},{9,... | collective-permute-start | bytes 884744 | tf_op jit(solution)/shard_map/ppermute | solution.py:360
  228.9 25.5 %copy-start = (f32[256,64]{0,1:T(8,128)S(1)}, f32[256,64]{0,1:T(8,128)}, u32[]{:S(2)}) copy-start(f32[256,64]{0,1:T(8,128)} %param.20) | copy-start | bytes 196612
  228.9 26.1 %copy-start.1 = (f32[64,32]{0,1:T(8,128)S(1)}, f32[64,32]{0,1:T(8,128)}, u32[]{:S(2)}) copy-start(f32[64,32]{0,1:T(8,128)} %param.21) | copy-start | bytes 24580
  228.9 15.3 %collective-permute-start.4 = (f32[4,72,256]{2,1,0:T(8,128)S(1)}, f32[4,72,256]{2,1,0:T(8,128)S(1)}, u32[]{:S(2)}, u32[]{:S(2)}) collective-permute-start(f32[4,72,256]{2,1,0:T(8,128)S(1)} %get-tuple-element.14), channel_id=1, source_target_pairs={{0,17},{1,16},{2,19},{3,18},{4,21},{5,20},{6,23},{7,22},{8,25},{9,... | collective-permute-start | bytes 884744 | tf_op jit(solution)/shard_map/ppermute | solution.py:360
  245.3 4.9 %collective-permute-start.5 = (f32[72,256]{1,0:T(8,128)S(1)}, f32[72,256]{1,0:T(8,128)S(1)}, u32[]{:S(2)}, u32[]{:S(2)}) collective-permute-start(f32[72,256]{1,0:T(8,128)S(1)} %get-tuple-element.15), channel_id=1, source_target_pairs={{0,2},{1,3},{2,0},{3,1},{4,6},{5,7},{6,4},{7,5},{8,10},{9,11},{10,... | collective-permute-start | bytes 221192 | tf_op jit(solution)/shard_map/ppermute | solution.py:360
  246.6 7.7 %collective-permute-start.6 = (f32[72,256]{1,0:T(8,128)S(1)}, f32[72,256]{1,0:T(8,128)S(1)}, u32[]{:S(2)}, u32[]{:S(2)}) collective-permute-start(f32[72,256]{1,0:T(8,128)S(1)} %get-tuple-element.17), channel_id=1, source_target_pairs={{0,4},{1,5},{2,6},{3,7},{4,0},{5,1},{6,2},{7,3},{8,12},{9,13},{10,... | collective-permute-start | bytes 221192 | tf_op jit(solution)/shard_map/ppermute | solution.py:360
  246.6 7.7 %collective-permute-start.7 = (f32[72,256]{1,0:T(8,128)S(1)}, f32[72,256]{1,0:T(8,128)S(1)}, u32[]{:S(2)}, u32[]{:S(2)}) collective-permute-start(f32[72,256]{1,0:T(8,128)S(1)} %get-tuple-element.16), channel_id=1, source_target_pairs={{0,6},{1,7},{2,4},{3,5},{4,2},{5,3},{6,0},{7,1},{8,14},{9,15},{10,... | collective-permute-start | bytes 221192 | tf_op jit(solution)/shard_map/ppermute | solution.py:360
Sparse Core Ops, SparseCore 0:
  9.5 182.7 all-gather.2

commit v6 on v5

--- a/solution.py
+++ b/solution.py
@@ -27,9 +27,23 @@
     return lax.broadcasted_iota(jnp.int32, shape, axis)
 
 
-def pack_kernel(users, most, count_ref, owner_ref, tokens_ref, targets_ref, out_ref):
+def pack_kernel(
+    users, most, count_ref, owner_ref, tokens_ref, targets_ref, out_ref, rows_ref, goals_ref,
+    packed_ref, in_sem, out_sem,
+):
     rows = tokens_ref.shape[0]
     groups, rest = divmod(most, SUB)
+    chunks = [
+        (source, held, source.shape[1] // SUB, part)
+        for source, held in ((tokens_ref, rows_ref), (targets_ref, goals_ref))
+        for part in range(SUB)
+    ]
+    loads = []
+    for place, (source, held, piece, part) in enumerate(chunks):
+        lanes = pl.ds(part * piece, piece)
+        copy = pltpu.make_async_copy(source.at[:, lanes], held.at[:, lanes], in_sem.at[place])
+        copy.start()
+        loads.append(copy)
     owner_row = owner_ref[...]
     first, second = (iota((rows, rows), 0), iota((rows, rows), 1))
     owner = jnp.sum(jnp.where(first == second, owner_row, 0), axis=1, keepdims=True)
@@ -38,32 +52,48 @@
     line = iota((users * SUB, rows), 0)
     mine = line // SUB == owner_row
     slot = line % SUB
+    stores = []
+
+    def store(first, size):
+        lanes = pl.ds(first, size)
+        copy = pltpu.make_async_copy(
+            packed_ref.at[:, lanes], out_ref.at[:, lanes], out_sem.at[len(stores)]
+        )
+        copy.start()
+        stores.append(copy)
+
     column = 0
-    for source in (tokens_ref, targets_ref):
+    place = 0
+    for source in (rows_ref, goals_ref):
         width = source.shape[1]
-        for group in range(groups):
-            pick = (mine & (rank == slot + group * SUB)).astype(BF16)
-            step = min(width, 1024)
-            for at in range(0, width, step):
-                out_ref[:, column + at : column + at + step] = dot(
-                    pick, source[:, at : at + step]
-                ).astype(BF16)
-            column += width
         piece = width // SUB
-        for extra in range(rest):
-            here = mine & (rank == groups * SUB + extra)
-            total = None
-            for part in range(SUB):
-                pick = (here & (slot == part)).astype(BF16)
-                term = dot(pick, source[:, part * piece : (part + 1) * piece])
-                total = term if total is None else total + term
-            out_ref[:, column : column + piece] = total.astype(BF16)
+        totals = [None] * rest
+        for part in range(SUB):
+            loads[place].wait()
+            place += 1
+            values = source[:, part * piece : (part + 1) * piece]
+            for group in range(groups):
+                pick = (mine & (rank == slot + group * SUB)).astype(BF16)
+                spot = column + group * width + part * piece
+                packed_ref[:, spot : spot + piece] = dot(pick, values).astype(BF16)
+                store(spot, piece)
+            for extra in range(rest):
+                here = mine & (rank == groups * SUB + extra)
+                term = dot((here & (slot == part)).astype(BF16), values)
+                totals[extra] = term if totals[extra] is None else totals[extra] + term
+        column += groups * width
+        for total in totals:
+            packed_ref[:, column : column + piece] = total.astype(BF16)
+            store(column, piece)
             column += piece
     used = mine & (iota((users * SUB, rows), 1) < count_ref[0])
     number = jnp.sum(used.astype(F32), axis=1, keepdims=True)
-    out_ref[:, column : column + LANES] = jnp.broadcast_to(number, (users * SUB, LANES)).astype(
-        BF16
-    )
+    packed_ref[:, column : column + LANES] = jnp.broadcast_to(
+        number, (users * SUB, LANES)
+    ).astype(BF16)
+    store(column, LANES)
+    for copy in stores:
+        copy.wait()
 
 
 def weight_rings(groups, members):
@@ -112,28 +142,12 @@
         pltpu.make_async_copy(block, block, sems.at[place, pair]).wait()
 
 
-def near_kernel(
-    groups_of,
-    members,
-    most,
-    got_ref,
-    near_ref,
-    down_ref,
-    x_out_ref,
-    frozen_ref,
-    hidden_ref,
-    x_ref,
-    cut_ref,
-    w_ref,
-    got_sem,
-    out_sem,
-    w_sem,
+def rows_kernel(
+    devices, most, got_ref, down_ref, x_out_ref, hidden_ref, x_ref, cut_ref, got_sem, out_sem
 ):
     groups, rest = divmod(most, SUB)
-    devices = groups_of * members
     width = x_ref.shape[1]
     whole = devices * SUB
-    half = w_ref.shape[1]
     copies = []
     column = 0
     for group in range(groups):
@@ -150,31 +164,46 @@
     ]
     for copy in copies:
         copy.start()
-    weights = weight_copies(0, groups_of, members, near_ref, w_ref, w_sem)
-    for place, pieces in enumerate(weights):
-        if place == 2:
-            for copy in copies:
-                copy.wait()
-        for copy in pieces:
-            copy.start()
+    for copy in copies:
+        copy.wait()
     join_pieces(devices, groups * whole, rest, x_ref, cut_ref)
     out = pltpu.make_async_copy(x_ref, x_out_ref, out_sem)
     out.start()
-
+    hidden_ref[...] = jnp.zeros_like(hidden_ref)
+    block = min(width, 1024)
+
+    def add_block(at, unused):
+        lanes = pl.ds(pl.multiple_of(at * block, block), block)
+        hidden_ref[...] += dot(x_ref[:, lanes], down_ref[:, lanes], ((1,), (1,)))
+        return unused
+
+    lax.fori_loop(0, width // block, add_block, 0, unroll=4)
+    out.wait()
+
+
+def near_kernel(groups_of, members, rows_ref, near_ref, frozen_ref, x_ref, w_ref, x_sem, w_sem):
+    half = w_ref.shape[1]
+    side = lax.rem(lax.axis_index("grp"), 2)
+    weights = weight_copies(0, groups_of, members, near_ref, w_ref, w_sem)
+
+    def row_copy(shard):
+        lanes = pl.ds(pl.multiple_of((2 * shard + side) * half, half), half)
+        return pltpu.make_async_copy(rows_ref.at[:, lanes], x_ref.at[:, lanes], x_sem.at[shard])
+
+    for shard, copies in enumerate(weights):
+        row_copy(shard).start()
+        for copy in copies:
+            copy.start()
     frozen_ref[...] = jnp.zeros_like(frozen_ref)
-    hidden_ref[...] = jnp.zeros_like(hidden_ref)
-    side = lax.rem(lax.axis_index("grp"), 2)
 
     def add_shard(shard, unused):
+        row_copy(shard).wait()
         wait_block(w_ref, shard, groups_of // 2, w_sem)
         near = pl.ds(pl.multiple_of((2 * shard + side) * half, half), half)
-        both = pl.ds(pl.multiple_of(2 * shard * half, 2 * half), 2 * half)
         frozen_ref[...] += dot(x_ref[:, near], w_ref[shard])
-        hidden_ref[...] += dot(x_ref[:, both], down_ref[:, both], ((1,), (1,)))
         return unused
 
-    lax.fori_loop(0, members, add_shard, 0, unroll=2)
-    out.wait()
+    lax.fori_loop(0, members, add_shard, 0, unroll=4)
 
 
 def join_pieces(devices, bottom, rest, full, cut):
@@ -278,7 +307,7 @@
         frozen_ref[...] += dot(x_ref[:, far], w_ref[shard])
         return unused
 
-    lax.fori_loop(0, members, add_shard, 0, unroll=2)
+    lax.fori_loop(0, members, add_shard, 0, unroll=4)
 
     rate = ADAPTER_SCALE * LEARN_RATE
     block = min(width, 1024)
@@ -312,7 +341,7 @@
             return unused
 
         squares = lax.fori_loop(
-            0, width // block, down_block, jnp.zeros((rank, LANES), F32), unroll=2
+            0, width // block, down_block, jnp.zeros((rank, LANES), F32), unroll=4
         )
 
     total = jnp.sum(squares) + jnp.sum(up_delta * up_delta) + EPSILON
@@ -389,6 +418,7 @@
     vmem = pl.BlockSpec(memory_space=pltpu.VMEM)
     anywhere = pl.BlockSpec(memory_space=pl.ANY)
 
+    params = pltpu.CompilerParams(vmem_limit_bytes=VMEM_BYTES)
     half = value_weight.shape[0] // 2
     piece = kv_width // (groups // 2)
     pair = lax.axis_index("grp") // 2
@@ -401,9 +431,16 @@
     packed = pl.pallas_call(
         lambda *refs: pack_kernel(users, most, *refs),
         out_shape=jax.ShapeDtypeStruct((users * SUB, columns), BF16),
-        in_specs=[smem, vmem, vmem, vmem],
-        out_specs=vmem,
-        compiler_params=pltpu.CompilerParams(vmem_limit_bytes=VMEM_BYTES),
+        in_specs=[smem, vmem, anywhere, anywhere],
+        out_specs=anywhere,
+        scratch_shapes=[
+            pltpu.VMEM((per_dev, width), BF16),
+            pltpu.VMEM((per_dev, kv_width), BF16),
+            pltpu.VMEM((users * SUB, columns), BF16),
+            pltpu.SemaphoreType.DMA((2 * SUB,)),
+            pltpu.SemaphoreType.DMA((2 * (SUB * whole_groups + rest) + 1,)),
+        ],
+        compiler_params=params,
         name="pack_rows",
     )(device_row_count, row_owner_user.reshape(1, per_dev), tokens, targets)
     got = lax.all_to_all(
@@ -412,29 +449,40 @@
     share = width // devices
     tall = rank + kv_width // devices * rank // share
     down = adapter_down.T
-    rows, near_frozen, near_hidden = pl.pallas_call(
-        lambda *refs: near_kernel(groups, members, most, *refs),
+    rows, hidden = pl.pallas_call(
+        lambda *refs: rows_kernel(devices, most, *refs),
         out_shape=[
             jax.ShapeDtypeStruct((slots, width), BF16),
-            jax.ShapeDtypeStruct((slots, kv_width), F32),
             jax.ShapeDtypeStruct((slots, rank), F32),
         ],
-        in_specs=[anywhere, anywhere, vmem],
-        out_specs=[anywhere, vmem, vmem],
+        in_specs=[anywhere, vmem],
+        out_specs=[anywhere, vmem],
         scratch_shapes=[
             pltpu.VMEM((slots, width), BF16),
             pltpu.VMEM((max(rest, 1), whole, width // SUB), BF16),
-            pltpu.VMEM((members, half, kv_width), BF16),
             pltpu.SemaphoreType.DMA((whole_groups + rest,)),
             pltpu.SemaphoreType.DMA,
+        ],
+        compiler_params=params,
+        name="join_rows",
+    )(got, down)
+    near_frozen = pl.pallas_call(
+        lambda *refs: near_kernel(groups, members, *refs),
+        out_shape=jax.ShapeDtypeStruct((slots, kv_width), F32),
+        in_specs=[anywhere, anywhere],
+        out_specs=vmem,
+        scratch_shapes=[
+            pltpu.VMEM((slots, width), BF16),
+            pltpu.VMEM((members, half, kv_width), BF16),
+            pltpu.SemaphoreType.DMA((members,)),
             pltpu.SemaphoreType.DMA((members, groups // 2)),
         ],
-        compiler_params=pltpu.CompilerParams(vmem_limit_bytes=VMEM_BYTES),
+        compiler_params=params,
         cost_estimate=pl.CostEstimate(
             flops=slots * width * kv_width, bytes_accessed=3 * 10**7, transcendentals=0
         ),
         name="near_product",
-    )(got, near, down)
+    )(rows, near)
 
     package = jax.ShapeDtypeStruct((groups // 2, members, tall, share), F32)
     keep, send = pl.pallas_call(
@@ -454,9 +502,9 @@
             pltpu.SemaphoreType.DMA((whole_groups + rest + 2,)),
             pltpu.SemaphoreType.DMA((members, groups // 2)),
         ],
-        compiler_params=pltpu.CompilerParams(vmem_limit_bytes=VMEM_BYTES),
+        compiler_params=params,
         name="user_steps",
-    )(user_row_cap, clip_norm_bound, got, rows, near_frozen, near_hidden, far, down, adapter_up)
+    )(user_row_cap, clip_norm_bound, got, rows, near_frozen, hidden, far, down, adapter_up)
 
     other = lax.ppermute(send, "grp", swap)
     keep = keep.reshape(groups // 2, members // 2, 2, tall, share)

time: 263 us -> 264 us (level)
    pallas_call x1 -> x2, Pallas kernels: 10.7 us -> 13.8 us  [the longest x1 7.21 us: body(): pl.pallas_call(lambda *refs: rows_kernel(devices, most, *refs), out_shape...]
  transfers between devices with their start and end apart: 10 -> 10, of which waited for: 7 -> 6; matrix products, arithmetic and copies ran while one was open for 0% -> 0% of each run, Pallas kernels for 7% -> 8%
where the time goes in v6:
time: 264 us; the launch traced here: 263 us
  waiting for transfers between devices  188 us (71%)
  Pallas kernels  38.7 us (15%)
  starting transfers between devices  16 us (6%)
  between operations  15.5 us (6%)
  other arithmetic  3.58 us (1%)
    all_gather x1, waiting for transfers between devices, body(): lax.all_gather(mine, BOTH, axis=0, axis_index_groups=weight_rings(groups,...  168 us
    pallas_call x1, Pallas kernels, body(): pl.pallas_call(lambda *refs: user_kernel(groups, members, most, *refs), o...  17.6 us
    ppermute x6, waiting for transfers between devices, exchange(): total = total + lax.ppermute(blocks[place], BOTH, pairs)  16.6 us
    ppermute x6, starting transfers between devices, exchange(): total = total + lax.ppermute(blocks[place], BOTH, pairs)  7.98 us
    all_to_all x1, starting transfers between devices, body(): lax.all_to_all(packed.reshape(users, SUB, columns), BOTH, split_axis=0, c...  7.42 us
    pallas_call x1, Pallas kernels, body(): pl.pallas_call(lambda *refs: pack_kernel(users, most, *refs), out_shape=j...  7.28 us
    pallas_call x1, Pallas kernels, body(): pl.pallas_call(lambda *refs: rows_kernel(devices, most, *refs), out_shape...  7.21 us
    pallas_call x1, Pallas kernels, body(): pl.pallas_call(lambda *refs: near_kernel(groups, members, *refs), out_sha...  6.6 us
  transfers between devices with their start and end apart: 10, of which 6 were waited for; matrix products, arithmetic and copies ran while one was open for 0% of the time, Pallas kernels for 8%

profile of v6, /device:TPU:0, one launch (start us, length us, event | category | flops | bytes accessed | tf_op | source)
XLA Modules:
  0.0 263.3 jit_solution(18366843423604557734)
XLA Ops:
  7.2 0.0 all-gather.3.cloned.1.call-start
  7.2 1.9 dynamic_slice.3
  9.2 0.0 all-gather.3.cloned.1.call-update
  9.8 7.3 %pack_rows.1 = bf16[256,10496]{1,0:T(8,128)(2,1)} custom-call(s32[1]{0:T(128)S(6)} %copy.31.refs_0_, s32[1,192]{1,0:T(1,128)} %bitcast.103, bf16[192,8192]{1,0:T(8,128)(2,1)} %refs_2_.1, bf16[192,1024]{1,0:T(8,128)(2,1)} %refs_3_.1), custom_call_target="tpu_custom_call" | custom-call | tf_op jit(solution)/shard_map/pack_rows/pallas_call | solution.py:431
  17.1 7.4 %all-to-all-start = ((bf16[32,8,10496]{2,1,0:T(8,128)(2,1)}), bf16[32,8,10496]{2,1,0:T(8,128)(2,1)}, u32[]{:S(2)}, u32[]{:S(2)}) async-start(bf16[32,8,10496]{2,1,0:T(8,128)(2,1)} %bitcast.94), calls=%async_computation | async-start | bytes 10747904 | tf_op jit(solution)/shard_map/all_to_all | solution.py:446
  24.5 168.2 %all-gather.3.cloned.1.call-done = bf16[8192,512]{1,0:T(8,128)(2,1)} async-done(((bf16[512,512]{1,0:T(8,128)(2,1)}), bf16[8192,512]{1,0:T(8,128)(2,1)}) %all-gather.3.cloned.1.call-update) | async-done | bytes 8388624 | tf_op jit(solution)/shard_map/all_gather | solution.py:426
  192.7 0.0 collective-permute-start
  193.4 0.0 all-to-all-done
  193.4 7.2 %join_rows.1 = (bf16[288,8192]{1,0:T(8,128)(2,1)}, f32[288,64]{1,0:T(8,128)}) custom-call(bf16[256,10496]{1,0:T(8,128)(2,1)} %bitcast.2.refs_0_.refs_2_, bf16[64,8192]{1,0:T(8,128)(2,1)} %bitcast.97), custom_call_target="tpu_custom_call" | custom-call | tf_op jit(solution)/shard_map/join_rows/pallas_call | solution.py:452
  200.6 6.6 %near_product.1.refs_4_ = f32[288,1024]{1,0:T(8,128)} custom-call(bf16[288,8192]{1,0:T(8,128)(2,1)} %get-tuple-element.6.refs_0_.refs_3_, bf16[16,512,512]{2,1,0:T(8,128)(2,1)} %bitcast.96), custom_call_target="tpu_custom_call" | custom-call | flops 2415919104 | bytes 30000000 | tf_op jit(solution)/shard_map/near_product/pallas_call | solution.py:469
  207.2 0.0 collective-permute-done.refs_6_
  207.2 17.6 %user_steps.1 = (f32[2,8,72,256]{3,2,1,0:T(8,128)}, f32[2,8,72,256]{3,2,1,0:T(8,128)}) custom-call(s32[32]{0:T(128)} %refs_0_.2, f32[1]{0:T(128)} %copy.32.refs_1_, bf16[256,10496]{1,0:T(8,128)(2,1)} %bitcast.2.refs_0_.refs_2_, bf16[288,8192]{1,0:T(8,128)(2,1)} %get-tuple-element.6.refs_0_.refs_3_, f32[288,1024]{1,0:T(8,128)} %near_product.1.refs_4_, ...), custom_call_target="tpu_custom_call" | custom-call | tf_op jit(solution)/shard_map/user_steps/pallas_call | solution.py:488
  224.8 0.6 collective-permute-start.1
  225.4 2.7 %collective-permute-done.1 = f32[2,8,72,256]{3,2,1,0:T(8,128)S(1)} collective-permute-done((f32[2,8,72,256]{3,2,1,0:T(8,128)}, f32[2,8,72,256]{3,2,1,0:T(8,128)S(1)}, u32[]{:S(2)}, u32[]{:S(2)}) %collective-permute-start.1) | collective-permute-done | bytes 1179680 | tf_op jit(solution)/shard_map/ppermute | solution.py:509
  228.1 1.3 fusion.5
  229.3 0.1 collective-permute-start.2
  229.4 0.1 collective-permute-start.3
  229.5 0.0 copy-start
  229.5 0.0 copy-start.1
  229.5 3.4 %collective-permute-start.4 = (f32[4,72,256]{2,1,0:T(8,128)S(1)}, f32[4,72,256]{2,1,0:T(8,128)S(1)}, u32[]{:S(2)}, u32[]{:S(2)}) collective-permute-start(f32[4,72,256]{2,1,0:T(8,128)S(1)} %get-tuple-element.12), channel_id=1, source_target_pairs={{0,17},{1,16},{2,19},{3,18},{4,21},{5,20},{6,23},{7,22},{8,25},{9,... | collective-permute-start | bytes 884744 | tf_op jit(solution)/shard_map/ppermute | solution.py:389
  232.9 6.3 %collective-permute-done.2 = f32[4,72,256]{2,1,0:T(8,128)S(1)} collective-permute-done((f32[4,72,256]{2,1,0:T(8,128)S(1)}, f32[4,72,256]{2,1,0:T(8,128)S(1)}, u32[]{:S(2)}, u32[]{:S(2)}) %collective-permute-start.2) | collective-permute-done | bytes 294944 | tf_op jit(solution)/shard_map/ppermute | solution.py:389
  239.2 5.8 %collective-permute-done.3 = f32[4,72,256]{2,1,0:T(8,128)S(1)} collective-permute-done((f32[4,72,256]{2,1,0:T(8,128)S(1)}, f32[4,72,256]{2,1,0:T(8,128)S(1)}, u32[]{:S(2)}, u32[]{:S(2)}) %collective-permute-start.3) | collective-permute-done | bytes 294944 | tf_op jit(solution)/shard_map/ppermute | solution.py:389
  245.1 0.0 collective-permute-done.4
  245.1 1.1 fusion.10
  246.2 1.1 collective-permute-start.5
  247.2 0.0 collective-permute-start.6
  247.2 3.4 %collective-permute-start.7 = (f32[72,256]{1,0:T(8,128)S(1)}, f32[72,256]{1,0:T(8,128)S(1)}, u32[]{:S(2)}, u32[]{:S(2)}) collective-permute-start(f32[72,256]{1,0:T(8,128)S(1)} %get-tuple-element.14), channel_id=1, source_target_pairs={{0,6},{1,7},{2,4},{3,5},{4,2},{5,3},{6,0},{7,1},{8,14},{9,15},{10,... | collective-permute-start | bytes 221192 | tf_op jit(solution)/shard_map/ppermute | solution.py:389
  250.6 0.5 collective-permute-done.5
  251.1 3.9 %collective-permute-done.6 = f32[72,256]{1,0:T(8,128)S(1)} collective-permute-done((f32[72,256]{1,0:T(8,128)S(1)}, f32[72,256]{1,0:T(8,128)S(1)}, u32[]{:S(2)}, u32[]{:S(2)}) %collective-permute-start.6) | collective-permute-done | bytes 73760 | tf_op jit(solution)/shard_map/ppermute | solution.py:389
  255.1 0.0 collective-permute-done.7
  255.1 0.1 reshape.34
  255.2 0.0 copy-done
  255.2 0.6 fusion.14
  255.8 0.0 copy-done.1
  255.8 0.6 bitcast_add_fusion
  (3 shorter events, 0.0 us)
Async XLA Ops:
  7.2 185.6 %all-gather.3.cloned.1.call-start = ((), (), s32[]{:S(2)}) async-start(), calls=%async_computation.1 | async-start | bytes 8912896 | tf_op jit(solution)/shard_map/all_gather | solution.py:426
  17.1 176.3 %all-to-all-start = ((bf16[32,8,10496]{2,1,0:T(8,128)(2,1)}), bf16[32,8,10496]{2,1,0:T(8,128)(2,1)}, u32[]{:S(2)}, u32[]{:S(2)}) async-start(bf16[32,8,10496]{2,1,0:T(8,128)(2,1)} %bitcast.94), calls=%async_computation | async-start | bytes 10747904 | tf_op jit(solution)/shard_map/all_to_all | solution.py:446
  192.7 14.5 %collective-permute-start = (bf16[16,512,512]{2,1,0:T(8,128)(2,1)}, bf16[16,512,512]{2,1,0:T(8,128)(2,1)}, u32[]{:S(2)}, u32[]{:S(2)}) collective-permute-start(bf16[16,512,512]{2,1,0:T(8,128)(2,1)} %bitcast.95), channel_id=1, source_target_pairs={{0,8},{8,0},{16,24},{24,16},{1,9},{9,1},{17,25},{25,17},{2,10},{10... | collective-permute-start | bytes 25165832 | tf_op jit(solution)/shard_map/ppermute | solution.py:428
  224.8 3.3 %collective-permute-start.1 = (f32[2,8,72,256]{3,2,1,0:T(8,128)}, f32[2,8,72,256]{3,2,1,0:T(8,128)S(1)}, u32[]{:S(2)}, u32[]{:S(2)}) collective-permute-start(f32[2,8,72,256]{3,2,1,0:T(8,128)} %get-tuple-element.9), channel_id=1, source_target_pairs={{0,8},{8,0},{16,24},{24,16},{1,9},{9,1},{17,25},{25,17},{2,10},{10... | collective-permute-start | bytes 3538952 | tf_op jit(solution)/shard_map/ppermute | solution.py:509
  229.3 9.9 %collective-permute-start.2 = (f32[4,72,256]{2,1,0:T(8,128)S(1)}, f32[4,72,256]{2,1,0:T(8,128)S(1)}, u32[]{:S(2)}, u32[]{:S(2)}) collective-permute-start(f32[4,72,256]{2,1,0:T(8,128)S(1)} %get-tuple-element.10), channel_id=1, source_target_pairs={{0,1},{1,0},{2,3},{3,2},{4,5},{5,4},{6,7},{7,6},{8,9},{9,8},{10,11... | collective-permute-start | bytes 884744 | tf_op jit(solution)/shard_map/ppermute | solution.py:389
  229.4 15.7 %collective-permute-start.3 = (f32[4,72,256]{2,1,0:T(8,128)S(1)}, f32[4,72,256]{2,1,0:T(8,128)S(1)}, u32[]{:S(2)}, u32[]{:S(2)}) collective-permute-start(f32[4,72,256]{2,1,0:T(8,128)S(1)} %get-tuple-element.11), channel_id=1, source_target_pairs={{0,16},{1,17},{2,18},{3,19},{4,20},{5,21},{6,22},{7,23},{8,24},{9,... | collective-permute-start | bytes 884744 | tf_op jit(solution)/shard_map/ppermute | solution.py:389
  229.5 25.7 %copy-start = (f32[256,64]{0,1:T(8,128)S(1)}, f32[256,64]{0,1:T(8,128)}, u32[]{:S(2)}) copy-start(f32[256,64]{0,1:T(8,128)} %param.20) | copy-start | bytes 196612
  229.5 26.3 %copy-start.1 = (f32[64,32]{0,1:T(8,128)S(1)}, f32[64,32]{0,1:T(8,128)}, u32[]{:S(2)}) copy-start(f32[64,32]{0,1:T(8,128)} %param.21) | copy-start | bytes 24580
  229.5 15.6 %collective-permute-start.4 = (f32[4,72,256]{2,1,0:T(8,128)S(1)}, f32[4,72,256]{2,1,0:T(8,128)S(1)}, u32[]{:S(2)}, u32[]{:S(2)}) collective-permute-start(f32[4,72,256]{2,1,0:T(8,128)S(1)} %get-tuple-element.12), channel_id=1, source_target_pairs={{0,17},{1,16},{2,19},{3,18},{4,21},{5,20},{6,23},{7,22},{8,25},{9,... | collective-permute-start | bytes 884744 | tf_op jit(solution)/shard_map/ppermute | solution.py:389
  246.2 5.0 %collective-permute-start.5 = (f32[72,256]{1,0:T(8,128)S(1)}, f32[72,256]{1,0:T(8,128)S(1)}, u32[]{:S(2)}, u32[]{:S(2)}) collective-permute-start(f32[72,256]{1,0:T(8,128)S(1)} %get-tuple-element.13), channel_id=1, source_target_pairs={{0,2},{1,3},{2,0},{3,1},{4,6},{5,7},{6,4},{7,5},{8,10},{9,11},{10,... | collective-permute-start | bytes 221192 | tf_op jit(solution)/shard_map/ppermute | solution.py:389
  247.2 7.8 %collective-permute-start.6 = (f32[72,256]{1,0:T(8,128)S(1)}, f32[72,256]{1,0:T(8,128)S(1)}, u32[]{:S(2)}, u32[]{:S(2)}) collective-permute-start(f32[72,256]{1,0:T(8,128)S(1)} %get-tuple-element.15), channel_id=1, source_target_pairs={{0,4},{1,5},{2,6},{3,7},{4,0},{5,1},{6,2},{7,3},{8,12},{9,13},{10,... | collective-permute-start | bytes 221192 | tf_op jit(solution)/shard_map/ppermute | solution.py:389
  247.2 7.8 %collective-permute-start.7 = (f32[72,256]{1,0:T(8,128)S(1)}, f32[72,256]{1,0:T(8,128)S(1)}, u32[]{:S(2)}, u32[]{:S(2)}) collective-permute-start(f32[72,256]{1,0:T(8,128)S(1)} %get-tuple-element.14), channel_id=1, source_target_pairs={{0,6},{1,7},{2,4},{3,5},{4,2},{5,3},{6,0},{7,1},{8,14},{9,15},{10,... | collective-permute-start | bytes 221192 | tf_op jit(solution)/shard_map/ppermute | solution.py:389
Sparse Core Ops, SparseCore 0:
  9.5 183.1 all-gather.2

commit v7 on v6

--- a/solution.py
+++ b/solution.py
@@ -27,23 +27,20 @@
     return lax.broadcasted_iota(jnp.int32, shape, axis)
 
 
-def pack_kernel(
-    users, most, count_ref, owner_ref, tokens_ref, targets_ref, out_ref, rows_ref, goals_ref,
-    packed_ref, in_sem, out_sem,
-):
-    rows = tokens_ref.shape[0]
-    groups, rest = divmod(most, SUB)
-    chunks = [
-        (source, held, source.shape[1] // SUB, part)
-        for source, held in ((tokens_ref, rows_ref), (targets_ref, goals_ref))
-        for part in range(SUB)
-    ]
+def pack_kernel(users, most, part_of, with_goals, count_ref, owner_ref, *refs):
+    tokens_ref, targets_ref, out_ref, rows_ref, sems = refs
+    rows, size = rows_ref.shape
+    block = size // sems.shape[0]
     loads = []
-    for place, (source, held, piece, part) in enumerate(chunks):
-        lanes = pl.ds(part * piece, piece)
-        copy = pltpu.make_async_copy(source.at[:, lanes], held.at[:, lanes], in_sem.at[place])
+    for place in range(sems.shape[0]):
+        copy = pltpu.make_async_copy(
+            tokens_ref.at[:, pl.ds((2 * place + part_of) * block, block)],
+            rows_ref.at[:, pl.ds(place * block, block)],
+            sems.at[place],
+        )
         copy.start()
         loads.append(copy)
+    groups, rest = divmod(most, SUB)
     owner_row = owner_ref[...]
     first, second = (iota((rows, rows), 0), iota((rows, rows), 1))
     owner = jnp.sum(jnp.where(first == second, owner_row, 0), axis=1, keepdims=True)
@@ -52,48 +49,38 @@
     line = iota((users * SUB, rows), 0)
     mine = line // SUB == owner_row
     slot = line % SUB
-    stores = []
-
-    def store(first, size):
-        lanes = pl.ds(first, size)
-        copy = pltpu.make_async_copy(
-            packed_ref.at[:, lanes], out_ref.at[:, lanes], out_sem.at[len(stores)]
-        )
-        copy.start()
-        stores.append(copy)
-
+    whole_picks = [
+        (mine & (rank == slot + group * SUB)).astype(BF16) for group in range(groups)
+    ]
+    rest_picks = [
+        [(mine & (rank == groups * SUB + extra) & (slot == part)).astype(BF16) for part in range(SUB)]
+        for extra in range(rest)
+    ]
+    for copy in loads:
+        copy.wait()
     column = 0
-    place = 0
-    for source in (rows_ref, goals_ref):
+    for source in (rows_ref, targets_ref) if with_goals else (rows_ref,):
         width = source.shape[1]
         piece = width // SUB
         totals = [None] * rest
         for part in range(SUB):
-            loads[place].wait()
-            place += 1
             values = source[:, part * piece : (part + 1) * piece]
             for group in range(groups):
-                pick = (mine & (rank == slot + group * SUB)).astype(BF16)
                 spot = column + group * width + part * piece
-                packed_ref[:, spot : spot + piece] = dot(pick, values).astype(BF16)
-                store(spot, piece)
+                out_ref[:, spot : spot + piece] = dot(whole_picks[group], values).astype(BF16)
             for extra in range(rest):
-                here = mine & (rank == groups * SUB + extra)
-                term = dot((here & (slot == part)).astype(BF16), values)
+                term = dot(rest_picks[extra][part], values)
                 totals[extra] = term if totals[extra] is None else totals[extra] + term
         column += groups * width
         for total in totals:
-            packed_ref[:, column : column + piece] = total.astype(BF16)
-            store(column, piece)
+            out_ref[:, column : column + piece] = total.astype(BF16)
             column += piece
-    used = mine & (iota((users * SUB, rows), 1) < count_ref[0])
-    number = jnp.sum(used.astype(F32), axis=1, keepdims=True)
-    packed_ref[:, column : column + LANES] = jnp.broadcast_to(
-        number, (users * SUB, LANES)
-    ).astype(BF16)
-    store(column, LANES)
-    for copy in stores:
-        copy.wait()
+    if with_goals:
+        used = mine & (iota((users * SUB, rows), 1) < count_ref[0])
+        number = jnp.sum(used.astype(F32), axis=1, keepdims=True)
+        out_ref[:, column : column + LANES] = jnp.broadcast_to(
+            number, (users * SUB, LANES)
+        ).astype(BF16)
 
 
 def weight_rings(groups, members):
@@ -117,9 +104,9 @@
     return rings
 
 
-def weight_copies(ring_of, groups, members, source, target, sems):
+def weight_copies(ring_of, groups, members, source, target, sems, first=0):
     pairs = groups // 2
-    columns = source.shape[2]
+    depth, columns = source.shape[1:]
     side = lax.rem(lax.axis_index("grp"), 2)
     rings = weight_rings(groups, members)
 
@@ -128,18 +115,18 @@
         spot = jnp.where(side == ring_of, spots[0], spots[1])
         return pltpu.make_async_copy(
             source.at[spot],
-            target.at[member, :, pl.ds(pair * columns, columns)],
+            target.at[member, pl.ds(first, depth), pl.ds(pair * columns, columns)],
             sems.at[member, pair],
         )
 
     return [[copy(member, pair) for pair in range(pairs)] for member in range(members)]
 
 
-def wait_block(target, place, pairs, sems):
-    columns = target.shape[2] // pairs
+def wait_block(target, pairs, sems):
+    columns = target.shape[1] // pairs
     for pair in range(pairs):
-        block = target.at[place, :, pl.ds(pair * columns, columns)]
-        pltpu.make_async_copy(block, block, sems.at[place, pair]).wait()
+        block = target.at[:, pl.ds(pair * columns, columns)]
+        pltpu.make_async_copy(block, block, sems.at[pair]).wait()
 
 
 def rows_kernel(
@@ -181,29 +168,36 @@
     out.wait()
 
 
-def near_kernel(groups_of, members, rows_ref, near_ref, frozen_ref, x_ref, w_ref, x_sem, w_sem):
-    half = w_ref.shape[1]
+def near_kernel(groups_of, members, *refs):
+    *before, rows_ref, near_ref, frozen_ref, x_ref, w_ref, x_sem, w_sem = refs
+    depth = w_ref.shape[1]
     side = lax.rem(lax.axis_index("grp"), 2)
     weights = weight_copies(0, groups_of, members, near_ref, w_ref, w_sem)
 
+    def near(shard):
+        return pl.ds(pl.multiple_of((2 * shard + side) * depth, depth), depth)
+
     def row_copy(shard):
-        lanes = pl.ds(pl.multiple_of((2 * shard + side) * half, half), half)
+        lanes = near(shard)
         return pltpu.make_async_copy(rows_ref.at[:, lanes], x_ref.at[:, lanes], x_sem.at[shard])
 
     for shard, copies in enumerate(weights):
         row_copy(shard).start()
         for copy in copies:
             copy.start()
-    frozen_ref[...] = jnp.zeros_like(frozen_ref)
-
-    def add_shard(shard, unused):
-        row_copy(shard).wait()
-        wait_block(w_ref, shard, groups_of // 2, w_sem)
-        near = pl.ds(pl.multiple_of((2 * shard + side) * half, half), half)
-        frozen_ref[...] += dot(x_ref[:, near], w_ref[shard])
+    frozen_ref[...] = before[0][...] if before else jnp.zeros_like(frozen_ref)
+
+    def add_shards(pair, unused):
+        total = None
+        for shard in (2 * pair, 2 * pair + 1):
+            row_copy(shard).wait()
+            wait_block(w_ref.at[shard], groups_of // 2, w_sem.at[shard])
+            term = dot(x_ref[:, near(shard)], w_ref[shard])
+            total = term if total is None else total + term
+        frozen_ref[...] += total
         return unused
 
-    lax.fori_loop(0, members, add_shard, 0, unroll=4)
+    lax.fori_loop(0, members // 2, add_shards, 0, unroll=2)
 
 
 def join_pieces(devices, bottom, rest, full, cut):
@@ -225,10 +219,10 @@
     cap_ref,
     clip_ref,
     got_ref,
-    rows_ref,
+    rows_refs,
     near_frozen_ref,
-    near_hidden_ref,
-    far_ref,
+    hidden_refs,
+    far_refs,
     down_ref,
     up_ref,
     *refs,
@@ -252,8 +246,12 @@
     kv_width = up_ref.shape[1]
     whole = devices * SUB
     half = w_ref.shape[1]
-    copies = [(rows_ref, x_ref)]
-    column = groups * width + rest * width // SUB
+    depth = half // 2
+    size = width // 2
+    copies = [
+        (source, x_ref.at[:, pl.ds(place * size, size)]) for place, source in enumerate(rows_refs)
+    ]
+    column = groups * size + rest * size // SUB
     for group in range(groups):
         copies.append(
             (got_ref.at[:, pl.ds(column, kv_width)], goal_ref.at[pl.ds(group * whole, whole), :])
@@ -267,12 +265,16 @@
         pltpu.make_async_copy(source, target, got_sem.at[place])
         for place, (source, target) in enumerate(copies)
     ]
-    for copy in copies[1:] + copies[:1]:
+    for copy in copies[2:] + copies[:2]:
         copy.start()
-    for pieces in weight_copies(1, groups_of, members, far_ref, w_ref, w_sem):
-        for copy in pieces:
+    weights = [
+        weight_copies(1, groups_of, members, far, w_ref, w_sem.at[place], place * depth)
+        for place, far in enumerate(far_refs)
+    ]
+    for shard in range(members):
+        for copy in weights[0][shard] + weights[1][shard]:
             copy.start()
-    for copy in copies[1:]:
+    for copy in copies[2:]:
         copy.wait()
     join_pieces(devices, groups * whole, rest, goal_ref, cut_goal_ref)
 
@@ -297,14 +299,21 @@
     scale = jnp.concatenate(pieces, axis=0) if len(pieces) > 1 else pieces[0]
 
     frozen_ref[...] = near_frozen_ref[...]
-    hidden_ref[...] = near_hidden_ref[...]
+    hidden_ref[...] = hidden_refs[0][...] + hidden_refs[1][...]
     side = lax.rem(lax.axis_index("grp"), 2)
     copies[0].wait()
+    copies[1].wait()
 
     def add_shard(shard, unused):
-        wait_block(w_ref, shard, groups_of // 2, w_sem)
-        far = pl.ds(pl.multiple_of((2 * shard + 1 - side) * half, half), half)
-        frozen_ref[...] += dot(x_ref[:, far], w_ref[shard])
+        total = None
+        for place in range(2):
+            target = w_ref.at[shard, pl.ds(place * depth, depth), :]
+            wait_block(target, groups_of // 2, w_sem.at[place, shard])
+            first = place * size + (2 * shard + 1 - side) * depth
+            far = pl.ds(pl.multiple_of(first, depth), depth)
+            term = dot(x_ref[:, far], w_ref[shard, place * depth : (place + 1) * depth])
+            total = term if total is None else total + term
+        frozen_ref[...] += total
         return unused
 
     lax.fori_loop(0, members, add_shard, 0, unroll=4)
@@ -359,7 +368,9 @@
                 device = (2 * pair + core) * members + member
                 spot = lax.bitwise_xor(lax.div(lax.axis_index("grp"), 2), pair)
                 place = lax.bitwise_xor(lax.axis_index("fsdp"), member)
-                moved = delta_ref[:, device * share : (device + 1) * share]
+                block = device * share // depth
+                first = block % 2 * size + block // 2 * depth + device * share % depth
+                moved = delta_ref[:, first : first + share]
                 target[spot, place, :rank, :] = factor * moved
                 first = device * up_share
                 parts = [
@@ -420,75 +431,94 @@
 
     params = pltpu.CompilerParams(vmem_limit_bytes=VMEM_BYTES)
     half = value_weight.shape[0] // 2
+    depth = half // 2
+    blocks = width // (2 * depth)
     piece = kv_width // (groups // 2)
     pair = lax.axis_index("grp") // 2
-    mine = lax.dynamic_slice(value_weight, (side * half, pair * piece), (half, piece))
-    near = lax.all_gather(mine, BOTH, axis=0, axis_index_groups=weight_rings(groups, members))
     swap = [(at, at ^ 1) for at in range(groups)]
-    far = lax.ppermute(near, "grp", swap)
-
-    columns = whole_groups * (width + kv_width) + rest * (width + kv_width) // SUB + LANES
-    packed = pl.pallas_call(
-        lambda *refs: pack_kernel(users, most, *refs),
-        out_shape=jax.ShapeDtypeStruct((users * SUB, columns), BF16),
-        in_specs=[smem, vmem, anywhere, anywhere],
-        out_specs=anywhere,
-        scratch_shapes=[
-            pltpu.VMEM((per_dev, width), BF16),
-            pltpu.VMEM((per_dev, kv_width), BF16),
-            pltpu.VMEM((users * SUB, columns), BF16),
-            pltpu.SemaphoreType.DMA((2 * SUB,)),
-            pltpu.SemaphoreType.DMA((2 * (SUB * whole_groups + rest) + 1,)),
-        ],
-        compiler_params=params,
-        name="pack_rows",
-    )(device_row_count, row_owner_user.reshape(1, per_dev), tokens, targets)
-    got = lax.all_to_all(
-        packed.reshape(users, SUB, columns), BOTH, split_axis=0, concat_axis=0, tiled=True
-    ).reshape(whole, columns)
+    rings = weight_rings(groups, members)
+    owners = row_owner_user.reshape(1, per_dev)
+    near, far, got = ([], [], [])
+    for part in range(2):
+        columns = whole_groups * width // 2 + rest * width // 2 // SUB
+        if part:
+            columns += whole_groups * kv_width + rest * kv_width // SUB + LANES
+        packed = pl.pallas_call(
+            lambda *refs: pack_kernel(users, most, part, part == 1, *refs),
+            out_shape=jax.ShapeDtypeStruct((users * SUB, columns), BF16),
+            in_specs=[smem, vmem, anywhere, vmem],
+            out_specs=vmem,
+            scratch_shapes=[
+                pltpu.VMEM((per_dev, width // 2), BF16),
+                pltpu.SemaphoreType.DMA((blocks,)),
+            ],
+            compiler_params=params,
+            name="pack_rows",
+        )(device_row_count, owners, tokens, targets)
+        got.append(
+            lax.all_to_all(
+                packed.reshape(users, SUB, columns), BOTH, split_axis=0, concat_axis=0, tiled=True
+            ).reshape(whole, columns)
+        )
+        mine = lax.dynamic_slice(
+            value_weight, (side * half + part * depth, pair * piece), (depth, piece)
+        )
+        near.append(lax.all_gather(mine, BOTH, axis=0, axis_index_groups=rings))
+        far.append(lax.ppermute(near[-1], "grp", swap))
+
     share = width // devices
     tall = rank + kv_width // devices * rank // share
-    down = adapter_down.T
-    rows, hidden = pl.pallas_call(
-        lambda *refs: rows_kernel(devices, most, *refs),
-        out_shape=[
-            jax.ShapeDtypeStruct((slots, width), BF16),
-            jax.ShapeDtypeStruct((slots, rank), F32),
-        ],
-        in_specs=[anywhere, vmem],
-        out_specs=[anywhere, vmem],
-        scratch_shapes=[
-            pltpu.VMEM((slots, width), BF16),
-            pltpu.VMEM((max(rest, 1), whole, width // SUB), BF16),
-            pltpu.SemaphoreType.DMA((whole_groups + rest,)),
-            pltpu.SemaphoreType.DMA,
-        ],
-        compiler_params=params,
-        name="join_rows",
-    )(got, down)
-    near_frozen = pl.pallas_call(
-        lambda *refs: near_kernel(groups, members, *refs),
-        out_shape=jax.ShapeDtypeStruct((slots, kv_width), F32),
-        in_specs=[anywhere, anywhere],
-        out_specs=vmem,
-        scratch_shapes=[
-            pltpu.VMEM((slots, width), BF16),
-            pltpu.VMEM((members, half, kv_width), BF16),
-            pltpu.SemaphoreType.DMA((members,)),
-            pltpu.SemaphoreType.DMA((members, groups // 2)),
-        ],
-        compiler_params=params,
-        cost_estimate=pl.CostEstimate(
-            flops=slots * width * kv_width, bytes_accessed=3 * 10**7, transcendentals=0
-        ),
-        name="near_product",
-    )(rows, near)
+    down = adapter_down.T.reshape(rank, blocks, 2, depth)
+    down = [down[:, :, part].reshape(rank, width // 2) for part in range(2)]
+    frozen = []
+    rows, hidden = ([], [])
+    for part in range(2):
+        joined, partial = pl.pallas_call(
+            lambda *refs: rows_kernel(devices, most, *refs),
+            out_shape=[
+                jax.ShapeDtypeStruct((slots, width // 2), BF16),
+                jax.ShapeDtypeStruct((slots, rank), F32),
+            ],
+            in_specs=[anywhere, vmem],
+            out_specs=[anywhere, vmem],
+            scratch_shapes=[
+                pltpu.VMEM((slots, width // 2), BF16),
+                pltpu.VMEM((max(rest, 1), whole, width // 2 // SUB), BF16),
+                pltpu.SemaphoreType.DMA((whole_groups + rest,)),
+                pltpu.SemaphoreType.DMA,
+            ],
+            compiler_params=params,
+            name="join_rows",
+        )(got[part], down[part])
+        rows.append(joined)
+        hidden.append(partial)
+        frozen = [
+            pl.pallas_call(
+                lambda *refs: near_kernel(groups, members, *refs),
+                out_shape=jax.ShapeDtypeStruct((slots, kv_width), F32),
+                in_specs=[vmem] * len(frozen) + [anywhere, anywhere],
+                out_specs=vmem,
+                scratch_shapes=[
+                    pltpu.VMEM((slots, width // 2), BF16),
+                    pltpu.VMEM((members, depth, kv_width), BF16),
+                    pltpu.SemaphoreType.DMA((members,)),
+                    pltpu.SemaphoreType.DMA((members, groups // 2)),
+                ],
+                compiler_params=params,
+                cost_estimate=pl.CostEstimate(
+                    flops=slots * width * kv_width // 2, bytes_accessed=10**7, transcendentals=0
+                ),
+                name="near_product",
+            )(*frozen, joined, near[part])
+        ]
 
     package = jax.ShapeDtypeStruct((groups // 2, members, tall, share), F32)
     keep, send = pl.pallas_call(
-        lambda *refs: user_kernel(groups, members, most, *refs),
+        lambda cap, clip, got, x0, x1, frozen, h0, h1, w0, w1, *refs: user_kernel(
+            groups, members, most, cap, clip, got, (x0, x1), frozen, (h0, h1), (w0, w1), *refs
+        ),
         out_shape=[package] * 2,
-        in_specs=[smem, smem, anywhere, anywhere, vmem, vmem, anywhere, vmem, vmem],
+        in_specs=[smem] * 2 + [anywhere] * 3 + [vmem] * 3 + [anywhere] * 2 + [vmem] * 2,
         out_specs=[vmem] * 2,
         scratch_shapes=[
             pltpu.VMEM((slots, width), BF16),
@@ -499,12 +529,22 @@
             pltpu.VMEM((slots, kv_width), F32),
             pltpu.VMEM((slots, rank), F32),
             pltpu.VMEM((rank, width), F32),
-            pltpu.SemaphoreType.DMA((whole_groups + rest + 2,)),
-            pltpu.SemaphoreType.DMA((members, groups // 2)),
+            pltpu.SemaphoreType.DMA((whole_groups + rest + 3,)),
+            pltpu.SemaphoreType.DMA((2, members, groups // 2)),
         ],
         compiler_params=params,
         name="user_steps",
-    )(user_row_cap, clip_norm_bound, got, rows, near_frozen, hidden, far, down, adapter_up)
+    )(
+        user_row_cap,
+        clip_norm_bound,
+        got[1],
+        *rows,
+        *frozen,
+        *hidden,
+        *far,
+        jnp.concatenate(down, axis=1),
+        adapter_up,
+    )
 
     other = lax.ppermute(send, "grp", swap)
     keep = keep.reshape(groups // 2, members // 2, 2, tall, share)

time: 264 us -> 297 us (1.12)
  Pallas kernels: 38.7 us -> 50.9 us
  local copies, waits for them, and re-layouts: 2.03 us -> 14 us
  waiting for transfers between devices: 188 us -> 192 us
  starting transfers between devices: 16 us -> 19 us
    all_to_all x1 -> x2, waiting for transfers between devices: 0.01 us -> 60.5 us  [body(): lax.all_to_all(packed.reshape(users, SUB, columns), BOTH, split_axis=0, c...]
    all_gather x1 -> x2, waiting for transfers between devices: 168 us -> 111 us  [body(): near.append(lax.all_gather(mine, BOTH, axis=0, axis_index_groups=rings))]
    slice x0 -> x1, local copies, waits for them, and re-layouts: none -> 6.09 us  [body(): down = [down[:, :, part].reshape(rank, width // 2) for part in range(2)]]
    pallas_call x2 -> x3, Pallas kernels: 24.9 us -> 29.7 us  [the longest x1 18.2 us: body(): pl.pallas_call(lambda cap, clip, got, x0, x1, frozen, h0, h1, w0, w1, *re...]
    pallas_call x1 -> x2, Pallas kernels: 6.6 us -> 10.7 us  [body(): pl.pallas_call(lambda *refs: near_kernel(groups, members, *refs), out_sha...]
    unnamed x4 -> x14, local copies, waits for them, and re-layouts: 0.01 us -> 3.37 us
    pallas_call x1 -> x2, Pallas kernels: 7.21 us -> 10.5 us  [body(): pl.pallas_call(lambda *refs: rows_kernel(devices, most, *refs), out_shape...]
    all_to_all x1 -> x2, starting transfers between devices: 7.42 us -> 10.3 us  [body(): lax.all_to_all(packed.reshape(users, SUB, columns), BOTH, split_axis=0, c...]
  transfers between devices with their start and end apart: 10 -> 13, of which waited for: 6 -> 10; matrix products, arithmetic and copies ran while one was open for 0% -> 3% of each run, Pallas kernels for 8% -> 11%
where the time goes in v7:
time: 297 us; the launch traced here: 296 us
  waiting for transfers between devices  192 us (65%)
  Pallas kernels  50.9 us (17%)
  starting transfers between devices  19 us (6%)
  between operations  15.5 us (5%)
  local copies, waits for them, and re-layouts  14 us (5%)
  other arithmetic  4.66 us (2%)
    all_gather x2, waiting for transfers between devices, body(): near.append(lax.all_gather(mine, BOTH, axis=0, axis_index_groups=rings))  111 us
    all_to_all x2, waiting for transfers between devices, body(): lax.all_to_all(packed.reshape(users, SUB, columns), BOTH, split_axis=0, c...  60.5 us
    pallas_call x1, Pallas kernels, body(): pl.pallas_call(lambda cap, clip, got, x0, x1, frozen, h0, h1, w0, w1, *re...  18.2 us
    ppermute x6, waiting for transfers between devices, exchange(): total = total + lax.ppermute(blocks[place], BOTH, pairs)  17.8 us
    pallas_call x2, Pallas kernels, body(): pl.pallas_call(lambda *refs: pack_kernel(users, most, part, part == 1, *r...  11.4 us
    pallas_call x2, Pallas kernels, body(): pl.pallas_call(lambda *refs: near_kernel(groups, members, *refs), out_sha...  10.7 us
    pallas_call x2, Pallas kernels, body(): pl.pallas_call(lambda *refs: rows_kernel(devices, most, *refs), out_shape...  10.5 us
    all_to_all x2, starting transfers between devices, body(): lax.all_to_all(packed.reshape(users, SUB, columns), BOTH, split_axis=0, c...  10.3 us
  transfers between devices with their start and end apart: 13, of which 10 were waited for; matrix products, arithmetic and copies ran while one was open for 3% of the time, Pallas kernels for 11%

profile of v7, /device:TPU:0, one launch (start us, length us, event | category | flops | bytes accessed | tf_op | source)
XLA Modules:
  0.0 296.3 jit_solution(4076521256868684557)
XLA Ops:
  7.2 0.0 all-gather.5.cloned.1.call-start
  7.2 1.9 fusion.15
  9.1 0.0 all-gather.5.cloned.1.call-update
  9.1 0.0 all-gather.7.cloned.1.call-start
  9.2 0.7 all-gather.7.cloned.1.call-update
  10.5 5.4 %pack_rows.3 = bf16[256,4608]{1,0:T(8,128)(2,1)} custom-call(s32[1]{0:T(128)S(6)} %copy.37.refs_0_, s32[1,192]{1,0:T(1,128)} %bitcast.121, bf16[192,8192]{1,0:T(8,128)(2,1)} %refs_2_.3, bf16[192,1024]{1,0:T(8,128)(2,1)} %refs_3_.3), custom_call_target="tpu_custom_call" | custom-call | tf_op jit(solution)/shard_map/pack_rows/pallas_call | solution.py:446
  15.9 7.3 %all-to-all-start.1 = ((bf16[32,8,4608]{2,1,0:T(8,128)(2,1)}), bf16[32,8,4608]{2,1,0:T(8,128)(2,1)S(1)}, u32[]{:S(2)}, u32[]{:S(2)}) async-start(bf16[32,8,4608]{2,1,0:T(8,128)(2,1)} %bitcast.104), calls=%async_computation.1 | async-start | bytes 4718592 | tf_op jit(solution)/shard_map/all_to_all | solution.py:459
  23.2 6.0 %pack_rows.2 = bf16[256,5888]{1,0:T(8,128)(2,1)} custom-call(s32[1]{0:T(128)S(6)} %copy.37.refs_0_, s32[1,192]{1,0:T(1,128)} %bitcast.122, bf16[192,8192]{1,0:T(8,128)(2,1)} %refs_2_.3, bf16[192,1024]{1,0:T(8,128)(2,1)} %refs_3_.3), custom_call_target="tpu_custom_call" | custom-call | tf_op jit(solution)/shard_map/pack_rows/pallas_call | solution.py:446
  29.3 60.5 %all-to-all-done.1 = bf16[32,8,4608]{2,1,0:T(8,128)(2,1)S(1)} async-done(((bf16[32,8,4608]{2,1,0:T(8,128)(2,1)}), bf16[32,8,4608]{2,1,0:T(8,128)(2,1)S(1)}, u32[]{:S(2)}, u32[]{:S(2)}) %all-to-all-start.1) | async-done | bytes 2359328 | tf_op jit(solution)/shard_map/all_to_all | solution.py:459
  89.8 1.4 copy-done.1
  91.2 3.0 all-to-all-start
  94.2 35.1 %all-gather.5.cloned.1.call-done = bf16[4096,512]{1,0:T(8,128)(2,1)} async-done(((bf16[256,512]{1,0:T(8,128)(2,1)}), bf16[4096,512]{1,0:T(8,128)(2,1)}) %all-gather.5.cloned.1.call-update) | async-done | bytes 4194320 | tf_op jit(solution)/shard_map/all_gather | solution.py:466
  129.2 0.0 collective-permute-start
  129.2 75.5 %all-gather.7.cloned.1.call-done = bf16[4096,512]{1,0:T(8,128)(2,1)} async-done(((bf16[256,512]{1,0:T(8,128)(2,1)}), bf16[4096,512]{1,0:T(8,128)(2,1)}) %all-gather.7.cloned.1.call-update) | async-done | bytes 4194320 | tf_op jit(solution)/shard_map/all_gather | solution.py:466
  204.7 0.0 collective-permute-start.1
  204.7 2.6 reshape.43
  207.3 6.1 %slice_reduce_fusion = (bf16[64,16,256]{2,1,0:T(8,128)(2,1)S(1)}, bf16[64,16,256]{2,1,0:T(8,128)(2,1)S(1)}) fusion(bf16[64,16,2,256]{3,2,1,0:T(2,128)(2,1)} %reshape.43), kind=kLoop, calls=%fused_computation | loop fusion | bytes 2097152 | tf_op jit(solution)/shard_map/slice | solution.py:472
  213.4 0.2 copy.34
  213.6 0.2 copy.35
  214.5 1.0 pad_maximum_fusion.refs_0_
  215.5 5.3 %join_rows.2 = (bf16[288,4096]{1,0:T(8,128)(2,1)}, f32[288,64]{1,0:T(8,128)}) custom-call(bf16[256,4608]{1,0:T(8,128)(2,1)} %bitcast.105, bf16[64,4096]{1,0:T(8,128)(2,1)} %bitcast.109), custom_call_target="tpu_custom_call" | custom-call | tf_op jit(solution)/shard_map/join_rows/pallas_call | solution.py:476
  220.8 0.0 all-to-all-done
  220.8 1.6 copy-done
  222.4 5.2 %join_rows.3 = (bf16[288,4096]{1,0:T(8,128)(2,1)}, f32[288,64]{1,0:T(8,128)}) custom-call(bf16[256,5888]{1,0:T(8,128)(2,1)} %bitcast.101, bf16[64,4096]{1,0:T(8,128)(2,1)} %bitcast.107), custom_call_target="tpu_custom_call" | custom-call | tf_op jit(solution)/shard_map/join_rows/pallas_call | solution.py:476
  227.6 4.7 %near_product.2.refs_0_ = f32[288,1024]{1,0:T(8,128)} custom-call(bf16[288,4096]{1,0:T(8,128)(2,1)} %get-tuple-element.8.refs_0_.x0, bf16[16,256,512]{2,1,0:T(8,128)(2,1)} %bitcast.113), custom_call_target="tpu_custom_call" | custom-call | flops 1207959552 | bytes 10000000 | tf_op jit(solution)/shard_map/near_product/pallas_call | solution.py:496
  232.3 6.0 %near_product.3.frozen = f32[288,1024]{1,0:T(8,128)} custom-call(f32[288,1024]{1,0:T(8,128)} %near_product.2.refs_0_, bf16[288,4096]{1,0:T(8,128)(2,1)} %get-tuple-element.9.refs_1_.x1, bf16[16,256,512]{2,1,0:T(8,128)(2,1)} %bitcast.111), custom_call_target="tpu_custom_call" | custom-call | flops 1207959552 | bytes 10000000 | tf_op jit(solution)/shard_map/near_product/pallas_call | solution.py:496
  238.4 0.0 collective-permute-done.w0
  238.4 0.0 collective-permute-done.1.w1
  238.4 18.2 %user_steps.1 = (f32[2,8,72,256]{3,2,1,0:T(8,128)}, f32[2,8,72,256]{3,2,1,0:T(8,128)}) custom-call(s32[32]{0:T(128)} %cap.1, f32[1]{0:T(128)} %copy.38.clip, bf16[256,5888]{1,0:T(8,128)(2,1)} %bitcast.102, bf16[288,4096]{1,0:T(8,128)(2,1)} %get-tuple-element.8.refs_0_.x0, bf16[288,4096]{1,0:T(8,128)(2,1)} %get-tuple-element.9.refs_1_.x1, ...), custom_call_target="tpu_custom_call" | custom-call | tf_op jit(solution)/shard_map/user_steps/pallas_call | solution.py:516
  256.6 0.6 collective-permute-start.2
  257.2 2.7 collective-permute-done.2
  259.9 1.3 fusion.5
  261.2 1.0 collective-permute-start.3
  262.2 1.3 collective-permute-start.4
  263.6 1.2 collective-permute-start.5
  264.8 6.3 %collective-permute-done.3 = f32[4,72,256]{2,1,0:T(8,128)S(1)} collective-permute-done((f32[4,72,256]{2,1,0:T(8,128)S(1)}, f32[4,72,256]{2,1,0:T(8,128)S(1)}, u32[]{:S(2)}, u32[]{:S(2)}) %collective-permute-start.3) | collective-permute-done | bytes 294944 | tf_op jit(solution)/shard_map/ppermute | solution.py:400
  271.1 5.3 %collective-permute-done.4 = f32[4,72,256]{2,1,0:T(8,128)S(1)} collective-permute-done((f32[4,72,256]{2,1,0:T(8,128)S(1)}, f32[4,72,256]{2,1,0:T(8,128)S(1)}, u32[]{:S(2)}, u32[]{:S(2)}) %collective-permute-start.4) | collective-permute-done | bytes 294944 | tf_op jit(solution)/shard_map/ppermute | solution.py:400
  276.4 1.1 collective-permute-done.5
  277.6 1.1 fusion.10
  278.6 1.4 collective-permute-start.6
  280.0 1.8 collective-permute-start.7
  281.8 1.2 collective-permute-start.8
  283.1 0.6 collective-permute-done.6
  283.7 3.4 %collective-permute-done.7 = f32[72,256]{1,0:T(8,128)S(1)} collective-permute-done((f32[72,256]{1,0:T(8,128)S(1)}, f32[72,256]{1,0:T(8,128)S(1)}, u32[]{:S(2)}, u32[]{:S(2)}) %collective-permute-start.7) | collective-permute-done | bytes 73760 | tf_op jit(solution)/shard_map/ppermute | solution.py:400
  287.1 1.0 collective-permute-done.8
  288.1 0.1 reshape.46
  288.2 0.6 fusion.14
  288.9 0.6 bitcast_add_fusion
  (13 shorter events, 0.1 us)
Async XLA Ops:
  7.2 122.1 %all-gather.5.cloned.1.call-start = ((), (), s32[]{:S(2)}) async-start(), calls=%async_computation.2 | async-start | bytes 4456448 | tf_op jit(solution)/shard_map/all_gather | solution.py:466
  9.1 195.6 %all-gather.7.cloned.1.call-start = ((), (), s32[]{:S(2)}) async-start(), calls=%async_computation.3 | async-start | bytes 4456448 | tf_op jit(solution)/shard_map/all_gather | solution.py:466
  15.9 73.9 %all-to-all-start.1 = ((bf16[32,8,4608]{2,1,0:T(8,128)(2,1)}), bf16[32,8,4608]{2,1,0:T(8,128)(2,1)S(1)}, u32[]{:S(2)}, u32[]{:S(2)}) async-start(bf16[32,8,4608]{2,1,0:T(8,128)(2,1)} %bitcast.104), calls=%async_computation.1 | async-start | bytes 4718592 | tf_op jit(solution)/shard_map/all_to_all | solution.py:459
  89.8 1.4 copy-start.1
  91.2 129.6 %all-to-all-start = ((bf16[32,8,5888]{2,1,0:T(8,128)(2,1)}), bf16[32,8,5888]{2,1,0:T(8,128)(2,1)S(1)}, u32[]{:S(2)}, u32[]{:S(2)}) async-start(bf16[32,8,5888]{2,1,0:T(8,128)(2,1)} %bitcast.103), calls=%async_computation | async-start | bytes 6029312 | tf_op jit(solution)/shard_map/all_to_all | solution.py:459
  129.2 109.1 %collective-permute-start = (bf16[16,256,512]{2,1,0:T(8,128)(2,1)}, bf16[16,256,512]{2,1,0:T(8,128)(2,1)}, u32[]{:S(2)}, u32[]{:S(2)}) collective-permute-start(bf16[16,256,512]{2,1,0:T(8,128)(2,1)} %bitcast.112), channel_id=1, source_target_pairs={{0,8},{8,0},{16,24},{24,16},{1,9},{9,1},{17,25},{25,17},{2,10},{10... | collective-permute-start | bytes 12582920 | tf_op jit(solution)/shard_map/ppermute | solution.py:467
  204.7 33.7 %collective-permute-start.1 = (bf16[16,256,512]{2,1,0:T(8,128)(2,1)}, bf16[16,256,512]{2,1,0:T(8,128)(2,1)}, u32[]{:S(2)}, u32[]{:S(2)}) collective-permute-start(bf16[16,256,512]{2,1,0:T(8,128)(2,1)} %bitcast.110), channel_id=1, source_target_pairs={{0,8},{8,0},{16,24},{24,16},{1,9},{9,1},{17,25},{25,17},{2,10},{10... | collective-permute-start | bytes 12582920 | tf_op jit(solution)/shard_map/ppermute | solution.py:467
  213.6 1.9 copy-start.3
  213.8 7.0 %copy-start.2 = (bf16[8,8,16,256]{3,1,2,0:T(8,128)(2,1)}, bf16[8,8,16,256]{3,1,2,0:T(8,128)(2,1)S(1)}, u32[]{:S(2)}) copy-start(bf16[8,8,16,256]{3,1,2,0:T(8,128)(2,1)S(1)} %copy.35) | copy-start | bytes 1572868
  220.8 1.6 copy-start
  256.6 3.3 %collective-permute-start.2 = (f32[2,8,72,256]{3,2,1,0:T(8,128)}, f32[2,8,72,256]{3,2,1,0:T(8,128)S(1)}, u32[]{:S(2)}, u32[]{:S(2)}) collective-permute-start(f32[2,8,72,256]{3,2,1,0:T(8,128)} %get-tuple-element.13), channel_id=1, source_target_pairs={{0,8},{8,0},{16,24},{24,16},{1,9},{9,1},{17,25},{25,17},{2,10},{10... | collective-permute-start | bytes 3538952 | tf_op jit(solution)/shard_map/ppermute | solution.py:549
  259.9 28.3 %copy-start.4 = (f32[256,64]{0,1:T(8,128)S(1)}, f32[256,64]{0,1:T(8,128)}, u32[]{:S(2)}) copy-start(f32[256,64]{0,1:T(8,128)} %param.20) | copy-start | bytes 196612
  259.9 28.9 %copy-start.5 = (f32[64,32]{0,1:T(8,128)S(1)}, f32[64,32]{0,1:T(8,128)}, u32[]{:S(2)}) copy-start(f32[64,32]{0,1:T(8,128)} %param.21) | copy-start | bytes 24580
  261.2 9.9 %collective-permute-start.3 = (f32[4,72,256]{2,1,0:T(8,128)S(1)}, f32[4,72,256]{2,1,0:T(8,128)S(1)}, u32[]{:S(2)}, u32[]{:S(2)}) collective-permute-start(f32[4,72,256]{2,1,0:T(8,128)S(1)} %get-tuple-element.16), channel_id=1, source_target_pairs={{0,1},{1,0},{2,3},{3,2},{4,5},{5,4},{6,7},{7,6},{8,9},{9,8},{10,11... | collective-permute-start | bytes 884744 | tf_op jit(solution)/shard_map/ppermute | solution.py:400
  262.2 14.2 %collective-permute-start.4 = (f32[4,72,256]{2,1,0:T(8,128)S(1)}, f32[4,72,256]{2,1,0:T(8,128)S(1)}, u32[]{:S(2)}, u32[]{:S(2)}) collective-permute-start(f32[4,72,256]{2,1,0:T(8,128)S(1)} %get-tuple-element.17), channel_id=1, source_target_pairs={{0,16},{1,17},{2,18},{3,19},{4,20},{5,21},{6,22},{7,23},{8,24},{9,... | collective-permute-start | bytes 884744 | tf_op jit(solution)/shard_map/ppermute | solution.py:400
  263.6 14.0 %collective-permute-start.5 = (f32[4,72,256]{2,1,0:T(8,128)S(1)}, f32[4,72,256]{2,1,0:T(8,128)S(1)}, u32[]{:S(2)}, u32[]{:S(2)}) collective-permute-start(f32[4,72,256]{2,1,0:T(8,128)S(1)} %get-tuple-element.18), channel_id=1, source_target_pairs={{0,17},{1,16},{2,19},{3,18},{4,21},{5,20},{6,23},{7,22},{8,25},{9,... | collective-permute-start | bytes 884744 | tf_op jit(solution)/shard_map/ppermute | solution.py:400
  278.6 5.1 %collective-permute-start.6 = (f32[72,256]{1,0:T(8,128)S(1)}, f32[72,256]{1,0:T(8,128)S(1)}, u32[]{:S(2)}, u32[]{:S(2)}) collective-permute-start(f32[72,256]{1,0:T(8,128)S(1)} %get-tuple-element.21), channel_id=1, source_target_pairs={{0,2},{1,3},{2,0},{3,1},{4,6},{5,7},{6,4},{7,5},{8,10},{9,11},{10,... | collective-permute-start | bytes 221192 | tf_op jit(solution)/shard_map/ppermute | solution.py:400
  280.0 7.0 %collective-permute-start.7 = (f32[72,256]{1,0:T(8,128)S(1)}, f32[72,256]{1,0:T(8,128)S(1)}, u32[]{:S(2)}, u32[]{:S(2)}) collective-permute-start(f32[72,256]{1,0:T(8,128)S(1)} %get-tuple-element.23), channel_id=1, source_target_pairs={{0,4},{1,5},{2,6},{3,7},{4,0},{5,1},{6,2},{7,3},{8,12},{9,13},{10,... | collective-permute-start | bytes 221192 | tf_op jit(solution)/shard_map/ppermute | solution.py:400
  281.8 6.3 %collective-permute-start.8 = (f32[72,256]{1,0:T(8,128)S(1)}, f32[72,256]{1,0:T(8,128)S(1)}, u32[]{:S(2)}, u32[]{:S(2)}) collective-permute-start(f32[72,256]{1,0:T(8,128)S(1)} %get-tuple-element.22), channel_id=1, source_target_pairs={{0,6},{1,7},{2,4},{3,5},{4,2},{5,3},{6,0},{7,1},{8,14},{9,15},{10,... | collective-permute-start | bytes 221192 | tf_op jit(solution)/shard_map/ppermute | solution.py:400
Sparse Core Ops, SparseCore 0:
  9.5 119.6 all-gather.4
  130.8 73.9 all-gather.6

commit v8 on v4

--- a/solution.py
+++ b/solution.py
@@ -27,7 +27,9 @@
     return lax.broadcasted_iota(jnp.int32, shape, axis)
 
 
-def pack_kernel(users, most, count_ref, owner_ref, tokens_ref, targets_ref, out_ref):
+def pack_kernel(
+    users, most, count_ref, owner_ref, tokens_ref, targets_ref, out_ref, cut_ref, cut_goal_ref
+):
     rows = tokens_ref.shape[0]
     groups, rest = divmod(most, SUB)
     owner_row = owner_ref[...]
@@ -38,26 +40,28 @@
     line = iota((users * SUB, rows), 0)
     mine = line // SUB == owner_row
     slot = line % SUB
+    picks = [mine & (rank == slot + group * SUB) for group in range(groups)]
+    user = iota((users, rows), 0) == owner_row
+    picks += [user & (rank == groups * SUB + extra) for extra in range(rest)]
+    pick = jnp.concatenate([one.astype(BF16) for one in picks], axis=0)
+    whole = users * SUB
+    line, other = (iota((whole, whole), 0), iota((whole, whole), 1))
+    turn = (other == line % SUB * users + line // SUB).astype(BF16)
     column = 0
-    for source in (tokens_ref, targets_ref):
+    for source, cut in ((tokens_ref, cut_ref), (targets_ref, cut_goal_ref)):
         width = source.shape[1]
-        for group in range(groups):
-            pick = (mine & (rank == slot + group * SUB)).astype(BF16)
-            step = min(width, 1024)
-            for at in range(0, width, step):
-                out_ref[:, column + at : column + at + step] = dot(
-                    pick, source[:, at : at + step]
-                ).astype(BF16)
-            column += width
         piece = width // SUB
+        for part in range(SUB):
+            found = dot(pick, source[:, part * piece : (part + 1) * piece]).astype(BF16)
+            for group in range(groups):
+                spot = column + group * width + part * piece
+                out_ref[:, spot : spot + piece] = found[group * whole : (group + 1) * whole]
+            for extra in range(rest):
+                first = groups * whole + extra * users
+                cut[extra, part * users : (part + 1) * users] = found[first : first + users]
+        column += groups * width
         for extra in range(rest):
-            here = mine & (rank == groups * SUB + extra)
-            total = None
-            for part in range(SUB):
-                pick = (here & (slot == part)).astype(BF16)
-                term = dot(pick, source[:, part * piece : (part + 1) * piece])
-                total = term if total is None else total + term
-            out_ref[:, column : column + piece] = total.astype(BF16)
+            out_ref[:, column : column + piece] = dot(turn, cut[extra]).astype(BF16)
             column += piece
     used = mine & (iota((users * SUB, rows), 1) < count_ref[0])
     number = jnp.sum(used.astype(F32), axis=1, keepdims=True)
@@ -173,20 +177,22 @@
         hidden_ref[...] += dot(x_ref[:, both], down_ref[:, both], ((1,), (1,)))
         return unused
 
-    lax.fori_loop(0, members, add_shard, 0)
+    lax.fori_loop(0, members, add_shard, 0, unroll=4)
     out.wait()
 
 
 def join_pieces(devices, bottom, rest, full, cut):
-    line, other = (iota((devices, devices * SUB), 0), iota((devices, devices * SUB), 1))
+    whole = devices * SUB
+    line, other = (iota((whole, whole), 0), iota((whole, whole), 1))
+    turn = (other == line % devices * SUB + line // devices).astype(BF16)
     piece = full.shape[1] // SUB
     for extra in range(rest):
         first = bottom + extra * devices
+        rows = dot(turn, cut[extra]).astype(BF16)
         for part in range(SUB):
-            pick = (other == line * SUB + part).astype(BF16)
-            full[first : first + devices, part * piece : (part + 1) * piece] = dot(
-                pick, cut[extra]
-            ).astype(BF16)
+            full[first : first + devices, part * piece : (part + 1) * piece] = rows[
+                part * devices : (part + 1) * devices
+            ]
 
 
 def user_kernel(
@@ -278,7 +284,7 @@
         frozen_ref[...] += dot(x_ref[:, far], w_ref[shard])
         return unused
 
-    lax.fori_loop(0, members, add_shard, 0)
+    lax.fori_loop(0, members, add_shard, 0, unroll=4)
 
     rate = ADAPTER_SCALE * LEARN_RATE
     block = min(width, 1024)
@@ -306,11 +312,16 @@
                 half_down = (down_ref[:, lanes].astype(F32) + moved).astype(BF16)
                 hidden_ref[...] += dot(x_ref[:, lanes], half_down, ((1,), (1,)))
                 return unused
-            return unused + jnp.sum(moved * moved)
-
-        squares = lax.fori_loop(0, width // block, down_block, jnp.zeros((), F32))
-
-    total = squares + jnp.sum(up_delta * up_delta) + EPSILON
+            square = moved * moved
+            for at in range(0, block, LANES):
+                unused = unused + square[:, at : at + LANES]
+            return unused
+
+        squares = lax.fori_loop(
+            0, width // block, down_block, jnp.zeros((rank, LANES), F32), unroll=4
+        )
+
+    total = jnp.sum(squares) + jnp.sum(up_delta * up_delta) + EPSILON
     total = jnp.full((1, LANES), total, F32)
     factor = jnp.minimum(1.0, clip_ref[0] / jnp.sqrt(total))[:, :1]
     share = width // devices
@@ -403,6 +414,10 @@
         out_shape=jax.ShapeDtypeStruct((users * SUB, columns), BF16),
         in_specs=[smem, vmem, vmem, vmem],
         out_specs=vmem,
+        scratch_shapes=[
+            pltpu.VMEM((max(rest, 1), users * SUB, width // SUB), BF16),
+            pltpu.VMEM((max(rest, 1), users * SUB, kv_width // SUB), BF16),
+        ],
         compiler_params=pltpu.CompilerParams(vmem_limit_bytes=VMEM_BYTES),
         name="pack_rows",
     )(device_row_count, row_owner_user.reshape(1, per_dev), tokens, targets)

time: 267 us -> 263 us (0.985)
  Pallas kernels: 39.5 us -> 34.8 us
    pallas_call x1, Pallas kernels: 21.5 us -> 17.6 us  [body(): pl.pallas_call(lambda *refs: user_kernel(groups, members, most, *refs), o...]
where the time goes in v8:
time: 263 us
  waiting for transfers between devices  186 us (71%)
  Pallas kernels  34.8 us (13%)
  between operations  15.5 us (6%)
  starting transfers between devices  10.6 us (4%)
  blocking collectives  10.5 us (4%)
  other arithmetic  3.7 us (1%)
    all_gather x1, waiting for transfers between devices, body(): lax.all_gather(mine, BOTH, axis=0, axis_index_groups=weight_rings(groups,...  168 us
    pallas_call x1, Pallas kernels, body(): pl.pallas_call(lambda *refs: user_kernel(groups, members, most, *refs), o...  17.6 us
    ppermute x4, waiting for transfers between devices, halve(): package = lax.ppermute(send, axis, pairs) + keep  13.5 us
    pallas_call x1, Pallas kernels, body(): pl.pallas_call(lambda *refs: near_kernel(groups, members, most, *refs), o...  10.7 us
    all_to_all x1, blocking collectives, body(): lax.all_to_all(package, 'fsdp', split_axis=0, concat_axis=0, axis_index_g...  10.5 us
    all_to_all x1, starting transfers between devices, body(): lax.all_to_all(packed.reshape(users, SUB, columns), BOTH, split_axis=0, c...  7.41 us
    pallas_call x1, Pallas kernels, body(): pl.pallas_call(lambda *refs: pack_kernel(users, most, *refs), out_shape=j...  6.6 us
  transfers between devices with their start and end apart: 9, of which 6 were waited for; matrix products, arithmetic and copies ran while one was open for 1% of the time, Pallas kernels for 7%

profile of v8, /device:TPU:0, one launch (start us, length us, event | category | flops | bytes accessed | tf_op | source)
XLA Modules:
  0.0 262.6 jit_solution(10407809334964657750)
XLA Ops:
  7.2 0.0 all-gather.3.cloned.1.call-start
  7.2 1.9 dynamic_slice.3
  9.1 0.0 all-gather.3.cloned.1.call-update
  9.8 6.6 %pack_rows.1 = bf16[256,10496]{1,0:T(8,128)(2,1)} custom-call(s32[1]{0:T(128)S(6)} %copy.15.refs_0_, s32[1,192]{1,0:T(1,128)} %bitcast.27, bf16[192,8192]{1,0:T(8,128)(2,1)} %refs_2_.1, bf16[192,1024]{1,0:T(8,128)(2,1)} %refs_3_.1), custom_call_target="tpu_custom_call" | custom-call | tf_op jit(solution)/shard_map/pack_rows/pallas_call | solution.py:412
  16.4 7.4 %all-to-all-start = ((bf16[32,8,10496]{2,1,0:T(8,128)(2,1)}), bf16[32,8,10496]{2,1,0:T(8,128)(2,1)}, u32[]{:S(2)}, u32[]{:S(2)}) async-start(bf16[32,8,10496]{2,1,0:T(8,128)(2,1)} %bitcast.22), calls=%async_computation | async-start | bytes 10747904 | tf_op jit(solution)/shard_map/all_to_all | solution.py:424
  23.8 168.2 %all-gather.3.cloned.1.call-done = bf16[8192,512]{1,0:T(8,128)(2,1)} async-done(((bf16[512,512]{1,0:T(8,128)(2,1)}), bf16[8192,512]{1,0:T(8,128)(2,1)}) %all-gather.3.cloned.1.call-update) | async-done | bytes 8388624 | tf_op jit(solution)/shard_map/all_gather | solution.py:407
  192.1 0.0 collective-permute-start
  192.7 0.0 all-to-all-done
  192.7 10.7 %near_product.1 = (bf16[288,8192]{1,0:T(8,128)(2,1)}, f32[288,1024]{1,0:T(8,128)}, f32[288,64]{1,0:T(8,128)}) custom-call(bf16[256,10496]{1,0:T(8,128)(2,1)} %bitcast.2.refs_0_.refs_2_, bf16[16,512,512]{2,1,0:T(8,128)(2,1)} %bitcast.24, bf16[64,8192]{1,0:T(8,128)(2,1)} %bitcast.25), custom_call_target="tpu_custom_call" | custom-call | flops 2415919104 | bytes 30000000 | tf_op jit(solution)/shard_map/near_product/pallas_call | solution.py:430
  203.4 2.2 collective-permute-done.refs_6_
  205.6 17.6 %user_steps.1 = (f32[2,2,4,32,256]{4,3,2,1,0:T(8,128)}, f32[2,2,4,40,256]{4,3,2,1,0:T(8,128)}, f32[2,2,4,32,256]{4,3,2,1,0:T(8,128)}, f32[2,2,4,40,256]{4,3,2,1,0:T(8,128)}) custom-call(s32[32]{0:T(128)} %refs_0_.2, f32[1]{0:T(128)} %copy.16.refs_1_, bf16[256,10496]{1,0:T(8,128)(2,1)} %bitcast.2.refs_0_.refs_2_, bf16[288,8192]{1,0:T(8,128)(2,1)} %get-tuple-element.9.refs_3_, ...), custom_call_target="tpu_custom_call" | custom-call | tf_op jit(solution)/shard_map/user_steps/pallas_call | solution.py:457
  223.1 0.0 copy-start
  223.1 0.0 copy-start.1
  223.1 0.2 collective-permute-start.1
  223.3 0.4 collective-permute-start.4
  223.7 1.6 collective-permute-done.1
  225.3 1.1 add.38
  226.5 0.1 collective-permute-start.2
  226.6 0.0 collective-permute-done.4
  226.6 1.2 add.41
  227.8 0.1 collective-permute-start.5
  227.9 7.0 %collective-permute-done.2 = f32[1,2,4,32,256]{4,3,2,1,0:T(8,128)S(1)} collective-permute-done((f32[1,2,4,32,256]{4,3,2,1,0:T(8,128)S(1)}, f32[1,2,4,32,256]{4,3,2,1,0:T(8,128)S(1)}, u32[]{:S(2)}, u32[]{:S(2)}) %collective-permute-start.2) | collective-permute-done | bytes 262176 | tf_op jit(solution)/shard_map/ppermute | solution.py:370
  234.9 0.1 collective-permute-start.3
  235.0 3.2 %collective-permute-done.5 = f32[2,1,4,40,256]{4,3,2,1,0:T(8,128)S(1)} collective-permute-done((f32[2,1,4,40,256]{4,3,2,1,0:T(8,128)S(1)}, f32[2,1,4,40,256]{4,3,2,1,0:T(8,128)S(1)}, u32[]{:S(2)}, u32[]{:S(2)}) %collective-permute-start.5) | collective-permute-done | bytes 327712 | tf_op jit(solution)/shard_map/ppermute | solution.py:370
  238.3 2.3 collective-permute-start.6
  240.6 0.0 collective-permute-done.3
  240.6 3.3 %collective-permute-done.6 = f32[1,1,4,40,256]{4,3,2,1,0:T(8,128)S(1)} collective-permute-done((f32[1,1,4,40,256]{4,3,2,1,0:T(8,128)S(1)}, f32[1,1,4,40,256]{4,3,2,1,0:T(8,128)S(1)}, u32[]{:S(2)}, u32[]{:S(2)}) %collective-permute-start.6) | collective-permute-done | bytes 163872 | tf_op jit(solution)/shard_map/ppermute | solution.py:370
  243.9 10.5 %all_to_all.10 = f32[4,72,256]{2,1,0:T(8,128)S(1)} all-to-all(f32[4,72,256]{2,1,0:T(8,128)S(1)} %pad_maximum_fusion), channel_id=1, replica_groups={{0,2,4,6},{1,3,5,7},{8,10,12,14},{9,11,13,15},{16,18,20,22},{17,19,21,2..., dimensions={0} | all-to-all | bytes 589824 | tf_op jit(solution)/shard_map/all_to_all | solution.py:484
  254.4 0.1 reshape.22
  254.5 0.0 copy-done
  254.5 0.6 fusion.2
  255.2 0.0 copy-done.1
  255.2 0.6 bitcast_add_fusion
  (11 shorter events, 0.2 us)
Async XLA Ops:
  7.2 184.9 %all-gather.3.cloned.1.call-start = ((), (), s32[]{:S(2)}) async-start(), calls=%async_computation.2 | async-start | bytes 8912896 | tf_op jit(solution)/shard_map/all_gather | solution.py:407
  16.4 176.3 %all-to-all-start = ((bf16[32,8,10496]{2,1,0:T(8,128)(2,1)}), bf16[32,8,10496]{2,1,0:T(8,128)(2,1)}, u32[]{:S(2)}, u32[]{:S(2)}) async-start(bf16[32,8,10496]{2,1,0:T(8,128)(2,1)} %bitcast.22), calls=%async_computation | async-start | bytes 10747904 | tf_op jit(solution)/shard_map/all_to_all | solution.py:424
  192.1 13.5 %collective-permute-start = (bf16[16,512,512]{2,1,0:T(8,128)(2,1)}, bf16[16,512,512]{2,1,0:T(8,128)(2,1)}, u32[]{:S(2)}, u32[]{:S(2)}) collective-permute-start(bf16[16,512,512]{2,1,0:T(8,128)(2,1)} %bitcast.23), channel_id=1, source_target_pairs={{0,8},{8,0},{16,24},{24,16},{1,9},{9,1},{17,25},{25,17},{2,10},{10... | collective-permute-start | bytes 25165832 | tf_op jit(solution)/shard_map/ppermute | solution.py:409
  223.1 31.4 %copy-start = (f32[256,64]{0,1:T(8,128)S(1)}, f32[256,64]{0,1:T(8,128)}, u32[]{:S(2)}) copy-start(f32[256,64]{0,1:T(8,128)} %param.20) | copy-start | bytes 196612
  223.1 32.0 %copy-start.1 = (f32[64,32]{0,1:T(8,128)S(1)}, f32[64,32]{0,1:T(8,128)}, u32[]{:S(2)}) copy-start(f32[64,32]{0,1:T(8,128)} %param.21) | copy-start | bytes 24580
  223.1 2.2 collective-permute-start.1
  223.3 3.2 %collective-permute-start.4 = (f32[2,2,4,40,256]{4,3,2,1,0:T(8,128)}, f32[2,2,4,40,256]{4,3,2,1,0:T(8,128)S(1)}, u32[]{:S(2)}, u32[]{:S(2)}) collective-permute-start(f32[2,2,4,40,256]{4,3,2,1,0:T(8,128)} %get-tuple-element.15), channel_id=1, source_target_pairs={{0,8},{8,0},{16,24},{24,16},{1,9},{9,1},{17,25},{25,17},{2,10},{10... | collective-permute-start | bytes 1966088 | tf_op jit(solution)/shard_map/ppermute | solution.py:479
  226.5 8.4 %collective-permute-start.2 = (f32[1,2,4,32,256]{4,3,2,1,0:T(8,128)S(1)}, f32[1,2,4,32,256]{4,3,2,1,0:T(8,128)S(1)}, u32[]{:S(2)}, u32[]{:S(2)}) collective-permute-start(f32[1,2,4,32,256]{4,3,2,1,0:T(8,128)S(1)} %slice.40), channel_id=1, source_target_pairs={{0,16},{8,24},{16,0},{24,8},{1,17},{9,25},{17,1},{25,9},{2,18},{10... | collective-permute-start | bytes 786440 | tf_op jit(solution)/shard_map/ppermute | solution.py:370
  227.8 10.4 %collective-permute-start.5 = (f32[2,1,4,40,256]{4,3,2,1,0:T(8,128)S(1)}, f32[2,1,4,40,256]{4,3,2,1,0:T(8,128)S(1)}, u32[]{:S(2)}, u32[]{:S(2)}) collective-permute-start(f32[2,1,4,40,256]{4,3,2,1,0:T(8,128)S(1)} %slice.44), channel_id=1, source_target_pairs={{0,1},{1,0},{2,3},{3,2},{4,5},{5,4},{6,7},{7,6},{8,9},{9,8},{10,11... | collective-permute-start | bytes 983048 | tf_op jit(solution)/shard_map/ppermute | solution.py:370
  234.9 5.6 %collective-permute-start.3 = (f32[1,1,4,32,256]{4,3,2,1,0:T(8,128)S(1)}, f32[1,1,4,32,256]{4,3,2,1,0:T(8,128)S(1)}, u32[]{:S(2)}, u32[]{:S(2)}) collective-permute-start(f32[1,1,4,32,256]{4,3,2,1,0:T(8,128)S(1)} %slice.42), channel_id=1, source_target_pairs={{0,1},{1,0},{2,3},{3,2},{4,5},{5,4},{6,7},{7,6},{8,9},{9,8},{10,11... | collective-permute-start | bytes 393224 | tf_op jit(solution)/shard_map/ppermute | solution.py:370
  238.3 5.6 %collective-permute-start.6 = (f32[1,1,4,40,256]{4,3,2,1,0:T(8,128)S(1)}, f32[1,1,4,40,256]{4,3,2,1,0:T(8,128)S(1)}, u32[]{:S(2)}, u32[]{:S(2)}) collective-permute-start(f32[1,1,4,40,256]{4,3,2,1,0:T(8,128)S(1)} %slice.46), channel_id=1, source_target_pairs={{0,16},{8,24},{16,0},{24,8},{1,17},{9,25},{17,1},{25,9},{2,18},{10... | collective-permute-start | bytes 491528 | tf_op jit(solution)/shard_map/ppermute | solution.py:370
Sparse Core Ops, SparseCore 0:
  9.5 182.4 all-gather.2

commit v9 on v8

--- a/solution.py
+++ b/solution.py
@@ -73,7 +73,7 @@
 def weight_rings(groups, members):
     round_trip = [(at, 0) for at in range(groups // 2)]
     round_trip += [(at, 1) for at in reversed(range(groups // 2))]
-    length, layers = (len(round_trip), members // 2)
+    length, layers = (len(round_trip), members // 4)
     rings = []
     for core in range(2):
         up, down = ([], [])
@@ -93,16 +93,19 @@
 
 def weight_copies(ring_of, groups, members, source, target, sems):
     pairs = groups // 2
-    columns = source.shape[2]
+    depth = source.shape[2]
     side = lax.rem(lax.axis_index("grp"), 2)
+    far_end = lax.div(lax.axis_index("fsdp"), members // 2)
     rings = weight_rings(groups, members)
 
     def copy(member, pair):
-        spots = [ring.index((2 * pair + core) * members + member) for core, ring in enumerate(rings)]
+        holder = member % (members // 2)
+        spots = [ring.index((2 * pair + core) * members + holder) for core, ring in enumerate(rings)]
         spot = jnp.where(side == ring_of, spots[0], spots[1])
+        swapped = lax.bitwise_xor(far_end, member // (members // 2))
         return pltpu.make_async_copy(
-            source.at[spot],
-            target.at[member, :, pl.ds(pair * columns, columns)],
+            source.at[spot, swapped],
+            target.at[member, pl.ds(pair * depth, depth), :],
             sems.at[member, pair],
         )
 
@@ -110,9 +113,9 @@
 
 
 def wait_block(target, place, pairs, sems):
-    columns = target.shape[2] // pairs
+    depth = target.shape[1] // pairs
     for pair in range(pairs):
-        block = target.at[place, :, pl.ds(pair * columns, columns)]
+        block = target.at[place, pl.ds(pair * depth, depth), :]
         pltpu.make_async_copy(block, block, sems.at[place, pair]).wait()
 
 
@@ -401,10 +404,14 @@
     anywhere = pl.BlockSpec(memory_space=pl.ANY)
 
     half = value_weight.shape[0] // 2
-    piece = kv_width // (groups // 2)
+    depth = half // (groups // 2)
     pair = lax.axis_index("grp") // 2
-    mine = lax.dynamic_slice(value_weight, (side * half, pair * piece), (half, piece))
-    near = lax.all_gather(mine, BOTH, axis=0, axis_index_groups=weight_rings(groups, members))
+    mine = lax.dynamic_slice_in_dim(value_weight, side * half + pair * depth, depth, axis=0)
+    across = [(at, at ^ (members // 2)) for at in range(members)]
+    both = jnp.stack([mine, lax.ppermute(mine, "fsdp", across)])
+    rings = weight_rings(groups, members)
+    rings += [[at + members // 2 for at in ring] for ring in rings]
+    near = lax.all_gather(both, BOTH, axis=0, axis_index_groups=rings)
     swap = [(at, at ^ 1) for at in range(groups)]
     far = lax.ppermute(near, "grp", swap)
 

time: 263 us -> 256 us (0.973)
  waiting for transfers between devices: 186 us -> 170 us
  starting transfers between devices: 10.6 us -> 16.5 us
    all_gather x1, waiting for transfers between devices: 168 us -> 133 us  [body(): near = lax.all_gather(both, BOTH, axis=0, axis_index_groups=rings)]
    ppermute x0 -> x1, waiting for transfers between devices: none -> 23.1 us  [body(): both = jnp.stack([mine, lax.ppermute(mine, 'fsdp', across)])]
    ppermute x0 -> x1, starting transfers between devices: none -> 4.1 us  [body(): both = jnp.stack([mine, lax.ppermute(mine, 'fsdp', across)])]
    ppermute x4, starting transfers between devices: 2.53 us -> 5.92 us  [halve(): package = lax.ppermute(send, axis, pairs) + keep]
    ppermute x4, waiting for transfers between devices: 13.5 us -> 10.1 us  [halve(): package = lax.ppermute(send, axis, pairs) + keep]
  transfers between devices with their start and end apart: 9 -> 10, of which waited for: 6 -> 7; matrix products, arithmetic and copies ran while one was open for 1% -> 1% of each run, Pallas kernels for 7% -> 7%
where the time goes in v9:
time: 256 us
  waiting for transfers between devices  170 us (66%)
  Pallas kernels  35.1 us (14%)
  starting transfers between devices  16.5 us (6%)
  between operations  15.5 us (6%)
  blocking collectives  12.5 us (5%)
  other arithmetic  4.81 us (2%)
    all_gather x1, waiting for transfers between devices, body(): near = lax.all_gather(both, BOTH, axis=0, axis_index_groups=rings)  133 us
    ppermute x1, waiting for transfers between devices, body(): both = jnp.stack([mine, lax.ppermute(mine, 'fsdp', across)])  23.1 us
    pallas_call x1, Pallas kernels, body(): pl.pallas_call(lambda *refs: user_kernel(groups, members, most, *refs), o...  17.6 us
    all_to_all x1, blocking collectives, body(): lax.all_to_all(package, 'fsdp', split_axis=0, concat_axis=0, axis_index_g...  12.5 us
    pallas_call x1, Pallas kernels, body(): pl.pallas_call(lambda *refs: near_kernel(groups, members, most, *refs), o...  10.9 us
    ppermute x4, waiting for transfers between devices, halve(): package = lax.ppermute(send, axis, pairs) + keep  10.1 us
    pallas_call x1, Pallas kernels, body(): pl.pallas_call(lambda *refs: pack_kernel(users, most, *refs), out_shape=j...  6.61 us
    ppermute x4, starting transfers between devices, halve(): package = lax.ppermute(send, axis, pairs) + keep  5.92 us
  transfers between devices with their start and end apart: 10, of which 7 were waited for; matrix products, arithmetic and copies ran while one was open for 1% of the time, Pallas kernels for 7%

profile of v9, /device:TPU:0, one launch (start us, length us, event | category | flops | bytes accessed | tf_op | source)
XLA Modules:
  0.0 256.0 jit_solution(10723582196529509439)
XLA Ops:
  7.2 0.0 copy-start
  7.2 0.0 all-gather.3.cloned.1.call-start
  7.2 1.5 copy-done
  8.8 4.1 %collective-permute-start = (bf16[256,1024]{1,0:T(8,128)(2,1)S(1)}, bf16[256,1024]{1,0:T(8,128)(2,1)S(1)}, u32[]{:S(2)}, u32[]{:S(2)}) collective-permute-start(bf16[256,1024]{1,0:T(8,128)(2,1)S(1)} %constant_dynamic-slice_fusion), channel_id=1, source_target_pairs={{0,4},{1,5},{2,6},{3,7},{4,0},{5,1},{6,2},{7,3},{8,12},{9,13},{10,... | collective-permute-start | bytes 1572872 | tf_op jit(solution)/shard_map/ppermute | solution.py:411
  12.9 23.1 %collective-permute-done = bf16[256,1024]{1,0:T(8,128)(2,1)S(1)} collective-permute-done((bf16[256,1024]{1,0:T(8,128)(2,1)S(1)}, bf16[256,1024]{1,0:T(8,128)(2,1)S(1)}, u32[]{:S(2)}, u32[]{:S(2)}) %collective-permute-start) | collective-permute-done | bytes 524320 | tf_op jit(solution)/shard_map/ppermute | solution.py:411
  36.1 1.1 pad_maximum_fusion
  37.1 0.0 all-gather.3.cloned.1.call-update
  37.8 6.6 %pack_rows.1 = bf16[256,10496]{1,0:T(8,128)(2,1)} custom-call(s32[1]{0:T(128)S(6)} %copy.16.refs_0_, s32[1,192]{1,0:T(1,128)} %bitcast.31, bf16[192,8192]{1,0:T(8,128)(2,1)} %refs_2_.1, bf16[192,1024]{1,0:T(8,128)(2,1)} %refs_3_.1), custom_call_target="tpu_custom_call" | custom-call | tf_op jit(solution)/shard_map/pack_rows/pallas_call | solution.py:419
  44.4 5.9 %all-to-all-start = ((bf16[32,8,10496]{2,1,0:T(8,128)(2,1)}), bf16[32,8,10496]{2,1,0:T(8,128)(2,1)}, u32[]{:S(2)}, u32[]{:S(2)}) async-start(bf16[32,8,10496]{2,1,0:T(8,128)(2,1)} %bitcast.25), calls=%async_computation | async-start | bytes 10747904 | tf_op jit(solution)/shard_map/all_to_all | solution.py:431
  50.3 133.0 %all-gather.3.cloned.1.call-done = bf16[16,256,1024]{2,1,0:T(8,128)(2,1)} async-done(((bf16[2,256,1024]{2,1,0:T(8,128)(2,1)}), bf16[16,256,1024]{2,1,0:T(8,128)(2,1)}) %all-gather.3.cloned.1.call-update) | async-done | bytes 8388624 | tf_op jit(solution)/shard_map/all_gather | solution.py:414
  183.3 0.0 collective-permute-start.1
  184.0 0.0 all-to-all-done
  184.0 10.9 %near_product.1 = (bf16[288,8192]{1,0:T(8,128)(2,1)}, f32[288,1024]{1,0:T(8,128)}, f32[288,64]{1,0:T(8,128)}) custom-call(bf16[256,10496]{1,0:T(8,128)(2,1)} %bitcast.2.refs_0_.refs_2_, bf16[8,2,256,1024]{3,2,1,0:T(8,128)(2,1)} %bitcast.27, bf16[64,8192]{1,0:T(8,128)(2,1)} %bitcast.28), custom_call_target="tpu_custom_call" | custom-call | flops 2415919104 | bytes 30000000 | tf_op jit(solution)/shard_map/near_product/pallas_call | solution.py:437
  194.9 1.9 collective-permute-done.1.refs_6_
  196.8 17.6 %user_steps.1 = (f32[2,2,4,32,256]{4,3,2,1,0:T(8,128)}, f32[2,2,4,40,256]{4,3,2,1,0:T(8,128)}, f32[2,2,4,32,256]{4,3,2,1,0:T(8,128)}, f32[2,2,4,40,256]{4,3,2,1,0:T(8,128)}) custom-call(s32[32]{0:T(128)} %refs_0_.2, f32[1]{0:T(128)} %copy.17.refs_1_, bf16[256,10496]{1,0:T(8,128)(2,1)} %bitcast.2.refs_0_.refs_2_, bf16[288,8192]{1,0:T(8,128)(2,1)} %get-tuple-element.9.refs_3_, ...), custom_call_target="tpu_custom_call" | custom-call | tf_op jit(solution)/shard_map/user_steps/pallas_call | solution.py:464
  214.4 0.1 collective-permute-start.2
  214.6 0.4 collective-permute-start.5
  215.0 1.6 collective-permute-done.2
  216.6 0.0 copy-start.1
  216.6 0.0 copy-start.2
  216.6 1.1 add.38
  217.8 0.3 collective-permute-start.3
  218.1 0.0 collective-permute-done.5
  218.1 1.2 add.41
  219.4 1.8 collective-permute-start.6
  221.1 5.1 %collective-permute-done.3 = f32[1,2,4,32,256]{4,3,2,1,0:T(8,128)S(1)} collective-permute-done((f32[1,2,4,32,256]{4,3,2,1,0:T(8,128)S(1)}, f32[1,2,4,32,256]{4,3,2,1,0:T(8,128)S(1)}, u32[]{:S(2)}, u32[]{:S(2)}) %collective-permute-start.3) | collective-permute-done | bytes 262176 | tf_op jit(solution)/shard_map/ppermute | solution.py:373
  226.3 1.5 collective-permute-start.4
  227.8 1.8 collective-permute-done.6
  229.6 2.3 collective-permute-start.7
  231.9 0.0 collective-permute-done.4
  231.9 3.3 %collective-permute-done.7 = f32[1,1,4,40,256]{4,3,2,1,0:T(8,128)S(1)} collective-permute-done((f32[1,1,4,40,256]{4,3,2,1,0:T(8,128)S(1)}, f32[1,1,4,40,256]{4,3,2,1,0:T(8,128)S(1)}, u32[]{:S(2)}, u32[]{:S(2)}) %collective-permute-start.7) | collective-permute-done | bytes 163872 | tf_op jit(solution)/shard_map/ppermute | solution.py:373
  235.3 12.5 %all_to_all.10 = f32[4,72,256]{2,1,0:T(8,128)S(1)} all-to-all(f32[4,72,256]{2,1,0:T(8,128)S(1)} %pad_maximum_fusion.1), channel_id=1, replica_groups={{0,2,4,6},{1,3,5,7},{8,10,12,14},{9,11,13,15},{16,18,20,22},{17,19,21,2..., dimensions={0} | all-to-all | bytes 589824 | tf_op jit(solution)/shard_map/all_to_all | solution.py:491
  247.8 0.1 reshape.22
  247.9 0.0 copy-done.1
  247.9 0.6 fusion.2
  248.5 0.0 copy-done.2
  248.5 0.6 bitcast_add_fusion
  (13 shorter events, 0.3 us)
Async XLA Ops:
  7.2 1.6 copy-start
  7.2 176.1 %all-gather.3.cloned.1.call-start = ((), (), s32[]{:S(2)}) async-start(), calls=%async_computation.2 | async-start | bytes 9437184 | tf_op jit(solution)/shard_map/all_gather | solution.py:414
  8.8 27.3 %collective-permute-start = (bf16[256,1024]{1,0:T(8,128)(2,1)S(1)}, bf16[256,1024]{1,0:T(8,128)(2,1)S(1)}, u32[]{:S(2)}, u32[]{:S(2)}) collective-permute-start(bf16[256,1024]{1,0:T(8,128)(2,1)S(1)} %constant_dynamic-slice_fusion), channel_id=1, source_target_pairs={{0,4},{1,5},{2,6},{3,7},{4,0},{5,1},{6,2},{7,3},{8,12},{9,13},{10,... | collective-permute-start | bytes 1572872 | tf_op jit(solution)/shard_map/ppermute | solution.py:411
  44.4 139.6 %all-to-all-start = ((bf16[32,8,10496]{2,1,0:T(8,128)(2,1)}), bf16[32,8,10496]{2,1,0:T(8,128)(2,1)}, u32[]{:S(2)}, u32[]{:S(2)}) async-start(bf16[32,8,10496]{2,1,0:T(8,128)(2,1)} %bitcast.25), calls=%async_computation | async-start | bytes 10747904 | tf_op jit(solution)/shard_map/all_to_all | solution.py:431
  183.3 13.5 %collective-permute-start.1 = (bf16[8,2,256,1024]{3,2,1,0:T(8,128)(2,1)}, bf16[8,2,256,1024]{3,2,1,0:T(8,128)(2,1)}, u32[]{:S(2)}, u32[]{:S(2)}) collective-permute-start(bf16[8,2,256,1024]{3,2,1,0:T(8,128)(2,1)} %bitcast.26), channel_id=1, source_target_pairs={{0,8},{8,0},{16,24},{24,16},{1,9},{9,1},{17,25},{25,17},{2,10},{10... | collective-permute-start | bytes 25165832 | tf_op jit(solution)/shard_map/ppermute | solution.py:416
  214.4 2.2 collective-permute-start.2
  214.6 3.6 %collective-permute-start.5 = (f32[2,2,4,40,256]{4,3,2,1,0:T(8,128)}, f32[2,2,4,40,256]{4,3,2,1,0:T(8,128)S(1)}, u32[]{:S(2)}, u32[]{:S(2)}) collective-permute-start(f32[2,2,4,40,256]{4,3,2,1,0:T(8,128)} %get-tuple-element.15), channel_id=1, source_target_pairs={{0,8},{8,0},{16,24},{24,16},{1,9},{9,1},{17,25},{25,17},{2,10},{10... | collective-permute-start | bytes 1966088 | tf_op jit(solution)/shard_map/ppermute | solution.py:486
  216.6 31.2 %copy-start.1 = (f32[256,64]{0,1:T(8,128)S(1)}, f32[256,64]{0,1:T(8,128)}, u32[]{:S(2)}) copy-start(f32[256,64]{0,1:T(8,128)} %param.20) | copy-start | bytes 196612
  216.6 31.9 %copy-start.2 = (f32[64,32]{0,1:T(8,128)S(1)}, f32[64,32]{0,1:T(8,128)}, u32[]{:S(2)}) copy-start(f32[64,32]{0,1:T(8,128)} %param.21) | copy-start | bytes 24580
  217.8 8.4 %collective-permute-start.3 = (f32[1,2,4,32,256]{4,3,2,1,0:T(8,128)S(1)}, f32[1,2,4,32,256]{4,3,2,1,0:T(8,128)S(1)}, u32[]{:S(2)}, u32[]{:S(2)}) collective-permute-start(f32[1,2,4,32,256]{4,3,2,1,0:T(8,128)S(1)} %slice.40), channel_id=1, source_target_pairs={{0,16},{8,24},{16,0},{24,8},{1,17},{9,25},{17,1},{25,9},{2,18},{10... | collective-permute-start | bytes 786440 | tf_op jit(solution)/shard_map/ppermute | solution.py:373
  219.4 10.2 %collective-permute-start.6 = (f32[2,1,4,40,256]{4,3,2,1,0:T(8,128)S(1)}, f32[2,1,4,40,256]{4,3,2,1,0:T(8,128)S(1)}, u32[]{:S(2)}, u32[]{:S(2)}) collective-permute-start(f32[2,1,4,40,256]{4,3,2,1,0:T(8,128)S(1)} %slice.44), channel_id=1, source_target_pairs={{0,1},{1,0},{2,3},{3,2},{4,5},{5,4},{6,7},{7,6},{8,9},{9,8},{10,11... | collective-permute-start | bytes 983048 | tf_op jit(solution)/shard_map/ppermute | solution.py:373
  226.3 5.6 %collective-permute-start.4 = (f32[1,1,4,32,256]{4,3,2,1,0:T(8,128)S(1)}, f32[1,1,4,32,256]{4,3,2,1,0:T(8,128)S(1)}, u32[]{:S(2)}, u32[]{:S(2)}) collective-permute-start(f32[1,1,4,32,256]{4,3,2,1,0:T(8,128)S(1)} %slice.42), channel_id=1, source_target_pairs={{0,1},{1,0},{2,3},{3,2},{4,5},{5,4},{6,7},{7,6},{8,9},{9,8},{10,11... | collective-permute-start | bytes 393224 | tf_op jit(solution)/shard_map/ppermute | solution.py:373
  229.6 5.6 %collective-permute-start.7 = (f32[1,1,4,40,256]{4,3,2,1,0:T(8,128)S(1)}, f32[1,1,4,40,256]{4,3,2,1,0:T(8,128)S(1)}, u32[]{:S(2)}, u32[]{:S(2)}) collective-permute-start(f32[1,1,4,40,256]{4,3,2,1,0:T(8,128)S(1)} %slice.46), channel_id=1, source_target_pairs={{0,16},{8,24},{16,0},{24,8},{1,17},{9,25},{17,1},{25,9},{2,18},{10... | collective-permute-start | bytes 491528 | tf_op jit(solution)/shard_map/ppermute | solution.py:373
Sparse Core Ops, SparseCore 0:
  37.3 145.9 all-gather.2

commit v10 on v9

--- a/solution.py
+++ b/solution.py
@@ -91,25 +91,32 @@
     return rings
 
 
-def weight_copies(ring_of, groups, members, source, target, sems):
+def start_weights(ring_of, groups, members, sources, target, sems):
     pairs = groups // 2
-    depth = source.shape[2]
+    depth = sources[0].shape[1]
     side = lax.rem(lax.axis_index("grp"), 2)
     far_end = lax.div(lax.axis_index("fsdp"), members // 2)
     rings = weight_rings(groups, members)
 
-    def copy(member, pair):
-        holder = member % (members // 2)
-        spots = [ring.index((2 * pair + core) * members + holder) for core, ring in enumerate(rings)]
-        spot = jnp.where(side == ring_of, spots[0], spots[1])
-        swapped = lax.bitwise_xor(far_end, member // (members // 2))
-        return pltpu.make_async_copy(
-            source.at[spot, swapped],
-            target.at[member, pl.ds(pair * depth, depth), :],
-            sems.at[member, pair],
-        )
-
-    return [[copy(member, pair) for pair in range(pairs)] for member in range(members)]
+    def start(member):
+        end, holder = divmod(member, members // 2)
+        for swapped, source in enumerate(sources):
+
+            @pl.when(far_end == (1 - end if swapped else end))
+            def _():
+                for pair in range(pairs):
+                    spots = [
+                        ring.index((2 * pair + core) * members + holder)
+                        for core, ring in enumerate(rings)
+                    ]
+                    spot = jnp.where(side == ring_of, spots[0], spots[1])
+                    pltpu.make_async_copy(
+                        source.at[spot],
+                        target.at[member, pl.ds(pair * depth, depth), :],
+                        sems.at[member, pair],
+                    ).start()
+
+    return start
 
 
 def wait_block(target, place, pairs, sems):
@@ -125,6 +132,7 @@
     most,
     got_ref,
     near_ref,
+    near_swapped_ref,
     down_ref,
     x_out_ref,
     frozen_ref,
@@ -157,13 +165,12 @@
     ]
     for copy in copies:
         copy.start()
-    weights = weight_copies(0, groups_of, members, near_ref, w_ref, w_sem)
-    for place, pieces in enumerate(weights):
-        if place == 2:
+    start = start_weights(0, groups_of, members, (near_ref, near_swapped_ref), w_ref, w_sem)
+    for member in range(members):
+        if member == 2:
             for copy in copies:
                 copy.wait()
-        for copy in pieces:
-            copy.start()
+        start(member)
     join_pieces(devices, groups * whole, rest, x_ref, cut_ref)
     out = pltpu.make_async_copy(x_ref, x_out_ref, out_sem)
     out.start()
@@ -209,6 +216,7 @@
     near_frozen_ref,
     near_hidden_ref,
     far_ref,
+    far_swapped_ref,
     down_ref,
     up_ref,
     *refs,
@@ -249,9 +257,9 @@
     ]
     for copy in copies[1:] + copies[:1]:
         copy.start()
-    for pieces in weight_copies(1, groups_of, members, far_ref, w_ref, w_sem):
-        for copy in pieces:
-            copy.start()
+    start = start_weights(1, groups_of, members, (far_ref, far_swapped_ref), w_ref, w_sem)
+    for member in range(members):
+        start(member)
     for copy in copies[1:]:
         copy.wait()
     join_pieces(devices, groups * whole, rest, goal_ref, cut_goal_ref)
@@ -408,12 +416,10 @@
     pair = lax.axis_index("grp") // 2
     mine = lax.dynamic_slice_in_dim(value_weight, side * half + pair * depth, depth, axis=0)
     across = [(at, at ^ (members // 2)) for at in range(members)]
-    both = jnp.stack([mine, lax.ppermute(mine, "fsdp", across)])
+    swapped = lax.ppermute(mine, "fsdp", across)
     rings = weight_rings(groups, members)
     rings += [[at + members // 2 for at in ring] for ring in rings]
-    near = lax.all_gather(both, BOTH, axis=0, axis_index_groups=rings)
     swap = [(at, at ^ 1) for at in range(groups)]
-    far = lax.ppermute(near, "grp", swap)
 
     columns = whole_groups * (width + kv_width) + rest * (width + kv_width) // SUB + LANES
     packed = pl.pallas_call(
@@ -428,6 +434,11 @@
         compiler_params=pltpu.CompilerParams(vmem_limit_bytes=VMEM_BYTES),
         name="pack_rows",
     )(device_row_count, row_owner_user.reshape(1, per_dev), tokens, targets)
+    near = lax.all_gather(mine, BOTH, axis=0, axis_index_groups=rings)
+    packed, swapped = lax.optimization_barrier((packed, swapped))
+    near_swapped = lax.all_gather(swapped, BOTH, axis=0, axis_index_groups=rings)
+    far = lax.ppermute(near, "grp", swap)
+    far_swapped = lax.ppermute(near_swapped, "grp", swap)
     got = lax.all_to_all(
         packed.reshape(users, SUB, columns), BOTH, split_axis=0, concat_axis=0, tiled=True
     ).reshape(whole, columns)
@@ -441,7 +452,7 @@
             jax.ShapeDtypeStruct((slots, kv_width), F32),
             jax.ShapeDtypeStruct((slots, rank), F32),
         ],
-        in_specs=[anywhere, anywhere, vmem],
+        in_specs=[anywhere, anywhere, anywhere, vmem],
         out_specs=[anywhere, vmem, vmem],
         scratch_shapes=[
             pltpu.VMEM((slots, width), BF16),
@@ -456,7 +467,7 @@
             flops=slots * width * kv_width, bytes_accessed=3 * 10**7, transcendentals=0
         ),
         name="near_product",
-    )(got, near, down)
+    )(got, near, near_swapped, down)
 
     edge = tall // (2 * SUB) * SUB
     grid = (groups // 2, 2, members // 2)
@@ -464,7 +475,7 @@
     kept_y, kept_x, sent_y, sent_x = pl.pallas_call(
         lambda *refs: user_kernel(groups, members, most, *refs),
         out_shape=streams * 2,
-        in_specs=[smem, smem, anywhere, anywhere, vmem, vmem, anywhere, vmem, vmem],
+        in_specs=[smem] * 2 + [anywhere] * 2 + [vmem] * 2 + [anywhere] * 2 + [vmem] * 2,
         out_specs=[vmem] * 4,
         scratch_shapes=[
             pltpu.VMEM((slots, width), BF16),
@@ -480,7 +491,18 @@
         ],
         compiler_params=pltpu.CompilerParams(vmem_limit_bytes=VMEM_BYTES),
         name="user_steps",
-    )(user_row_cap, clip_norm_bound, got, rows, near_frozen, near_hidden, far, down, adapter_up)
+    )(
+        user_row_cap,
+        clip_norm_bound,
+        got,
+        rows,
+        near_frozen,
+        near_hidden,
+        far,
+        far_swapped,
+        down,
+        adapter_up,
+    )
 
     first = kept_y + lax.ppermute(sent_y, "grp", swap)
     second = kept_x + lax.ppermute(sent_x, "grp", swap)

time: 256 us -> 253 us (0.988)
  starting transfers between devices: 16.5 us -> 13.2 us
    ppermute x1 -> x2, waiting for transfers between devices: 23.1 us -> 16.2 us  [the longest x1 16.2 us: body(): swapped = lax.ppermute(mine, 'fsdp', across)]
    all_gather x1 -> x2, waiting for transfers between devices: 133 us -> 140 us  [the longest x1 70 us: body(): lax.all_gather(swapped, BOTH, axis=0, axis_index_groups=rings)]
    ppermute x4, starting transfers between devices: 5.92 us -> 2.51 us  [halve(): package = lax.ppermute(send, axis, pairs) + keep]
    ppermute x4, waiting for transfers between devices: 10.1 us -> 13.5 us  [halve(): package = lax.ppermute(send, axis, pairs) + keep]
  transfers between devices with their start and end apart: 10 -> 12, of which waited for: 7 -> 8; matrix products, arithmetic and copies ran while one was open for 1% -> 1% of each run, Pallas kernels for 7% -> 7%
where the time goes in v10:
time: 253 us
  waiting for transfers between devices  171 us (68%)
  Pallas kernels  35.3 us (14%)
  between operations  15.5 us (6%)
  starting transfers between devices  13.2 us (5%)
  blocking collectives  10.4 us (4%)
  other arithmetic  3.7 us (1%)
  local copies, waits for them, and re-layouts  3.34 us (1%)
    all_gather x1, waiting for transfers between devices, body(): lax.all_gather(swapped, BOTH, axis=0, axis_index_groups=rings)  70 us
    all_gather x1, waiting for transfers between devices, body(): near = lax.all_gather(mine, BOTH, axis=0, axis_index_groups=rings)  69.7 us
    pallas_call x1, Pallas kernels, body(): pl.pallas_call(lambda *refs: user_kernel(groups, members, most, *refs), o...  17.5 us
    ppermute x1, waiting for transfers between devices, body(): swapped = lax.ppermute(mine, 'fsdp', across)  16.2 us
    ppermute x4, waiting for transfers between devices, halve(): package = lax.ppermute(send, axis, pairs) + keep  13.5 us
    pallas_call x1, Pallas kernels, body(): pl.pallas_call(lambda *refs: near_kernel(groups, members, most, *refs), o...  11.1 us
    all_to_all x1, blocking collectives, body(): lax.all_to_all(package, 'fsdp', split_axis=0, concat_axis=0, axis_index_g...  10.4 us
    pallas_call x1, Pallas kernels, body(): pl.pallas_call(lambda *refs: pack_kernel(users, most, *refs), out_shape=j...  6.62 us
  transfers between devices with their start and end apart: 12, of which 8 were waited for; matrix products, arithmetic and copies ran while one was open for 1% of the time, Pallas kernels for 7%

profile of v10, /device:TPU:0, one launch (start us, length us, event | category | flops | bytes accessed | tf_op | source)
XLA Modules:
  0.0 252.6 jit_solution(1285391508352331247)
XLA Ops:
  7.2 0.0 copy-start
  7.2 0.0 all-gather.5.cloned.1.call-start
  7.2 1.5 copy-done
  8.8 0.8 constant_dynamic-slice_fusion
  9.6 0.0 all-gather.5.cloned.1.call-update
  9.6 0.0 all-gather.7.cloned.1.call-start
  9.7 4.1 %collective-permute-start = (bf16[256,1024]{1,0:T(8,128)(2,1)}, bf16[256,1024]{1,0:T(8,128)(2,1)S(1)}, u32[]{:S(2)}, u32[]{:S(2)}) collective-permute-start(bf16[256,1024]{1,0:T(8,128)(2,1)} %constant_dynamic-slice_fusion), channel_id=1, source_target_pairs={{0,4},{1,5},{2,6},{3,7},{4,0},{5,1},{6,2},{7,3},{8,12},{9,13},{10,... | collective-permute-start | bytes 1572872 | tf_op jit(solution)/shard_map/ppermute | solution.py:419
  14.4 6.6 %pack_rows.1 = bf16[256,10496]{1,0:T(8,128)(2,1)} custom-call(s32[1]{0:T(128)S(6)} %copy.15.refs_0_, s32[1,192]{1,0:T(1,128)} %bitcast.30, bf16[192,8192]{1,0:T(8,128)(2,1)} %refs_2_.1, bf16[192,1024]{1,0:T(8,128)(2,1)} %refs_3_.1), custom_call_target="tpu_custom_call" | custom-call | tf_op jit(solution)/shard_map/pack_rows/pallas_call | solution.py:425
  21.0 16.2 %collective-permute-done = bf16[256,1024]{1,0:T(8,128)(2,1)S(1)} collective-permute-done((bf16[256,1024]{1,0:T(8,128)(2,1)}, bf16[256,1024]{1,0:T(8,128)(2,1)S(1)}, u32[]{:S(2)}, u32[]{:S(2)}) %collective-permute-start) | collective-permute-done | bytes 524320 | tf_op jit(solution)/shard_map/ppermute | solution.py:419
  37.2 0.0 copy-start.1
  37.3 0.8 copy-done.1
  38.1 0.0 all-gather.7.cloned.1.call-update
  38.1 5.9 %all-to-all-start = ((bf16[32,8,10496]{2,1,0:T(8,128)(2,1)}), bf16[32,8,10496]{2,1,0:T(8,128)(2,1)}, u32[]{:S(2)}, u32[]{:S(2)}) async-start(bf16[32,8,10496]{2,1,0:T(8,128)(2,1)} %bitcast.23), calls=%async_computation | async-start | bytes 10747904 | tf_op jit(solution)/shard_map/all_to_all | solution.py:442
  44.0 69.7 %all-gather.5.cloned.1.call-done = bf16[2048,1024]{1,0:T(8,128)(2,1)} async-done(((bf16[256,1024]{1,0:T(8,128)(2,1)}), bf16[2048,1024]{1,0:T(8,128)(2,1)}) %all-gather.5.cloned.1.call-update) | async-done | bytes 4194320 | tf_op jit(solution)/shard_map/all_gather | solution.py:437
  113.7 0.0 collective-permute-start.1
  113.7 70.0 %all-gather.7.cloned.1.call-done = bf16[2048,1024]{1,0:T(8,128)(2,1)} async-done(((bf16[256,1024]{1,0:T(8,128)(2,1)}), bf16[2048,1024]{1,0:T(8,128)(2,1)}) %all-gather.7.cloned.1.call-update) | async-done | bytes 4194320 | tf_op jit(solution)/shard_map/all_gather | solution.py:439
  183.7 0.0 collective-permute-start.2
  184.4 0.0 all-to-all-done
  184.4 11.1 %near_product.1 = (bf16[288,8192]{1,0:T(8,128)(2,1)}, f32[288,1024]{1,0:T(8,128)}, f32[288,64]{1,0:T(8,128)}) custom-call(bf16[256,10496]{1,0:T(8,128)(2,1)} %bitcast.2.refs_0_.refs_2_, bf16[8,256,1024]{2,1,0:T(8,128)(2,1)} %bitcast.27, bf16[8,256,1024]{2,1,0:T(8,128)(2,1)} %bitcast.29, bf16[64,8192]{1,0:T(8,128)(2,1)} %bitcast.24), custom_call_target="tpu_custom_call" | custom-call | flops 2415919104 | bytes 30000000 | tf_op jit(solution)/shard_map/near_product/pallas_call | solution.py:448
  195.5 0.0 collective-permute-done.1.refs_6_
  195.5 0.0 collective-permute-done.2.refs_7_
  195.5 17.5 %user_steps.1 = (f32[2,2,4,32,256]{4,3,2,1,0:T(8,128)}, f32[2,2,4,40,256]{4,3,2,1,0:T(8,128)}, f32[2,2,4,32,256]{4,3,2,1,0:T(8,128)}, f32[2,2,4,40,256]{4,3,2,1,0:T(8,128)}) custom-call(s32[32]{0:T(128)} %refs_0_.2, f32[1]{0:T(128)} %copy.16.refs_1_, bf16[256,10496]{1,0:T(8,128)(2,1)} %bitcast.2.refs_0_.refs_2_, ...), custom_call_target="tpu_custom_call" | custom-call | tf_op jit(solution)/shard_map/user_steps/pallas_call | solution.py:475
  213.1 0.5 collective-permute-start.3
  213.6 0.1 collective-permute-start.6
  213.7 1.7 collective-permute-done.3
  215.4 1.1 add.38
  216.5 0.0 copy-start.2
  216.5 0.0 copy-start.3
  216.5 0.1 collective-permute-start.4
  216.6 0.0 collective-permute-done.6
  216.6 1.2 add.41
  217.8 0.1 collective-permute-start.7
  217.9 7.3 %collective-permute-done.4 = f32[1,2,4,32,256]{4,3,2,1,0:T(8,128)S(1)} collective-permute-done((f32[1,2,4,32,256]{4,3,2,1,0:T(8,128)S(1)}, f32[1,2,4,32,256]{4,3,2,1,0:T(8,128)S(1)}, u32[]{:S(2)}, u32[]{:S(2)}) %collective-permute-start.4) | collective-permute-done | bytes 262176 | tf_op jit(solution)/shard_map/ppermute | solution.py:381
  225.2 0.1 collective-permute-start.5
  225.3 2.9 %collective-permute-done.7 = f32[2,1,4,40,256]{4,3,2,1,0:T(8,128)S(1)} collective-permute-done((f32[2,1,4,40,256]{4,3,2,1,0:T(8,128)S(1)}, f32[2,1,4,40,256]{4,3,2,1,0:T(8,128)S(1)}, u32[]{:S(2)}, u32[]{:S(2)}) %collective-permute-start.7) | collective-permute-done | bytes 327712 | tf_op jit(solution)/shard_map/ppermute | solution.py:381
  228.3 2.3 collective-permute-start.8
  230.6 0.1 collective-permute-done.5
  230.7 3.2 %collective-permute-done.8 = f32[1,1,4,40,256]{4,3,2,1,0:T(8,128)S(1)} collective-permute-done((f32[1,1,4,40,256]{4,3,2,1,0:T(8,128)S(1)}, f32[1,1,4,40,256]{4,3,2,1,0:T(8,128)S(1)}, u32[]{:S(2)}, u32[]{:S(2)}) %collective-permute-start.8) | collective-permute-done | bytes 163872 | tf_op jit(solution)/shard_map/ppermute | solution.py:381
  234.0 10.4 %all_to_all.10 = f32[4,72,256]{2,1,0:T(8,128)S(1)} all-to-all(f32[4,72,256]{2,1,0:T(8,128)S(1)} %pad_maximum_fusion), channel_id=1, replica_groups={{0,2,4,6},{1,3,5,7},{8,10,12,14},{9,11,13,15},{16,18,20,22},{17,19,21,2..., dimensions={0} | all-to-all | bytes 589824 | tf_op jit(solution)/shard_map/all_to_all | solution.py:513
  244.5 0.1 reshape.22
  244.5 0.0 copy-done.2
  244.5 0.6 fusion.2
  245.2 0.0 copy-done.3
  245.2 0.6 bitcast_add_fusion
  (11 shorter events, 0.2 us)
Async XLA Ops:
  7.2 1.6 copy-start
  7.2 106.5 %all-gather.5.cloned.1.call-start = ((), (), s32[]{:S(2)}) async-start(), calls=%async_computation.2 | async-start | bytes 4718592 | tf_op jit(solution)/shard_map/all_gather | solution.py:437
  9.6 174.1 %all-gather.7.cloned.1.call-start = ((), (), s32[]{:S(2)}) async-start(), calls=%async_computation.3 | async-start | bytes 4718592 | tf_op jit(solution)/shard_map/all_gather | solution.py:439
  9.7 27.6 %collective-permute-start = (bf16[256,1024]{1,0:T(8,128)(2,1)}, bf16[256,1024]{1,0:T(8,128)(2,1)S(1)}, u32[]{:S(2)}, u32[]{:S(2)}) collective-permute-start(bf16[256,1024]{1,0:T(8,128)(2,1)} %constant_dynamic-slice_fusion), channel_id=1, source_target_pairs={{0,4},{1,5},{2,6},{3,7},{4,0},{5,1},{6,2},{7,3},{8,12},{9,13},{10,... | collective-permute-start | bytes 1572872 | tf_op jit(solution)/shard_map/ppermute | solution.py:419
  37.2 0.8 copy-start.1
  38.1 146.3 %all-to-all-start = ((bf16[32,8,10496]{2,1,0:T(8,128)(2,1)}), bf16[32,8,10496]{2,1,0:T(8,128)(2,1)}, u32[]{:S(2)}, u32[]{:S(2)}) async-start(bf16[32,8,10496]{2,1,0:T(8,128)(2,1)} %bitcast.23), calls=%async_computation | async-start | bytes 10747904 | tf_op jit(solution)/shard_map/all_to_all | solution.py:442
  113.7 81.8 %collective-permute-start.1 = (bf16[8,256,1024]{2,1,0:T(8,128)(2,1)}, bf16[8,256,1024]{2,1,0:T(8,128)(2,1)}, u32[]{:S(2)}, u32[]{:S(2)}) collective-permute-start(bf16[8,256,1024]{2,1,0:T(8,128)(2,1)} %bitcast.26), channel_id=1, source_target_pairs={{0,8},{8,0},{16,24},{24,16},{1,9},{9,1},{17,25},{25,17},{2,10},{10... | collective-permute-start | bytes 12582920 | tf_op jit(solution)/shard_map/ppermute | solution.py:440
  183.7 11.8 %collective-permute-start.2 = (bf16[8,256,1024]{2,1,0:T(8,128)(2,1)}, bf16[8,256,1024]{2,1,0:T(8,128)(2,1)}, u32[]{:S(2)}, u32[]{:S(2)}) collective-permute-start(bf16[8,256,1024]{2,1,0:T(8,128)(2,1)} %bitcast.28), channel_id=1, source_target_pairs={{0,8},{8,0},{16,24},{24,16},{1,9},{9,1},{17,25},{25,17},{2,10},{10... | collective-permute-start | bytes 12582920 | tf_op jit(solution)/shard_map/ppermute | solution.py:441
  213.1 2.3 collective-permute-start.3
  213.6 3.0 %collective-permute-start.6 = (f32[2,2,4,40,256]{4,3,2,1,0:T(8,128)}, f32[2,2,4,40,256]{4,3,2,1,0:T(8,128)S(1)}, u32[]{:S(2)}, u32[]{:S(2)}) collective-permute-start(f32[2,2,4,40,256]{4,3,2,1,0:T(8,128)} %get-tuple-element.19), channel_id=1, source_target_pairs={{0,8},{8,0},{16,24},{24,16},{1,9},{9,1},{17,25},{25,17},{2,10},{10... | collective-permute-start | bytes 1966088 | tf_op jit(solution)/shard_map/ppermute | solution.py:508
  216.5 28.1 %copy-start.2 = (f32[256,64]{0,1:T(8,128)S(1)}, f32[256,64]{0,1:T(8,128)}, u32[]{:S(2)}) copy-start(f32[256,64]{0,1:T(8,128)} %param.20) | copy-start | bytes 196612
  216.5 28.7 %copy-start.3 = (f32[64,32]{0,1:T(8,128)S(1)}, f32[64,32]{0,1:T(8,128)}, u32[]{:S(2)}) copy-start(f32[64,32]{0,1:T(8,128)} %param.21) | copy-start | bytes 24580
  216.5 8.7 %collective-permute-start.4 = (f32[1,2,4,32,256]{4,3,2,1,0:T(8,128)S(1)}, f32[1,2,4,32,256]{4,3,2,1,0:T(8,128)S(1)}, u32[]{:S(2)}, u32[]{:S(2)}) collective-permute-start(f32[1,2,4,32,256]{4,3,2,1,0:T(8,128)S(1)} %slice.40), channel_id=1, source_target_pairs={{0,16},{8,24},{16,0},{24,8},{1,17},{9,25},{17,1},{25,9},{2,18},{10... | collective-permute-start | bytes 786440 | tf_op jit(solution)/shard_map/ppermute | solution.py:381
  217.8 10.4 %collective-permute-start.7 = (f32[2,1,4,40,256]{4,3,2,1,0:T(8,128)S(1)}, f32[2,1,4,40,256]{4,3,2,1,0:T(8,128)S(1)}, u32[]{:S(2)}, u32[]{:S(2)}) collective-permute-start(f32[2,1,4,40,256]{4,3,2,1,0:T(8,128)S(1)} %slice.44), channel_id=1, source_target_pairs={{0,1},{1,0},{2,3},{3,2},{4,5},{5,4},{6,7},{7,6},{8,9},{9,8},{10,11... | collective-permute-start | bytes 983048 | tf_op jit(solution)/shard_map/ppermute | solution.py:381
  225.2 5.5 %collective-permute-start.5 = (f32[1,1,4,32,256]{4,3,2,1,0:T(8,128)S(1)}, f32[1,1,4,32,256]{4,3,2,1,0:T(8,128)S(1)}, u32[]{:S(2)}, u32[]{:S(2)}) collective-permute-start(f32[1,1,4,32,256]{4,3,2,1,0:T(8,128)S(1)} %slice.42), channel_id=1, source_target_pairs={{0,1},{1,0},{2,3},{3,2},{4,5},{5,4},{6,7},{7,6},{8,9},{9,8},{10,11... | collective-permute-start | bytes 393224 | tf_op jit(solution)/shard_map/ppermute | solution.py:381
  228.3 5.6 %collective-permute-start.8 = (f32[1,1,4,40,256]{4,3,2,1,0:T(8,128)S(1)}, f32[1,1,4,40,256]{4,3,2,1,0:T(8,128)S(1)}, u32[]{:S(2)}, u32[]{:S(2)}) collective-permute-start(f32[1,1,4,40,256]{4,3,2,1,0:T(8,128)S(1)} %slice.46), channel_id=1, source_target_pairs={{0,16},{8,24},{16,0},{24,8},{1,17},{9,25},{17,1},{25,9},{2,18},{10... | collective-permute-start | bytes 491528 | tf_op jit(solution)/shard_map/ppermute | solution.py:381
Sparse Core Ops, SparseCore 0:
  9.7 103.9 all-gather.4
  115.2 68.4 all-gather.6

commit v11 on v10

--- a/solution.py
+++ b/solution.py
@@ -187,7 +187,7 @@
         hidden_ref[...] += dot(x_ref[:, both], down_ref[:, both], ((1,), (1,)))
         return unused
 
-    lax.fori_loop(0, members, add_shard, 0, unroll=4)
+    lax.fori_loop(0, members, add_shard, 0, unroll=8)
     out.wait()
 
 
@@ -295,7 +295,7 @@
         frozen_ref[...] += dot(x_ref[:, far], w_ref[shard])
         return unused
 
-    lax.fori_loop(0, members, add_shard, 0, unroll=4)
+    lax.fori_loop(0, members, add_shard, 0, unroll=8)
 
     rate = ADAPTER_SCALE * LEARN_RATE
     block = min(width, 1024)
@@ -329,7 +329,7 @@
             return unused
 
         squares = lax.fori_loop(
-            0, width // block, down_block, jnp.zeros((rank, LANES), F32), unroll=4
+            0, width // block, down_block, jnp.zeros((rank, LANES), F32), unroll=8
         )
 
     total = jnp.sum(squares) + jnp.sum(up_delta * up_delta) + EPSILON
@@ -372,15 +372,15 @@
             write(core, send_refs)
 
 
-def halve(package, axis, bits, partner):
-    bit = package.shape[bits] // 2
+def halve(terms, axis, bits, partner):
+    bit = terms[0].shape[bits] // 2
     while bit:
-        keep = lax.slice_in_dim(package, 0, bit, axis=bits)
-        send = lax.slice_in_dim(package, bit, 2 * bit, axis=bits)
+        send = sum(lax.slice_in_dim(term, bit, 2 * bit, axis=bits) for term in terms)
         pairs = [(at, at ^ (partner * bit)) for at in range(lax.axis_size(axis))]
-        package = lax.ppermute(send, axis, pairs) + keep
+        sent = lax.ppermute(send, axis, pairs)
+        terms = [lax.slice_in_dim(term, 0, bit, axis=bits) for term in terms] + [sent]
         bit //= 2
-    return package
+    return terms
 
 
 def body(
@@ -504,10 +504,10 @@
         adapter_up,
     )
 
-    first = kept_y + lax.ppermute(sent_y, "grp", swap)
-    second = kept_x + lax.ppermute(sent_x, "grp", swap)
-    first = halve(halve(first, "grp", 0, 2), "fsdp", 1, 1)
-    second = halve(halve(second, "fsdp", 1, 1), "grp", 0, 2)
+    first = [kept_y, lax.ppermute(sent_y, "grp", swap)]
+    second = [kept_x, lax.ppermute(sent_x, "grp", swap)]
+    first = sum(halve(halve(first, "grp", 0, 2), "fsdp", 1, 1))
+    second = sum(halve(halve(second, "fsdp", 1, 1), "grp", 0, 2))
     package = jnp.concatenate([first[0, 0], second[0, 0]], axis=1)
     lines = [list(range(one, members, 2)) for one in range(2)]
     package = lax.all_to_all(

time: 253 us -> 254 us (level)
  other arithmetic: 3.7 us -> 7.09 us
  transfers between devices with their start and end apart: 12 -> 12, of which waited for: 8 -> 8; matrix products, arithmetic and copies ran while one was open for 1% -> 2% of each run, Pallas kernels for 7% -> 7%
where the time goes in v11:
time: 254 us
  waiting for transfers between devices  169 us (67%)
  Pallas kernels  34.6 us (14%)
  between operations  15.5 us (6%)
  starting transfers between devices  13.4 us (5%)
  blocking collectives  10.9 us (4%)
  other arithmetic  7.09 us (3%)
  local copies, waits for them, and re-layouts  3.27 us (1%)
    all_gather x1, waiting for transfers between devices, body(): lax.all_gather(swapped, BOTH, axis=0, axis_index_groups=rings)  70 us
    all_gather x1, waiting for transfers between devices, body(): near = lax.all_gather(mine, BOTH, axis=0, axis_index_groups=rings)  69.5 us
    pallas_call x1, Pallas kernels, body(): pl.pallas_call(lambda *refs: user_kernel(groups, members, most, *refs), o...  16.9 us
    ppermute x1, waiting for transfers between devices, body(): swapped = lax.ppermute(mine, 'fsdp', across)  16.2 us
    ppermute x4, waiting for transfers between devices, halve(): sent = lax.ppermute(send, axis, pairs)  11.5 us
    pallas_call x1, Pallas kernels, body(): pl.pallas_call(lambda *refs: near_kernel(groups, members, most, *refs), o...  11.1 us
    all_to_all x1, blocking collectives, body(): lax.all_to_all(package, 'fsdp', split_axis=0, concat_axis=0, axis_index_g...  10.9 us
    pallas_call x1, Pallas kernels, body(): pl.pallas_call(lambda *refs: pack_kernel(users, most, *refs), out_shape=j...  6.62 us
  transfers between devices with their start and end apart: 12, of which 8 were waited for; matrix products, arithmetic and copies ran while one was open for 2% of the time, Pallas kernels for 7%

profile of v11, /device:TPU:0, one launch (start us, length us, event | category | flops | bytes accessed | tf_op | source)
XLA Modules:
  0.0 253.7 jit_solution(4481837027761124186)
XLA Ops:
  7.2 0.0 copy-start
  7.2 0.0 all-gather.5.cloned.1.call-start
  7.2 1.5 copy-done
  8.8 0.8 constant_dynamic-slice_fusion
  9.6 0.0 all-gather.5.cloned.1.call-update
  9.6 0.0 all-gather.7.cloned.1.call-start
  9.7 4.1 %collective-permute-start = (bf16[256,1024]{1,0:T(8,128)(2,1)}, bf16[256,1024]{1,0:T(8,128)(2,1)S(1)}, u32[]{:S(2)}, u32[]{:S(2)}) collective-permute-start(bf16[256,1024]{1,0:T(8,128)(2,1)} %constant_dynamic-slice_fusion), channel_id=1, source_target_pairs={{0,4},{1,5},{2,6},{3,7},{4,0},{5,1},{6,2},{7,3},{8,12},{9,13},{10,... | collective-permute-start | bytes 1572872 | tf_op jit(solution)/shard_map/ppermute | solution.py:419
  14.4 6.6 %pack_rows.1 = bf16[256,10496]{1,0:T(8,128)(2,1)} custom-call(s32[1]{0:T(128)S(6)} %copy.15.refs_0_, s32[1,192]{1,0:T(1,128)} %bitcast.30, bf16[192,8192]{1,0:T(8,128)(2,1)} %refs_2_.1, bf16[192,1024]{1,0:T(8,128)(2,1)} %refs_3_.1), custom_call_target="tpu_custom_call" | custom-call | tf_op jit(solution)/shard_map/pack_rows/pallas_call | solution.py:425
  21.0 16.2 %collective-permute-done = bf16[256,1024]{1,0:T(8,128)(2,1)S(1)} collective-permute-done((bf16[256,1024]{1,0:T(8,128)(2,1)}, bf16[256,1024]{1,0:T(8,128)(2,1)S(1)}, u32[]{:S(2)}, u32[]{:S(2)}) %collective-permute-start) | collective-permute-done | bytes 524320 | tf_op jit(solution)/shard_map/ppermute | solution.py:419
  37.2 0.0 copy-start.1
  37.3 0.8 copy-done.1
  38.1 0.0 all-gather.7.cloned.1.call-update
  38.1 6.1 %all-to-all-start = ((bf16[32,8,10496]{2,1,0:T(8,128)(2,1)}), bf16[32,8,10496]{2,1,0:T(8,128)(2,1)}, u32[]{:S(2)}, u32[]{:S(2)}) async-start(bf16[32,8,10496]{2,1,0:T(8,128)(2,1)} %bitcast.23), calls=%async_computation | async-start | bytes 10747904 | tf_op jit(solution)/shard_map/all_to_all | solution.py:442
  44.2 69.5 %all-gather.5.cloned.1.call-done = bf16[2048,1024]{1,0:T(8,128)(2,1)} async-done(((bf16[256,1024]{1,0:T(8,128)(2,1)}), bf16[2048,1024]{1,0:T(8,128)(2,1)}) %all-gather.5.cloned.1.call-update) | async-done | bytes 4194320 | tf_op jit(solution)/shard_map/all_gather | solution.py:437
  113.7 0.0 collective-permute-start.1
  113.7 70.0 %all-gather.7.cloned.1.call-done = bf16[2048,1024]{1,0:T(8,128)(2,1)} async-done(((bf16[256,1024]{1,0:T(8,128)(2,1)}), bf16[2048,1024]{1,0:T(8,128)(2,1)}) %all-gather.7.cloned.1.call-update) | async-done | bytes 4194320 | tf_op jit(solution)/shard_map/all_gather | solution.py:439
  183.7 0.0 collective-permute-start.2
  184.4 0.0 all-to-all-done
  184.4 11.1 %near_product.1 = (bf16[288,8192]{1,0:T(8,128)(2,1)}, f32[288,1024]{1,0:T(8,128)}, f32[288,64]{1,0:T(8,128)}) custom-call(bf16[256,10496]{1,0:T(8,128)(2,1)} %bitcast.2.refs_0_.refs_2_, bf16[8,256,1024]{2,1,0:T(8,128)(2,1)} %bitcast.27, bf16[8,256,1024]{2,1,0:T(8,128)(2,1)} %bitcast.29, bf16[64,8192]{1,0:T(8,128)(2,1)} %bitcast.24), custom_call_target="tpu_custom_call" | custom-call | flops 2415919104 | bytes 30000000 | tf_op jit(solution)/shard_map/near_product/pallas_call | solution.py:448
  195.5 0.0 collective-permute-done.1.refs_6_
  195.5 0.0 collective-permute-done.2.refs_7_
  195.5 16.9 %user_steps.1 = (f32[2,2,4,32,256]{4,3,2,1,0:T(8,128)}, f32[2,2,4,40,256]{4,3,2,1,0:T(8,128)}, f32[2,2,4,32,256]{4,3,2,1,0:T(8,128)}, f32[2,2,4,40,256]{4,3,2,1,0:T(8,128)}) custom-call(s32[32]{0:T(128)} %refs_0_.2, f32[1]{0:T(128)} %copy.16.refs_1_, bf16[256,10496]{1,0:T(8,128)(2,1)} %bitcast.2.refs_0_.refs_2_, ...), custom_call_target="tpu_custom_call" | custom-call | tf_op jit(solution)/shard_map/user_steps/pallas_call | solution.py:475
  212.4 0.0 copy-start.2
  212.4 0.0 copy-start.3
  212.5 0.6 collective-permute-start.3
  213.0 0.1 collective-permute-start.6
  213.1 1.7 collective-permute-done.3
  214.8 1.0 slice_add_fusion.1
  215.8 0.1 collective-permute-start.4
  215.9 0.0 collective-permute-done.6
  215.9 1.0 slice_add_fusion
  216.9 0.1 collective-permute-start.7
  217.0 7.5 %collective-permute-done.4 = f32[1,2,4,32,256]{4,3,2,1,0:T(8,128)S(1)} collective-permute-done((f32[1,2,4,32,256]{4,3,2,1,0:T(8,128)S(1)}, f32[1,2,4,32,256]{4,3,2,1,0:T(8,128)S(1)}, u32[]{:S(2)}, u32[]{:S(2)}) %collective-permute-start.4) | collective-permute-done | bytes 262176 | tf_op jit(solution)/shard_map/ppermute | solution.py:380
  224.4 0.9 slice_add_fusion.6
  225.4 0.1 collective-permute-start.5
  225.4 1.5 collective-permute-done.7
  226.9 0.9 slice_add_fusion.2
  227.9 2.3 collective-permute-start.8
  230.2 0.2 collective-permute-done.5
  230.4 0.9 fusion.3
  231.3 2.3 collective-permute-done.8
  233.6 1.0 fusion.1
  234.6 10.9 %all_to_all.10 = f32[4,72,256]{2,1,0:T(8,128)S(1)} all-to-all(f32[4,72,256]{2,1,0:T(8,128)S(1)} %pad_maximum_fusion), channel_id=1, replica_groups={{0,2,4,6},{1,3,5,7},{8,10,12,14},{9,11,13,15},{16,18,20,22},{17,19,21,2..., dimensions={0} | all-to-all | bytes 589824 | tf_op jit(solution)/shard_map/all_to_all | solution.py:513
  245.5 0.1 reshape.22
  245.6 0.0 copy-done.2
  245.6 0.6 fusion.4
  246.3 0.0 copy-done.3
  246.3 0.6 bitcast_add_fusion
  (3 shorter events, 0.0 us)
Async XLA Ops:
  7.2 1.6 copy-start
  7.2 106.5 %all-gather.5.cloned.1.call-start = ((), (), s32[]{:S(2)}) async-start(), calls=%async_computation.2 | async-start | bytes 4718592 | tf_op jit(solution)/shard_map/all_gather | solution.py:437
  9.6 174.1 %all-gather.7.cloned.1.call-start = ((), (), s32[]{:S(2)}) async-start(), calls=%async_computation.3 | async-start | bytes 4718592 | tf_op jit(solution)/shard_map/all_gather | solution.py:439
  9.7 27.6 %collective-permute-start = (bf16[256,1024]{1,0:T(8,128)(2,1)}, bf16[256,1024]{1,0:T(8,128)(2,1)S(1)}, u32[]{:S(2)}, u32[]{:S(2)}) collective-permute-start(bf16[256,1024]{1,0:T(8,128)(2,1)} %constant_dynamic-slice_fusion), channel_id=1, source_target_pairs={{0,4},{1,5},{2,6},{3,7},{4,0},{5,1},{6,2},{7,3},{8,12},{9,13},{10,... | collective-permute-start | bytes 1572872 | tf_op jit(solution)/shard_map/ppermute | solution.py:419
  37.2 0.8 copy-start.1
  38.1 146.3 %all-to-all-start = ((bf16[32,8,10496]{2,1,0:T(8,128)(2,1)}), bf16[32,8,10496]{2,1,0:T(8,128)(2,1)}, u32[]{:S(2)}, u32[]{:S(2)}) async-start(bf16[32,8,10496]{2,1,0:T(8,128)(2,1)} %bitcast.23), calls=%async_computation | async-start | bytes 10747904 | tf_op jit(solution)/shard_map/all_to_all | solution.py:442
  113.7 81.8 %collective-permute-start.1 = (bf16[8,256,1024]{2,1,0:T(8,128)(2,1)}, bf16[8,256,1024]{2,1,0:T(8,128)(2,1)}, u32[]{:S(2)}, u32[]{:S(2)}) collective-permute-start(bf16[8,256,1024]{2,1,0:T(8,128)(2,1)} %bitcast.26), channel_id=1, source_target_pairs={{0,8},{8,0},{16,24},{24,16},{1,9},{9,1},{17,25},{25,17},{2,10},{10... | collective-permute-start | bytes 12582920 | tf_op jit(solution)/shard_map/ppermute | solution.py:440
  183.7 11.8 %collective-permute-start.2 = (bf16[8,256,1024]{2,1,0:T(8,128)(2,1)}, bf16[8,256,1024]{2,1,0:T(8,128)(2,1)}, u32[]{:S(2)}, u32[]{:S(2)}) collective-permute-start(bf16[8,256,1024]{2,1,0:T(8,128)(2,1)} %bitcast.28), channel_id=1, source_target_pairs={{0,8},{8,0},{16,24},{24,16},{1,9},{9,1},{17,25},{25,17},{2,10},{10... | collective-permute-start | bytes 12582920 | tf_op jit(solution)/shard_map/ppermute | solution.py:441
  212.4 33.2 %copy-start.2 = (f32[256,64]{0,1:T(8,128)S(1)}, f32[256,64]{0,1:T(8,128)}, u32[]{:S(2)}) copy-start(f32[256,64]{0,1:T(8,128)} %param.20) | copy-start | bytes 196612
  212.4 33.8 %copy-start.3 = (f32[64,32]{0,1:T(8,128)S(1)}, f32[64,32]{0,1:T(8,128)}, u32[]{:S(2)}) copy-start(f32[64,32]{0,1:T(8,128)} %param.21) | copy-start | bytes 24580
  212.5 2.3 collective-permute-start.3
  213.0 2.8 %collective-permute-start.6 = (f32[2,2,4,40,256]{4,3,2,1,0:T(8,128)}, f32[2,2,4,40,256]{4,3,2,1,0:T(8,128)S(1)}, u32[]{:S(2)}, u32[]{:S(2)}) collective-permute-start(f32[2,2,4,40,256]{4,3,2,1,0:T(8,128)} %get-tuple-element.19), channel_id=1, source_target_pairs={{0,8},{8,0},{16,24},{24,16},{1,9},{9,1},{17,25},{25,17},{2,10},{10... | collective-permute-start | bytes 1966088 | tf_op jit(solution)/shard_map/ppermute | solution.py:508
  215.8 8.7 %collective-permute-start.4 = (f32[1,2,4,32,256]{4,3,2,1,0:T(8,128)S(1)}, f32[1,2,4,32,256]{4,3,2,1,0:T(8,128)S(1)}, u32[]{:S(2)}, u32[]{:S(2)}) collective-permute-start(f32[1,2,4,32,256]{4,3,2,1,0:T(8,128)S(1)} %slice_add_fusion.1), channel_id=1, source_target_pairs={{0,16},{8,24},{16,0},{24,8},{1,17},{9,25},{17,1},{25,9},{2,18},{10... | collective-permute-start | bytes 786440 | tf_op jit(solution)/shard_map/ppermute | solution.py:380
  216.9 10.1 %collective-permute-start.7 = (f32[2,1,4,40,256]{4,3,2,1,0:T(8,128)S(1)}, f32[2,1,4,40,256]{4,3,2,1,0:T(8,128)S(1)}, u32[]{:S(2)}, u32[]{:S(2)}) collective-permute-start(f32[2,1,4,40,256]{4,3,2,1,0:T(8,128)S(1)} %slice_add_fusion), channel_id=1, source_target_pairs={{0,1},{1,0},{2,3},{3,2},{4,5},{5,4},{6,7},{7,6},{8,9},{9,8},{10,11... | collective-permute-start | bytes 983048 | tf_op jit(solution)/shard_map/ppermute | solution.py:380
  225.4 5.0 %collective-permute-start.5 = (f32[1,1,4,32,256]{4,3,2,1,0:T(8,128)S(1)}, f32[1,1,4,32,256]{4,3,2,1,0:T(8,128)S(1)}, u32[]{:S(2)}, u32[]{:S(2)}) collective-permute-start(f32[1,1,4,32,256]{4,3,2,1,0:T(8,128)S(1)} %slice_add_fusion.6), channel_id=1, source_target_pairs={{0,1},{1,0},{2,3},{3,2},{4,5},{5,4},{6,7},{7,6},{8,9},{9,8},{10,11... | collective-permute-start | bytes 393224 | tf_op jit(solution)/shard_map/ppermute | solution.py:380
  227.9 5.7 %collective-permute-start.8 = (f32[1,1,4,40,256]{4,3,2,1,0:T(8,128)S(1)}, f32[1,1,4,40,256]{4,3,2,1,0:T(8,128)S(1)}, u32[]{:S(2)}, u32[]{:S(2)}) collective-permute-start(f32[1,1,4,40,256]{4,3,2,1,0:T(8,128)S(1)} %slice_add_fusion.2), channel_id=1, source_target_pairs={{0,16},{8,24},{16,0},{24,8},{1,17},{9,25},{17,1},{25,9},{2,18},{10... | collective-permute-start | bytes 491528 | tf_op jit(solution)/shard_map/ppermute | solution.py:380
Sparse Core Ops, SparseCore 0:
  9.7 103.9 all-gather.4
  115.2 68.4 all-gather.6

commit v12 on v10

--- a/solution.py
+++ b/solution.py
@@ -187,7 +187,7 @@
         hidden_ref[...] += dot(x_ref[:, both], down_ref[:, both], ((1,), (1,)))
         return unused
 
-    lax.fori_loop(0, members, add_shard, 0, unroll=4)
+    lax.fori_loop(0, members, add_shard, 0, unroll=8)
     out.wait()
 
 
@@ -295,7 +295,7 @@
         frozen_ref[...] += dot(x_ref[:, far], w_ref[shard])
         return unused
 
-    lax.fori_loop(0, members, add_shard, 0, unroll=4)
+    lax.fori_loop(0, members, add_shard, 0, unroll=8)
 
     rate = ADAPTER_SCALE * LEARN_RATE
     block = min(width, 1024)
@@ -329,7 +329,7 @@
             return unused
 
         squares = lax.fori_loop(
-            0, width // block, down_block, jnp.zeros((rank, LANES), F32), unroll=4
+            0, width // block, down_block, jnp.zeros((rank, LANES), F32), unroll=8
         )
 
     total = jnp.sum(squares) + jnp.sum(up_delta * up_delta) + EPSILON
@@ -435,7 +435,7 @@
         name="pack_rows",
     )(device_row_count, row_owner_user.reshape(1, per_dev), tokens, targets)
     near = lax.all_gather(mine, BOTH, axis=0, axis_index_groups=rings)
-    packed, swapped = lax.optimization_barrier((packed, swapped))
+    swapped, unused = lax.optimization_barrier((swapped, packed))
     near_swapped = lax.all_gather(swapped, BOTH, axis=0, axis_index_groups=rings)
     far = lax.ppermute(near, "grp", swap)
     far_swapped = lax.ppermute(near_swapped, "grp", swap)

time: 253 us -> 252 us (level)
  no operation moved by 1% of the time
where the time goes in v12:
time: 252 us
  waiting for transfers between devices  171 us (68%)
  Pallas kernels  34.6 us (14%)
  between operations  15.5 us (6%)
  starting transfers between devices  13.4 us (5%)
  blocking collectives  10.4 us (4%)
  other arithmetic  3.7 us (1%)
  local copies, waits for them, and re-layouts  3.34 us (1%)
    all_gather x1, waiting for transfers between devices, body(): lax.all_gather(swapped, BOTH, axis=0, axis_index_groups=rings)  70 us
    all_gather x1, waiting for transfers between devices, body(): near = lax.all_gather(mine, BOTH, axis=0, axis_index_groups=rings)  69.5 us
    pallas_call x1, Pallas kernels, body(): pl.pallas_call(lambda *refs: user_kernel(groups, members, most, *refs), o...  16.9 us
    ppermute x1, waiting for transfers between devices, body(): swapped = lax.ppermute(mine, 'fsdp', across)  16.2 us
    ppermute x4, waiting for transfers between devices, halve(): package = lax.ppermute(send, axis, pairs) + keep  13.5 us
    pallas_call x1, Pallas kernels, body(): pl.pallas_call(lambda *refs: near_kernel(groups, members, most, *refs), o...  11.1 us
    all_to_all x1, blocking collectives, body(): lax.all_to_all(package, 'fsdp', split_axis=0, concat_axis=0, axis_index_g...  10.4 us
    pallas_call x1, Pallas kernels, body(): pl.pallas_call(lambda *refs: pack_kernel(users, most, *refs), out_shape=j...  6.62 us
  transfers between devices with their start and end apart: 12, of which 8 were waited for; matrix products, arithmetic and copies ran while one was open for 1% of the time, Pallas kernels for 7%

profile of v12, /device:TPU:0, one launch (start us, length us, event | category | flops | bytes accessed | tf_op | source)
XLA Modules:
  0.0 252.0 jit_solution(10444103902450993906)
XLA Ops:
  7.2 0.0 copy-start
  7.2 0.0 all-gather.5.cloned.1.call-start
  7.2 1.5 copy-done
  8.8 0.8 constant_dynamic-slice_fusion
  9.6 0.0 all-gather.5.cloned.1.call-update
  9.6 0.0 all-gather.7.cloned.1.call-start
  9.7 4.1 %collective-permute-start = (bf16[256,1024]{1,0:T(8,128)(2,1)}, bf16[256,1024]{1,0:T(8,128)(2,1)S(1)}, u32[]{:S(2)}, u32[]{:S(2)}) collective-permute-start(bf16[256,1024]{1,0:T(8,128)(2,1)} %constant_dynamic-slice_fusion), channel_id=1, source_target_pairs={{0,4},{1,5},{2,6},{3,7},{4,0},{5,1},{6,2},{7,3},{8,12},{9,13},{10,... | collective-permute-start | bytes 1572872 | tf_op jit(solution)/shard_map/ppermute | solution.py:419
  14.4 6.6 %pack_rows.1 = bf16[256,10496]{1,0:T(8,128)(2,1)} custom-call(s32[1]{0:T(128)S(6)} %copy.15.refs_0_, s32[1,192]{1,0:T(1,128)} %bitcast.30, bf16[192,8192]{1,0:T(8,128)(2,1)} %refs_2_.1, bf16[192,1024]{1,0:T(8,128)(2,1)} %refs_3_.1), custom_call_target="tpu_custom_call" | custom-call | tf_op jit(solution)/shard_map/pack_rows/pallas_call | solution.py:425
  21.0 16.2 %collective-permute-done = bf16[256,1024]{1,0:T(8,128)(2,1)S(1)} collective-permute-done((bf16[256,1024]{1,0:T(8,128)(2,1)}, bf16[256,1024]{1,0:T(8,128)(2,1)S(1)}, u32[]{:S(2)}, u32[]{:S(2)}) %collective-permute-start) | collective-permute-done | bytes 524320 | tf_op jit(solution)/shard_map/ppermute | solution.py:419
  37.2 0.0 copy-start.1
  37.3 0.8 copy-done.1
  38.1 0.0 all-gather.7.cloned.1.call-update
  38.1 6.1 %all-to-all-start = ((bf16[32,8,10496]{2,1,0:T(8,128)(2,1)}), bf16[32,8,10496]{2,1,0:T(8,128)(2,1)}, u32[]{:S(2)}, u32[]{:S(2)}) async-start(bf16[32,8,10496]{2,1,0:T(8,128)(2,1)} %bitcast.23), calls=%async_computation | async-start | bytes 10747904 | tf_op jit(solution)/shard_map/all_to_all | solution.py:442
  44.2 69.5 %all-gather.5.cloned.1.call-done = bf16[2048,1024]{1,0:T(8,128)(2,1)} async-done(((bf16[256,1024]{1,0:T(8,128)(2,1)}), bf16[2048,1024]{1,0:T(8,128)(2,1)}) %all-gather.5.cloned.1.call-update) | async-done | bytes 4194320 | tf_op jit(solution)/shard_map/all_gather | solution.py:437
  113.7 0.0 collective-permute-start.1
  113.7 70.0 %all-gather.7.cloned.1.call-done = bf16[2048,1024]{1,0:T(8,128)(2,1)} async-done(((bf16[256,1024]{1,0:T(8,128)(2,1)}), bf16[2048,1024]{1,0:T(8,128)(2,1)}) %all-gather.7.cloned.1.call-update) | async-done | bytes 4194320 | tf_op jit(solution)/shard_map/all_gather | solution.py:439
  183.7 0.0 collective-permute-start.2
  184.4 0.0 all-to-all-done
  184.4 11.1 %near_product.1 = (bf16[288,8192]{1,0:T(8,128)(2,1)}, f32[288,1024]{1,0:T(8,128)}, f32[288,64]{1,0:T(8,128)}) custom-call(bf16[256,10496]{1,0:T(8,128)(2,1)} %bitcast.2.refs_0_.refs_2_, bf16[8,256,1024]{2,1,0:T(8,128)(2,1)} %bitcast.27, bf16[8,256,1024]{2,1,0:T(8,128)(2,1)} %bitcast.29, bf16[64,8192]{1,0:T(8,128)(2,1)} %bitcast.24), custom_call_target="tpu_custom_call" | custom-call | flops 2415919104 | bytes 30000000 | tf_op jit(solution)/shard_map/near_product/pallas_call | solution.py:448
  195.5 0.0 collective-permute-done.1.refs_6_
  195.5 0.0 collective-permute-done.2.refs_7_
  195.5 16.9 %user_steps.1 = (f32[2,2,4,32,256]{4,3,2,1,0:T(8,128)}, f32[2,2,4,40,256]{4,3,2,1,0:T(8,128)}, f32[2,2,4,32,256]{4,3,2,1,0:T(8,128)}, f32[2,2,4,40,256]{4,3,2,1,0:T(8,128)}) custom-call(s32[32]{0:T(128)} %refs_0_.2, f32[1]{0:T(128)} %copy.16.refs_1_, bf16[256,10496]{1,0:T(8,128)(2,1)} %bitcast.2.refs_0_.refs_2_, ...), custom_call_target="tpu_custom_call" | custom-call | tf_op jit(solution)/shard_map/user_steps/pallas_call | solution.py:475
  212.4 0.6 collective-permute-start.3
  213.0 0.1 collective-permute-start.6
  213.1 1.7 collective-permute-done.3
  214.8 1.1 add.38
  215.9 0.0 copy-start.2
  215.9 0.0 copy-start.3
  215.9 0.1 collective-permute-start.4
  216.0 0.0 collective-permute-done.6
  216.0 1.2 add.41
  217.2 0.1 collective-permute-start.7
  217.3 7.3 %collective-permute-done.4 = f32[1,2,4,32,256]{4,3,2,1,0:T(8,128)S(1)} collective-permute-done((f32[1,2,4,32,256]{4,3,2,1,0:T(8,128)S(1)}, f32[1,2,4,32,256]{4,3,2,1,0:T(8,128)S(1)}, u32[]{:S(2)}, u32[]{:S(2)}) %collective-permute-start.4) | collective-permute-done | bytes 262176 | tf_op jit(solution)/shard_map/ppermute | solution.py:381
  224.6 0.1 collective-permute-start.5
  224.7 2.9 %collective-permute-done.7 = f32[2,1,4,40,256]{4,3,2,1,0:T(8,128)S(1)} collective-permute-done((f32[2,1,4,40,256]{4,3,2,1,0:T(8,128)S(1)}, f32[2,1,4,40,256]{4,3,2,1,0:T(8,128)S(1)}, u32[]{:S(2)}, u32[]{:S(2)}) %collective-permute-start.7) | collective-permute-done | bytes 327712 | tf_op jit(solution)/shard_map/ppermute | solution.py:381
  227.7 2.3 collective-permute-start.8
  230.0 0.1 collective-permute-done.5
  230.1 3.2 %collective-permute-done.8 = f32[1,1,4,40,256]{4,3,2,1,0:T(8,128)S(1)} collective-permute-done((f32[1,1,4,40,256]{4,3,2,1,0:T(8,128)S(1)}, f32[1,1,4,40,256]{4,3,2,1,0:T(8,128)S(1)}, u32[]{:S(2)}, u32[]{:S(2)}) %collective-permute-start.8) | collective-permute-done | bytes 163872 | tf_op jit(solution)/shard_map/ppermute | solution.py:381
  233.4 10.4 %all_to_all.10 = f32[4,72,256]{2,1,0:T(8,128)S(1)} all-to-all(f32[4,72,256]{2,1,0:T(8,128)S(1)} %pad_maximum_fusion), channel_id=1, replica_groups={{0,2,4,6},{1,3,5,7},{8,10,12,14},{9,11,13,15},{16,18,20,22},{17,19,21,2..., dimensions={0} | all-to-all | bytes 589824 | tf_op jit(solution)/shard_map/all_to_all | solution.py:513
  243.8 0.1 reshape.22
  243.9 0.0 copy-done.2
  243.9 0.6 fusion.2
  244.6 0.0 copy-done.3
  244.6 0.6 bitcast_add_fusion
  (11 shorter events, 0.2 us)
Async XLA Ops:
  7.2 1.6 copy-start
  7.2 106.5 %all-gather.5.cloned.1.call-start = ((), (), s32[]{:S(2)}) async-start(), calls=%async_computation.2 | async-start | bytes 4718592 | tf_op jit(solution)/shard_map/all_gather | solution.py:437
  9.6 174.1 %all-gather.7.cloned.1.call-start = ((), (), s32[]{:S(2)}) async-start(), calls=%async_computation.3 | async-start | bytes 4718592 | tf_op jit(solution)/shard_map/all_gather | solution.py:439
  9.7 27.6 %collective-permute-start = (bf16[256,1024]{1,0:T(8,128)(2,1)}, bf16[256,1024]{1,0:T(8,128)(2,1)S(1)}, u32[]{:S(2)}, u32[]{:S(2)}) collective-permute-start(bf16[256,1024]{1,0:T(8,128)(2,1)} %constant_dynamic-slice_fusion), channel_id=1, source_target_pairs={{0,4},{1,5},{2,6},{3,7},{4,0},{5,1},{6,2},{7,3},{8,12},{9,13},{10,... | collective-permute-start | bytes 1572872 | tf_op jit(solution)/shard_map/ppermute | solution.py:419
  37.2 0.8 copy-start.1
  38.1 146.3 %all-to-all-start = ((bf16[32,8,10496]{2,1,0:T(8,128)(2,1)}), bf16[32,8,10496]{2,1,0:T(8,128)(2,1)}, u32[]{:S(2)}, u32[]{:S(2)}) async-start(bf16[32,8,10496]{2,1,0:T(8,128)(2,1)} %bitcast.23), calls=%async_computation | async-start | bytes 10747904 | tf_op jit(solution)/shard_map/all_to_all | solution.py:442
  113.7 81.8 %collective-permute-start.1 = (bf16[8,256,1024]{2,1,0:T(8,128)(2,1)}, bf16[8,256,1024]{2,1,0:T(8,128)(2,1)}, u32[]{:S(2)}, u32[]{:S(2)}) collective-permute-start(bf16[8,256,1024]{2,1,0:T(8,128)(2,1)} %bitcast.26), channel_id=1, source_target_pairs={{0,8},{8,0},{16,24},{24,16},{1,9},{9,1},{17,25},{25,17},{2,10},{10... | collective-permute-start | bytes 12582920 | tf_op jit(solution)/shard_map/ppermute | solution.py:440
  183.7 11.8 %collective-permute-start.2 = (bf16[8,256,1024]{2,1,0:T(8,128)(2,1)}, bf16[8,256,1024]{2,1,0:T(8,128)(2,1)}, u32[]{:S(2)}, u32[]{:S(2)}) collective-permute-start(bf16[8,256,1024]{2,1,0:T(8,128)(2,1)} %bitcast.28), channel_id=1, source_target_pairs={{0,8},{8,0},{16,24},{24,16},{1,9},{9,1},{17,25},{25,17},{2,10},{10... | collective-permute-start | bytes 12582920 | tf_op jit(solution)/shard_map/ppermute | solution.py:441
  212.4 2.3 collective-permute-start.3
  213.0 3.0 %collective-permute-start.6 = (f32[2,2,4,40,256]{4,3,2,1,0:T(8,128)}, f32[2,2,4,40,256]{4,3,2,1,0:T(8,128)S(1)}, u32[]{:S(2)}, u32[]{:S(2)}) collective-permute-start(f32[2,2,4,40,256]{4,3,2,1,0:T(8,128)} %get-tuple-element.17), channel_id=1, source_target_pairs={{0,8},{8,0},{16,24},{24,16},{1,9},{9,1},{17,25},{25,17},{2,10},{10... | collective-permute-start | bytes 1966088 | tf_op jit(solution)/shard_map/ppermute | solution.py:508
  215.9 28.1 %copy-start.2 = (f32[256,64]{0,1:T(8,128)S(1)}, f32[256,64]{0,1:T(8,128)}, u32[]{:S(2)}) copy-start(f32[256,64]{0,1:T(8,128)} %param.20) | copy-start | bytes 196612
  215.9 28.7 %copy-start.3 = (f32[64,32]{0,1:T(8,128)S(1)}, f32[64,32]{0,1:T(8,128)}, u32[]{:S(2)}) copy-start(f32[64,32]{0,1:T(8,128)} %param.21) | copy-start | bytes 24580
  215.9 8.7 %collective-permute-start.4 = (f32[1,2,4,32,256]{4,3,2,1,0:T(8,128)S(1)}, f32[1,2,4,32,256]{4,3,2,1,0:T(8,128)S(1)}, u32[]{:S(2)}, u32[]{:S(2)}) collective-permute-start(f32[1,2,4,32,256]{4,3,2,1,0:T(8,128)S(1)} %slice.40), channel_id=1, source_target_pairs={{0,16},{8,24},{16,0},{24,8},{1,17},{9,25},{17,1},{25,9},{2,18},{10... | collective-permute-start | bytes 786440 | tf_op jit(solution)/shard_map/ppermute | solution.py:381
  217.2 10.4 %collective-permute-start.7 = (f32[2,1,4,40,256]{4,3,2,1,0:T(8,128)S(1)}, f32[2,1,4,40,256]{4,3,2,1,0:T(8,128)S(1)}, u32[]{:S(2)}, u32[]{:S(2)}) collective-permute-start(f32[2,1,4,40,256]{4,3,2,1,0:T(8,128)S(1)} %slice.44), channel_id=1, source_target_pairs={{0,1},{1,0},{2,3},{3,2},{4,5},{5,4},{6,7},{7,6},{8,9},{9,8},{10,11... | collective-permute-start | bytes 983048 | tf_op jit(solution)/shard_map/ppermute | solution.py:381
  224.6 5.5 %collective-permute-start.5 = (f32[1,1,4,32,256]{4,3,2,1,0:T(8,128)S(1)}, f32[1,1,4,32,256]{4,3,2,1,0:T(8,128)S(1)}, u32[]{:S(2)}, u32[]{:S(2)}) collective-permute-start(f32[1,1,4,32,256]{4,3,2,1,0:T(8,128)S(1)} %slice.42), channel_id=1, source_target_pairs={{0,1},{1,0},{2,3},{3,2},{4,5},{5,4},{6,7},{7,6},{8,9},{9,8},{10,11... | collective-permute-start | bytes 393224 | tf_op jit(solution)/shard_map/ppermute | solution.py:381
  227.7 5.6 %collective-permute-start.8 = (f32[1,1,4,40,256]{4,3,2,1,0:T(8,128)S(1)}, f32[1,1,4,40,256]{4,3,2,1,0:T(8,128)S(1)}, u32[]{:S(2)}, u32[]{:S(2)}) collective-permute-start(f32[1,1,4,40,256]{4,3,2,1,0:T(8,128)S(1)} %slice.46), channel_id=1, source_target_pairs={{0,16},{8,24},{16,0},{24,8},{1,17},{9,25},{17,1},{25,9},{2,18},{10... | collective-permute-start | bytes 491528 | tf_op jit(solution)/shard_map/ppermute | solution.py:381
Sparse Core Ops, SparseCore 0:
  9.7 103.9 all-gather.4
  115.2 68.4 all-gather.6
